TPU v7x, 256 devices: a whole 4x4x8 slice. The times are simulated.
256 devices in a mesh: row: 8 (over x, y_hi), col: 32 (over z, y_lo, core).
Axes of the slice: x: 4, y: 4 (y_hi: 2, y_lo: 2; y = y_hi * 2 + y_lo), z: 8, core: 2. Of those that a mesh axis runs over, the one named last changes fastest.
Arguments:
- tokens: bfloat16 [512, 16384], P('col', 'row'), may hold values from -6 to 6
- gate_quant: bfloat16 [16384, 28672], P('row', 'col'), may hold values from -4 to 4
- gate_scale: float32 [128, 224], P('row', 'col'), may hold values from 0.004 to 0.016
- up_quant: bfloat16 [16384, 28672], P('row', 'col'), may hold values from -4 to 4
- up_scale: float32 [128, 224], P('row', 'col'), may hold values from 0.004 to 0.016
- down_quant: bfloat16 [28672, 16384], P('col', 'row'), may hold values from -4 to 4
- down_scale: float32 [224, 128], P('col', 'row'), may hold values from 0.003 to 0.012
Outputs:
- mixed: bfloat16 [512, 16384], P('col', 'row')
All inputs are finite; a program needn't handle non-finite values.
Results may differ from a plain program's by a relative error of at most 0.0071.
Values may be sent and summed in bfloat16 or wider, within the bound.
No kernel may reach another device: no remote copies, remote signals or barrier semaphores. Data moves between devices by JAX's collectives and lax.ppermute only.
A program may use at most 64 MiB of HBM per device.

v0:
```python
import jax
import jax.numpy as jnp
from jax import lax
from jax.sharding import PartitionSpec as P

BLOCK = 128


def dequant(quant, scale):
    height, width = quant.shape
    blocks = quant.astype(jnp.float32).reshape(height // BLOCK, BLOCK, width // BLOCK, BLOCK)
    return (blocks * scale[:, None, :, None]).reshape(height, width).astype(jnp.bfloat16)


def local(tokens, gate_quant, gate_scale, up_quant, up_scale, down_quant, down_scale):
    features = lax.all_gather(tokens, "col", axis=0, tiled=True)
    gate_weight = dequant(gate_quant, gate_scale)
    up_weight = dequant(up_quant, up_scale)
    width = gate_weight.shape[1]
    picked = features
    joined = lax.psum_scatter(
        jnp.concatenate(
            [
                jnp.dot(picked, gate_weight, preferred_element_type=jnp.float32),
                jnp.dot(picked, up_weight, preferred_element_type=jnp.float32),
            ],
            axis=1,
        ),
        "row",
        scatter_dimension=0,
        tiled=True,
    )
    local_hidden = (jax.nn.silu(joined[:, :width]) * joined[:, width:]).astype(jnp.bfloat16)
    hidden = lax.all_gather(local_hidden, "row", axis=0, tiled=True)
    down_weight = dequant(down_quant, down_scale)
    picked = hidden
    mixed = lax.psum_scatter(
        jnp.dot(picked, down_weight, preferred_element_type=jnp.float32),
        "col",
        scatter_dimension=0,
        tiled=True,
    )
    return mixed.astype(jnp.bfloat16)


def solution(mesh):
    placed = (
        P("col", "row"),
        P("row", "col"),
        P("row", "col"),
        P("row", "col"),
        P("row", "col"),
        P("col", "row"),
        P("col", "row"),
    )
    return jax.shard_map(
        local, mesh=mesh, in_specs=placed, out_specs=P("col", "row"), check_vma=False
    )
```

profile of v0, /device:TPU:1, one launch (start us, length us, event | category | flops | bytes accessed | tf_op | source)
XLA Modules:
  0.0 353.1 jit_solution(2375091479149697113)
XLA Ops:
  6.5 0.0 all-gather.2.cloned.1.call-start
  6.5 0.7 all-gather.2.cloned.1.call-update
  7.3 0.0 reduce-scatter.7.cloned.1.call-start
  7.3 6.1 %copy.15 = bf16[2048,896]{0,1:T(8,128)(2,1)} copy(bf16[2048,896]{1,0:T(8,128)(2,1)} %param.8) | data formatting | bytes 7340032 | tf_op args[1]
  13.4 0.0 copy-start.4
  13.4 6.2 %copy.16 = bf16[2048,896]{0,1:T(8,128)(2,1)} copy(bf16[2048,896]{1,0:T(8,128)(2,1)} %param.10) | data formatting | bytes 7340032 | tf_op args[3]
  19.6 58.5 %all-gather.2.cloned.1.call-done = bf16[512,2048]{1,0:T(8,128)(2,1)} async-done(((bf16[16,2048]{1,0:T(8,128)(2,1)}), bf16[512,2048]{1,0:T(8,128)(2,1)}) %all-gather.2.cloned.1.call-update) | async-done | bytes 2097168 | tf_op jit(solution)/shard_map/all_gather | solution.py:16
  78.1 0.0 copy-done.4
  78.1 0.0 copy-start.1
  78.2 0.5 mul.40
  78.7 1.5 copy-done.1
  80.2 0.7 copy-done.2
  80.9 2.6 fusion.12
  83.4 0.0 copy-done.5
  83.4 0.0 copy-start
  83.4 0.5 mul.43
  84.0 1.5 copy-done
  85.5 2.5 fusion.9
  88.0 2.2 pad_maximum_fusion
  90.2 5.2 %copy.19 = f32[512,1792]{1,0:T(8,128)} copy(f32[512,1792]{0,1:T(8,128)} %pad_maximum_fusion) | data formatting | bytes 7340032
  95.3 0.0 reduce-scatter.7.cloned.1.call-update
  95.4 0.0 reduce-scatter.5.cloned.1.call-start
  95.4 85.6 %reduce-scatter.7.cloned.1.call-done = f32[64,1792]{1,0:T(8,128)} async-done(((f32[512,1792]{1,0:T(8,128)}), f32[64,1792]{1,0:T(8,128)}) %reduce-scatter.7.cloned.1.call-update) | async-done | bytes 458768 | tf_op jit(solution)/shard_map/reduce_scatter | solution.py:21
  181.0 1.1 fusion.15
  182.2 30.8 %all_gather.7 = bf16[512,896]{1,0:T(8,128)(2,1)S(1)} all-gather(bf16[64,896]{1,0:T(8,128)(2,1)S(1)} %fusion.15), channel_id=1, replica_groups=mesh['row'=8,'col'=32] {'row'}, dimensions={0}, use_global_device_ids=true | all-gather | bytes 1032192 | tf_op jit(solution)/shard_map/all_gather | solution.py:34
  212.9 0.0 copy-done.6
  212.9 0.5 mul.48
  213.5 1.5 copy-done.3
  215.0 4.8 %fusion.7 = f32[512,2048]{1,0:T(8,128)} fusion(bf16[512,896]{1,0:T(8,128)(2,1)S(1)} %all_gather.7, f32[112,8,16,128]{3,2,1,0:T(8,128)S(1)} %bitcast.39, bf16[896,2048]{1,0:T(8,128)(2,1)S(1)} %copy-done.3), kind=kOutput, calls=%fused_computation.8 | convolution fusion | flops 1884553216 | bytes 16121856 | tf_op jit(solution)/shard_map/dot_general | solution.py:38
  219.8 0.0 reduce-scatter.5.cloned.1.call-update
  219.8 125.2 %reduce-scatter.5.cloned.1.call-done = f32[16,2048]{1,0:T(8,128)} async-done(((f32[512,2048]{1,0:T(8,128)}), f32[16,2048]{1,0:T(8,128)}) %reduce-scatter.5.cloned.1.call-update) | async-done | bytes 131088 | tf_op jit(solution)/shard_map/reduce_scatter | solution.py:37
  345.0 1.5 convert_element_type.31
  (4 shorter events, 0.0 us)
Async XLA Ops:
  6.5 71.6 %all-gather.2.cloned.1.call-start = ((), (), s32[]{:S(2)}) async-start(), calls=%async_computation.2 | async-start | bytes 2162688 | tf_op jit(solution)/shard_map/all_gather | solution.py:16
  7.3 173.8 %reduce-scatter.7.cloned.1.call-start = ((), (), s32[]{:S(2)}) async-start(), calls=%async_computation.4 | async-start | bytes 4128768 | tf_op jit(solution)/shard_map/reduce_scatter | solution.py:21
  13.4 64.7 %copy-start.4 = (f32[16,7]{0,1:T(8,128)S(1)}, f32[16,7]{0,1:T(8,128)}, u32[]{:S(2)}) copy-start(f32[16,7]{0,1:T(8,128)} %param.9) | copy-start | bytes 1348
  78.1 2.0 copy-start.1
  78.1 2.7 copy-start.2
  80.9 2.6 copy-start.5
  83.4 2.0 copy-start
  95.3 117.6 %copy-start.6 = (f32[7,16]{1,0:T(8,128)S(1)}, f32[7,16]{1,0:T(8,128)}, u32[]{:S(2)}) copy-start(f32[7,16]{1,0:T(8,128)} %param.13) | copy-start | bytes 1348
  95.4 249.6 %reduce-scatter.5.cloned.1.call-start = ((), (), s32[]{:S(2)}) async-start(), calls=%async_computation.3 | async-start | bytes 4325376 | tf_op jit(solution)/shard_map/reduce_scatter | solution.py:37
  212.9 2.0 copy-start.3
Sparse Core Ops, SparseCore 0:
  9.2 68.8 all-gather.1
  95.5 85.4 reduce-scatter.6
  219.9 124.9 reduce-scatter.4
where the time goes:
time: 357 us; the launch traced here: 353 us
  waiting for transfers between devices  270 us (76%)
  blocking collectives  30.8 us (9%)
  local copies, waits for them, and re-layouts  24.2 us (7%)
  between operations  13.2 us (4%)
  matrix products  9.92 us (3%)
  other arithmetic  4.85 us (1%)
    reduce_scatter x1, waiting for transfers between devices, local(): lax.psum_scatter(jnp.dot(picked, down_weight, preferred_element_type=jnp....  125 us
    reduce_scatter x1, waiting for transfers between devices, local(): lax.psum_scatter(jnp.concatenate([jnp.dot(picked, gate_weight, preferred_...  85.6 us
    all_gather x1, waiting for transfers between devices, local(): features = lax.all_gather(tokens, 'col', axis=0, tiled=True)  58.5 us
    all_gather x1, blocking collectives, local(): hidden = lax.all_gather(local_hidden, 'row', axis=0, tiled=True)  30.8 us
    unnamed x17, local copies, waits for them, and re-layouts  22.6 us
  transfers between devices with their start and end apart: 3, of which 3 were waited for; matrix products, arithmetic and copies ran while one was open for 3% of the time, Pallas kernels for 0%

commit v1 on v0

v1 whole, which is shorter than its diff:
```python
import jax
import jax.numpy as jnp
from jax import lax
from jax.experimental import pallas as pl
from jax.experimental.pallas import tpu as pltpu
from jax.sharding import Mesh, PartitionSpec as P

BLOCK = 128
COL = ("z", "yl", "core")
ROW = ("x", "yh")
LIMIT = 48 * 1024 * 1024


def shift(value, axis, count, by):
    return lax.ppermute(value, axis, [(i, (i + by) % count) for i in range(count)])


def dequant(quant, scale):
    parts = []
    for i in range(quant.shape[0] // BLOCK):
        rows = quant[i * BLOCK : (i + 1) * BLOCK, :].astype(jnp.float32)
        parts.append((rows * scale(i)).astype(jnp.bfloat16))
    return jnp.concatenate(parts, axis=0)


def gate_up_kernel(me, gate_scale, up_scale, *refs):
    pieces, gate, up = refs[:4], refs[4], refs[5]
    outs, features = refs[6:14], refs[14]
    step = pl.program_id(0)

    @pl.when(step == 0)
    def _():
        for chunk in range(8):
            slot = lax.rem(chunk + 8 - me[0], 8)
            rows = pieces[chunk // 2][64 * (chunk % 2) : 64 * (chunk % 2 + 1), :]
            features[pl.ds(pl.multiple_of(slot * 64, 64), 64), :] = rows

    weight = jnp.concatenate(
        [
            dequant(gate[...], lambda i: gate_scale[i, step]),
            dequant(up[...], lambda i: up_scale[i, step]),
        ],
        axis=1,
    )
    total = jnp.dot(features[...], weight, preferred_element_type=jnp.float32)
    for k, out in enumerate(outs):
        out[...] = total[64 * k : 64 * (k + 1)].astype(jnp.bfloat16)


def gate_up(me, pieces, gate, gate_scale, up, up_scale):
    depth, width = gate.shape
    whole = pl.BlockSpec((128, depth), lambda j, *_: (0, 0))
    column = pl.BlockSpec((depth, BLOCK), lambda j, *_: (0, j))
    return pl.pallas_call(
        gate_up_kernel,
        grid_spec=pltpu.PrefetchScalarGridSpec(
            num_scalar_prefetch=3,
            grid=(width // BLOCK,),
            in_specs=[whole] * 4 + [column] * 2,
            out_specs=[pl.BlockSpec((64, 2 * BLOCK), lambda j, *_: (0, j))] * 8,
            scratch_shapes=[pltpu.VMEM((512, depth), jnp.bfloat16)],
        ),
        out_shape=[jax.ShapeDtypeStruct((64, 2 * width), jnp.bfloat16)] * 8,
        compiler_params=pltpu.CompilerParams(vmem_limit_bytes=LIMIT),
        cost_estimate=pl.CostEstimate(
            flops=2 * 512 * depth * 2 * width, bytes_accessed=12 * 1024 * 1024, transcendentals=0
        ),
        name="gate_up",
    )(me, gate_scale, up_scale, *pieces, gate, up)


def silu_kernel(*refs):
    parts, out = refs[:-1], refs[-1]
    for j in range(out.shape[1] // BLOCK):
        at = slice(2 * j * BLOCK, 2 * (j + 1) * BLOCK)
        total = parts[0][:, at].astype(jnp.float32)
        for part in parts[1:]:
            total = total + part[:, at].astype(jnp.float32)
        gate, up = total[:, :BLOCK], total[:, BLOCK:]
        out[:, j * BLOCK : (j + 1) * BLOCK] = (gate / (1.0 + jnp.exp(-gate)) * up).astype(jnp.bfloat16)


def hidden_of(parts):
    rows, width = parts[0].shape
    return pl.pallas_call(
        silu_kernel,
        out_shape=jax.ShapeDtypeStruct((rows, width // 2), jnp.bfloat16),
        compiler_params=pltpu.CompilerParams(vmem_limit_bytes=LIMIT),
        name="hidden",
    )(*parts)


def down_kernel(me, scale, *refs):
    pieces, quant = refs[:8], refs[8]
    keep, send, hidden = refs[9:12]
    step = pl.program_id(0)

    @pl.when(step == 0)
    def _():
        for k, piece in enumerate(pieces):
            chunk = lax.rem(me[0] + 8 - k, 8)
            hidden[pl.ds(pl.multiple_of(chunk * 64, 64), 64), :] = piece[...]

    weight = jnp.concatenate(
        [
            dequant(quant[:, :BLOCK], lambda i: scale[i, 2 * step]),
            dequant(quant[:, BLOCK:], lambda i: scale[i, 2 * step + 1]),
        ],
        axis=1,
    )
    total = jnp.dot(hidden[...], weight, preferred_element_type=jnp.float32)
    keep[...] = total[:256].astype(jnp.bfloat16)
    send[...] = total[256:].astype(jnp.bfloat16)


def down(me, pieces, quant, scale):
    depth, width = quant.shape
    whole = pl.BlockSpec((64, depth), lambda j, *_: (0, 0))
    out = pl.BlockSpec((256, 2 * BLOCK), lambda j, *_: (0, j))
    return pl.pallas_call(
        down_kernel,
        grid_spec=pltpu.PrefetchScalarGridSpec(
            num_scalar_prefetch=2,
            grid=(width // (2 * BLOCK),),
            in_specs=[whole] * 8 + [pl.BlockSpec((depth, 2 * BLOCK), lambda j, *_: (0, j))],
            out_specs=[out] * 2,
            scratch_shapes=[pltpu.VMEM((512, depth), jnp.bfloat16)],
        ),
        out_shape=[jax.ShapeDtypeStruct((256, width), jnp.bfloat16)] * 2,
        compiler_params=pltpu.CompilerParams(vmem_limit_bytes=LIMIT),
        cost_estimate=pl.CostEstimate(
            flops=2 * 512 * depth * width, bytes_accessed=7 * 1024 * 1024, transcendentals=0
        ),
        name="down",
    )(me, scale, *pieces, quant)


def add(a, b):
    return (a.astype(jnp.float32) + b.astype(jnp.float32)).astype(jnp.bfloat16)


def local(tokens, gate_quant, gate_scale, up_quant, up_scale, down_quant, down_scale):
    me = (lax.axis_index("x") * 2 + lax.axis_index("yh")).astype(jnp.int32).reshape(1)
    own = jnp.concatenate([tokens] + [shift(tokens, "z", 8, k) for k in range(1, 8)], axis=0)
    own_core = shift(own, "core", 2, 1)
    other = shift(own, "yl", 2, 1)
    other_core = shift(other, "core", 2, 1)
    sums = gate_up(me, [own, other, own_core, other_core], gate_quant, gate_scale, up_quant, up_scale)
    hidden = hidden_of([sums[0]] + [shift(sums[k], ROW, 8, k) for k in range(1, 8)])
    pieces = [hidden] + [shift(hidden, ROW, 8, k) for k in range(1, 8)]
    keep, send = down(me, pieces, down_quant, down_scale)
    got = shift(send, "core", 2, 1)
    near = add(keep[:128], got[:128])
    far = add(keep[128:], got[128:])
    total = add(near, shift(far, "yl", 2, 1))
    mixed = total[:16].astype(jnp.float32)
    for k in range(1, 8):
        mixed = mixed + shift(total[16 * k : 16 * (k + 1)], "z", 8, -k).astype(jnp.float32)
    return mixed.astype(jnp.bfloat16)


def solution(mesh):
    fine = Mesh(mesh.devices.reshape(4, 2, 8, 2, 2), ROW + COL)
    placed = (
        P(COL, ROW),
        P(ROW, COL),
        P(ROW, COL),
        P(ROW, COL),
        P(ROW, COL),
        P(COL, ROW),
        P(COL, ROW),
    )
    return jax.shard_map(
        local, mesh=fine, in_specs=placed, out_specs=P(COL, ROW), check_vma=False
    )
```

time: 357 us -> 153 us (0.43); the launches traced: 353 us -> 153 us
  waiting for transfers between devices: 270 us -> 62.6 us
  starting transfers between devices: 0.08 us -> 69.7 us
  blocking collectives: 30.8 us -> 0 us
  local copies, waits for them, and re-layouts: 24.2 us -> 2.48 us
  Pallas kernels: 0 us -> 16.7 us
  between operations: 13.2 us -> 0.13 us
  matrix products: 9.92 us -> 0 us
  other arithmetic: 4.85 us -> 1.06 us
    reduce_scatter x2 -> x0, waiting for transfers between devices: 211 us -> none  [the longest x1 125 us: local(): lax.psum_scatter(jnp.dot(picked, down_weight, preferred_element_type=jnp....]
    ppermute x0 -> x33, starting transfers between devices: none -> 69.7 us  [shift(): lax.ppermute(value, axis, [(i, (i + by) % count) for i in range(count)])]
    ppermute x0 -> x33, waiting for transfers between devices: none -> 62.6 us  [shift(): lax.ppermute(value, axis, [(i, (i + by) % count) for i in range(count)])]
    all_gather x1 -> x0, waiting for transfers between devices: 58.5 us -> none  [local(): features = lax.all_gather(tokens, 'col', axis=0, tiled=True)]
    all_gather x1 -> x0, blocking collectives: 30.8 us -> none  [local(): hidden = lax.all_gather(local_hidden, 'row', axis=0, tiled=True)]
    unnamed x17 -> x11, local copies, waits for them, and re-layouts: 22.6 us -> 2.44 us
    pallas_call x0 -> x3, Pallas kernels: none -> 16.7 us  [the longest x1 9.04 us: gate_up(): pl.pallas_call(gate_up_kernel, grid_spec=pltpu.PrefetchScalarGridSpec(num...]
    dot_general x3 -> x0, matrix products: 9.92 us -> none  [the longest x1 4.82 us: local(): jnp.dot(picked, down_weight, preferred_element_type=jnp.float32)]
  transfers between devices with their start and end apart: 3 -> 33, of which waited for: 3 -> 14; matrix products, arithmetic and copies ran while one was open for 3% -> 2% of each run, Pallas kernels for 0% -> 0%
where the time goes in v1:
time: 153 us
  starting transfers between devices  69.7 us (46%)
  waiting for transfers between devices  62.6 us (41%)
  Pallas kernels  16.7 us (11%)
  local copies, waits for them, and re-layouts  2.48 us (2%)
    ppermute x33, starting transfers between devices, shift(): lax.ppermute(value, axis, [(i, (i + by) % count) for i in range(count)])  69.7 us
    ppermute x33, waiting for transfers between devices, shift(): lax.ppermute(value, axis, [(i, (i + by) % count) for i in range(count)])  62.6 us
    pallas_call x1, Pallas kernels, gate_up(): pl.pallas_call(gate_up_kernel, grid_spec=pltpu.PrefetchScalarGridSpec(num...  9.04 us
    pallas_call x1, Pallas kernels, down(): pl.pallas_call(down_kernel, grid_spec=pltpu.PrefetchScalarGridSpec(num_sc...  7.33 us
  transfers between devices with their start and end apart: 33, of which 14 were waited for; matrix products, arithmetic and copies ran while one was open for 2% of the time, Pallas kernels for 0%

profile of v1, /device:TPU:1, one launch (start us, length us, event | category | flops | bytes accessed | tf_op | source)
XLA Modules:
  0.0 152.7 jit_solution(6561376732857888604)
XLA Ops:
  0.0 6.8 %collective-permute-start.5 = (bf16[16,2048]{1,0:T(8,128)(2,1)}, bf16[16,2048]{1,0:T(8,128)(2,1)S(1)}, u32[]{:S(2)}, u32[]{:S(2)}) collective-permute-start(bf16[16,2048]{1,0:T(8,128)(2,1)} %param.7), channel_id=1, source_target_pairs={{0,24},{4,28},{8,0},{12,4},{16,8},{20,12},{24,16},{28,20},{1,25},{... | collective-permute-start | bytes 196616 | tf_op jit(solution)/shard_map/ppermute | solution.py:15
  7.6 4.2 %collective-permute-start.3 = (bf16[16,2048]{1,0:T(8,128)(2,1)}, bf16[16,2048]{1,0:T(8,128)(2,1)S(1)}, u32[]{:S(2)}, u32[]{:S(2)}) collective-permute-start(bf16[16,2048]{1,0:T(8,128)(2,1)} %param.7), channel_id=1, source_target_pairs={{0,16},{4,20},{8,24},{12,28},{16,0},{20,4},{24,8},{28,12},{1,17},{... | collective-permute-start | bytes 196616 | tf_op jit(solution)/shard_map/ppermute | solution.py:15
  14.1 7.2 %collective-permute-done = bf16[16,2048]{1,0:T(8,128)(2,1)S(1)} collective-permute-done((bf16[16,2048]{1,0:T(8,128)(2,1)}, bf16[16,2048]{1,0:T(8,128)(2,1)S(1)}, u32[]{:S(2)}, u32[]{:S(2)}) %collective-permute-start) | collective-permute-done | bytes 65568 | tf_op jit(solution)/shard_map/ppermute | solution.py:15
  21.3 2.6 %collective-permute-start.1 = (bf16[16,2048]{1,0:T(8,128)(2,1)}, bf16[16,2048]{1,0:T(8,128)(2,1)S(1)}, u32[]{:S(2)}, u32[]{:S(2)}) collective-permute-start(bf16[16,2048]{1,0:T(8,128)(2,1)} %param.7), channel_id=1, source_target_pairs={{0,8},{4,12},{8,16},{12,20},{16,24},{20,28},{24,0},{28,4},{1,9},{5... | collective-permute-start | bytes 196616 | tf_op jit(solution)/shard_map/ppermute | solution.py:15
  23.9 3.0 %collective-permute-done.1 = bf16[16,2048]{1,0:T(8,128)(2,1)S(1)} collective-permute-done((bf16[16,2048]{1,0:T(8,128)(2,1)}, bf16[16,2048]{1,0:T(8,128)(2,1)S(1)}, u32[]{:S(2)}, u32[]{:S(2)}) %collective-permute-start.1) | collective-permute-done | bytes 65568 | tf_op jit(solution)/shard_map/ppermute | solution.py:15
  27.2 3.0 %collective-permute-done.6 = bf16[16,2048]{1,0:T(8,128)(2,1)S(1)} collective-permute-done((bf16[16,2048]{1,0:T(8,128)(2,1)}, bf16[16,2048]{1,0:T(8,128)(2,1)S(1)}, u32[]{:S(2)}, u32[]{:S(2)}) %collective-permute-start.6) | collective-permute-done | bytes 65568 | tf_op jit(solution)/shard_map/ppermute | solution.py:15
  31.5 4.4 %collective-permute-start.8 = (bf16[128,2048]{1,0:T(8,128)(2,1)S(1)}, bf16[128,2048]{1,0:T(8,128)(2,1)S(1)}, u32[]{:S(2)}, u32[]{:S(2)}) collective-permute-start(bf16[128,2048]{1,0:T(8,128)(2,1)S(1)} %constant_dynamic-update-slice_fusion.refs_0_), channel_id=1, source_target_pairs={{0,1},{1,0},{2,3},{3,2},{4,5},{5,4},{6,7},{7,6},{8,9},{9,8},{10,11... | collective-permute-start | bytes 1572872 | tf_op jit(solution)/shard_map/ppermute | solution.py:15
  35.9 3.6 %collective-permute-done.7.refs_1_ = bf16[128,2048]{1,0:T(8,128)(2,1)S(1)} collective-permute-done((bf16[128,2048]{1,0:T(8,128)(2,1)S(1)}, bf16[128,2048]{1,0:T(8,128)(2,1)S(1)}, u32[]{:S(2)}, u32[]{:S(2)}) %collective-permute-start.7) | collective-permute-done | bytes 524320 | tf_op jit(solution)/shard_map/ppermute | solution.py:15
  39.5 5.1 %collective-permute-start.9 = (bf16[128,2048]{1,0:T(8,128)(2,1)S(1)}, bf16[128,2048]{1,0:T(8,128)(2,1)S(1)}, u32[]{:S(2)}, u32[]{:S(2)}) collective-permute-start(bf16[128,2048]{1,0:T(8,128)(2,1)S(1)} %collective-permute-done.7.refs_1_), channel_id=1, source_target_pairs={{0,1},{1,0},{2,3},{3,2},{4,5},{5,4},{6,7},{7,6},{8,9},{9,8},{10,11... | collective-permute-start | bytes 1572872 | tf_op jit(solution)/shard_map/ppermute | solution.py:15
  46.1 9.0 %gate_up.1 = (bf16[64,1792]{1,0:T(8,128)(2,1)S(1)}, bf16[64,1792]{1,0:T(8,128)(2,1)S(1)}, bf16[64,1792]{1,0:T(8,128)(2,1)S(1)}, bf16[64,1792]{1,0:T(8,128)(2,1)S...) custom-call(s32[1]{0:T(128)} %bitcast.me, ...), custom_call_target="tpu_custom_call" | custom-call | flops 3758096384 | bytes 12582912 | tf_op jit(solution)/shard_map/gate_up/pallas_call | solution.py:54
  55.2 3.0 %collective-permute-start.10 = (bf16[64,1792]{1,0:T(8,128)(2,1)S(1)}, bf16[64,1792]{1,0:T(8,128)(2,1)S(1)}, u32[]{:S(2)}, u32[]{:S(2)}) collective-permute-start(bf16[64,1792]{1,0:T(8,128)(2,1)S(1)} %get-tuple-element.16), channel_id=1, source_target_pairs={{0,32},{32,64},{64,96},{96,128},{128,160},{160,192},{192,224},{224... | collective-permute-start | bytes 688136 | tf_op jit(solution)/shard_map/ppermute | solution.py:15
  61.0 1.7 %collective-permute-start.13 = (bf16[64,1792]{1,0:T(8,128)(2,1)S(1)}, bf16[64,1792]{1,0:T(8,128)(2,1)S(1)}, u32[]{:S(2)}, u32[]{:S(2)}) collective-permute-start(bf16[64,1792]{1,0:T(8,128)(2,1)S(1)} %get-tuple-element.19), channel_id=1, source_target_pairs={{0,128},{32,160},{64,192},{96,224},{128,0},{160,32},{192,64},{224,... | collective-permute-start | bytes 688136 | tf_op jit(solution)/shard_map/ppermute | solution.py:15
  62.7 4.5 %collective-permute-start.14 = (bf16[64,1792]{1,0:T(8,128)(2,1)S(1)}, bf16[64,1792]{1,0:T(8,128)(2,1)S(1)}, u32[]{:S(2)}, u32[]{:S(2)}) collective-permute-start(bf16[64,1792]{1,0:T(8,128)(2,1)S(1)} %get-tuple-element.20), channel_id=1, source_target_pairs={{0,160},{32,192},{64,224},{96,0},{128,32},{160,64},{192,96},{224,1... | collective-permute-start | bytes 688136 | tf_op jit(solution)/shard_map/ppermute | solution.py:15
  68.4 3.5 %collective-permute-start.16 = (bf16[64,1792]{1,0:T(8,128)(2,1)S(1)}, bf16[64,1792]{1,0:T(8,128)(2,1)S(1)}, u32[]{:S(2)}, u32[]{:S(2)}) collective-permute-start(bf16[64,1792]{1,0:T(8,128)(2,1)S(1)} %get-tuple-element.22), channel_id=1, source_target_pairs={{0,224},{32,0},{64,32},{96,64},{128,96},{160,128},{192,160},{224,1... | collective-permute-start | bytes 688136 | tf_op jit(solution)/shard_map/ppermute | solution.py:15
  71.9 5.7 %collective-permute-done.12.refs_3_ = bf16[64,1792]{1,0:T(8,128)(2,1)S(1)} collective-permute-done((bf16[64,1792]{1,0:T(8,128)(2,1)S(1)}, bf16[64,1792]{1,0:T(8,128)(2,1)S(1)}, u32[]{:S(2)}, u32[]{:S(2)}) %collective-permute-start.12) | collective-permute-done | bytes 229408 | tf_op jit(solution)/shard_map/ppermute | solution.py:15
  77.6 3.2 %collective-permute-done.14.refs_5_ = bf16[64,1792]{1,0:T(8,128)(2,1)S(1)} collective-permute-done((bf16[64,1792]{1,0:T(8,128)(2,1)S(1)}, bf16[64,1792]{1,0:T(8,128)(2,1)S(1)}, u32[]{:S(2)}, u32[]{:S(2)}) %collective-permute-start.14) | collective-permute-done | bytes 229408 | tf_op jit(solution)/shard_map/ppermute | solution.py:15
  80.8 5.5 %collective-permute-done.16.refs_7_ = bf16[64,1792]{1,0:T(8,128)(2,1)S(1)} collective-permute-done((bf16[64,1792]{1,0:T(8,128)(2,1)S(1)}, bf16[64,1792]{1,0:T(8,128)(2,1)S(1)}, u32[]{:S(2)}, u32[]{:S(2)}) %collective-permute-start.16) | collective-permute-done | bytes 229408 | tf_op jit(solution)/shard_map/ppermute | solution.py:15
  86.7 2.7 %collective-permute-start.23 = (bf16[64,896]{1,0:T(8,128)(2,1)S(1)}, bf16[64,896]{1,0:T(8,128)(2,1)S(1)}, u32[]{:S(2)}, u32[]{:S(2)}) collective-permute-start(bf16[64,896]{1,0:T(8,128)(2,1)S(1)} %hidden.1.refs_0_), channel_id=1, source_target_pairs={{0,224},{32,0},{64,32},{96,64},{128,96},{160,128},{192,160},{224,1... | collective-permute-start | bytes 344072 | tf_op jit(solution)/shard_map/ppermute | solution.py:15
  90.6 1.8 %collective-permute-start.20 = (bf16[64,896]{1,0:T(8,128)(2,1)S(1)}, bf16[64,896]{1,0:T(8,128)(2,1)S(1)}, u32[]{:S(2)}, u32[]{:S(2)}) collective-permute-start(bf16[64,896]{1,0:T(8,128)(2,1)S(1)} %hidden.1.refs_0_), channel_id=1, source_target_pairs={{0,128},{32,160},{64,192},{96,224},{128,0},{160,32},{192,64},{224,... | collective-permute-start | bytes 344072 | tf_op jit(solution)/shard_map/ppermute | solution.py:15
  92.4 2.5 %collective-permute-start.19 = (bf16[64,896]{1,0:T(8,128)(2,1)S(1)}, bf16[64,896]{1,0:T(8,128)(2,1)S(1)}, u32[]{:S(2)}, u32[]{:S(2)}) collective-permute-start(bf16[64,896]{1,0:T(8,128)(2,1)S(1)} %hidden.1.refs_0_), channel_id=1, source_target_pairs={{0,96},{32,128},{64,160},{96,192},{128,224},{160,0},{192,32},{224,... | collective-permute-start | bytes 344072 | tf_op jit(solution)/shard_map/ppermute | solution.py:15
  95.0 2.2 %collective-permute-start.17 = (bf16[64,896]{1,0:T(8,128)(2,1)S(1)}, bf16[64,896]{1,0:T(8,128)(2,1)S(1)}, u32[]{:S(2)}, u32[]{:S(2)}) collective-permute-start(bf16[64,896]{1,0:T(8,128)(2,1)S(1)} %hidden.1.refs_0_), channel_id=1, source_target_pairs={{0,32},{32,64},{64,96},{96,128},{128,160},{160,192},{192,224},{224... | collective-permute-start | bytes 344072 | tf_op jit(solution)/shard_map/ppermute | solution.py:15
  97.1 3.9 %collective-permute-done.19.refs_3_ = bf16[64,896]{1,0:T(8,128)(2,1)S(1)} collective-permute-done((bf16[64,896]{1,0:T(8,128)(2,1)S(1)}, bf16[64,896]{1,0:T(8,128)(2,1)S(1)}, u32[]{:S(2)}, u32[]{:S(2)}) %collective-permute-start.19) | collective-permute-done | bytes 114720 | tf_op jit(solution)/shard_map/ppermute | solution.py:15
  101.1 5.4 %collective-permute-done.17.refs_1_ = bf16[64,896]{1,0:T(8,128)(2,1)S(1)} collective-permute-done((bf16[64,896]{1,0:T(8,128)(2,1)S(1)}, bf16[64,896]{1,0:T(8,128)(2,1)S(1)}, u32[]{:S(2)}, u32[]{:S(2)}) %collective-permute-start.17) | collective-permute-done | bytes 114720 | tf_op jit(solution)/shard_map/ppermute | solution.py:15
  106.4 7.3 %down.1 = (bf16[256,2048]{1,0:T(8,128)(2,1)S(1)}, bf16[256,2048]{1,0:T(8,128)(2,1)S(1)}) custom-call(s32[1]{0:T(128)} %bitcast.me, f32[7,16]{1,0:T(8,128)S(1)} %copy-done, bf16[64,896]{1,0:T(8,128)(2,1)S(1)} %hidden.1.refs_0_, bf16[64,896]{1,0:T(8,128)(2,1)S(1)} %collective-permute-done.17.refs_1_, bf16[64,896]{1,0:T(8,128)(2,1)S(1)} %collective-permute-done.18.refs_2_, ...), custom_call_target="tpu_custom_call" | custom-call | flops 1879048192 | bytes 7340032 | tf_op jit(solution)/shard_map/down/pallas_call | solution.py:120
  113.8 1.7 %collective-permute-start.24 = (bf16[256,2048]{1,0:T(8,128)(2,1)S(1)}, bf16[256,2048]{1,0:T(8,128)(2,1)S(1)}, u32[]{:S(2)}, u32[]{:S(2)}) collective-permute-start(bf16[256,2048]{1,0:T(8,128)(2,1)S(1)} %get-tuple-element.24), channel_id=1, source_target_pairs={{0,1},{1,0},{2,3},{3,2},{4,5},{5,4},{6,7},{7,6},{8,9},{9,8},{10,11... | collective-permute-start | bytes 3145736 | tf_op jit(solution)/shard_map/ppermute | solution.py:15
  115.5 2.3 %collective-permute-done.24 = bf16[256,2048]{1,0:T(8,128)(2,1)S(1)} collective-permute-done((bf16[256,2048]{1,0:T(8,128)(2,1)S(1)}, bf16[256,2048]{1,0:T(8,128)(2,1)S(1)}, u32[]{:S(2)}, u32[]{:S(2)}) %collective-permute-start.24) | collective-permute-done | bytes 1048608 | tf_op jit(solution)/shard_map/ppermute | solution.py:15
  118.6 12.5 %collective-permute-done.25 = bf16[128,2048]{1,0:T(8,128)(2,1)S(1)} collective-permute-done((bf16[128,2048]{1,0:T(8,128)(2,1)S(1)}, bf16[128,2048]{1,0:T(8,128)(2,1)S(1)}, u32[]{:S(2)}, u32[]{:S(2)}) %collective-permute-start.25) | collective-permute-done | bytes 524320 | tf_op jit(solution)/shard_map/ppermute | solution.py:15
  132.9 2.3 %collective-permute-start.31 = (bf16[16,2048]{1,0:T(8,128)(2,1)S(1)}, bf16[16,2048]{1,0:T(8,128)(2,1)S(1)}, u32[]{:S(2)}, u32[]{:S(2)}) collective-permute-start(bf16[16,2048]{1,0:T(8,128)(2,1)S(1)} %get-tuple-element.27), channel_id=1, source_target_pairs={{0,8},{4,12},{8,16},{12,20},{16,24},{20,28},{24,0},{28,4},{1,9},{5... | collective-permute-start | bytes 196616 | tf_op jit(solution)/shard_map/ppermute | solution.py:15
  136.7 2.9 %collective-permute-start.29 = (bf16[16,2048]{1,0:T(8,128)(2,1)S(1)}, bf16[16,2048]{1,0:T(8,128)(2,1)S(1)}, u32[]{:S(2)}, u32[]{:S(2)}) collective-permute-start(bf16[16,2048]{1,0:T(8,128)(2,1)S(1)} %get-tuple-element.29), channel_id=1, source_target_pairs={{0,16},{4,20},{8,24},{12,28},{16,0},{20,4},{24,8},{28,12},{1,17},{... | collective-permute-start | bytes 196616 | tf_op jit(solution)/shard_map/ppermute | solution.py:15
  141.2 3.5 %collective-permute-start.27 = (bf16[16,2048]{1,0:T(8,128)(2,1)S(1)}, bf16[16,2048]{1,0:T(8,128)(2,1)S(1)}, u32[]{:S(2)}, u32[]{:S(2)}) collective-permute-start(bf16[16,2048]{1,0:T(8,128)(2,1)S(1)} %get-tuple-element.31), channel_id=1, source_target_pairs={{0,24},{4,28},{8,0},{12,4},{16,8},{20,12},{24,16},{28,20},{1,25},{... | collective-permute-start | bytes 196616 | tf_op jit(solution)/shard_map/ppermute | solution.py:15
  144.8 1.7 %collective-permute-done.29 = bf16[16,2048]{1,0:T(8,128)(2,1)S(1)} collective-permute-done((bf16[16,2048]{1,0:T(8,128)(2,1)S(1)}, bf16[16,2048]{1,0:T(8,128)(2,1)S(1)}, u32[]{:S(2)}, u32[]{:S(2)}) %collective-permute-start.29) | collective-permute-done | bytes 65568 | tf_op jit(solution)/shard_map/ppermute | solution.py:15
  146.4 5.5 %collective-permute-done.27 = bf16[16,2048]{1,0:T(8,128)(2,1)S(1)} collective-permute-done((bf16[16,2048]{1,0:T(8,128)(2,1)S(1)}, bf16[16,2048]{1,0:T(8,128)(2,1)S(1)}, u32[]{:S(2)}, u32[]{:S(2)}) %collective-permute-start.27) | collective-permute-done | bytes 65568 | tf_op jit(solution)/shard_map/ppermute | solution.py:15
  (53 shorter events, 18.3 us)
Async XLA Ops:
  0.0 27.2 %collective-permute-start.5 = (bf16[16,2048]{1,0:T(8,128)(2,1)}, bf16[16,2048]{1,0:T(8,128)(2,1)S(1)}, u32[]{:S(2)}, u32[]{:S(2)}) collective-permute-start(bf16[16,2048]{1,0:T(8,128)(2,1)} %param.7), channel_id=1, source_target_pairs={{0,24},{4,28},{8,0},{12,4},{16,8},{20,12},{24,16},{28,20},{1,25},{... | collective-permute-start | bytes 196616 | tf_op jit(solution)/shard_map/ppermute | solution.py:15
  6.9 20.3 %collective-permute-start.4 = (bf16[16,2048]{1,0:T(8,128)(2,1)}, bf16[16,2048]{1,0:T(8,128)(2,1)S(1)}, u32[]{:S(2)}, u32[]{:S(2)}) collective-permute-start(bf16[16,2048]{1,0:T(8,128)(2,1)} %param.7), channel_id=1, source_target_pairs={{0,20},{4,24},{8,28},{12,0},{16,4},{20,8},{24,12},{28,16},{1,21},{... | collective-permute-start | bytes 196616 | tf_op jit(solution)/shard_map/ppermute | solution.py:15
  7.6 19.5 %collective-permute-start.3 = (bf16[16,2048]{1,0:T(8,128)(2,1)}, bf16[16,2048]{1,0:T(8,128)(2,1)S(1)}, u32[]{:S(2)}, u32[]{:S(2)}) collective-permute-start(bf16[16,2048]{1,0:T(8,128)(2,1)} %param.7), channel_id=1, source_target_pairs={{0,16},{4,20},{8,24},{12,28},{16,0},{20,4},{24,8},{28,12},{1,17},{... | collective-permute-start | bytes 196616 | tf_op jit(solution)/shard_map/ppermute | solution.py:15
  11.8 15.3 %collective-permute-start.2 = (bf16[16,2048]{1,0:T(8,128)(2,1)}, bf16[16,2048]{1,0:T(8,128)(2,1)S(1)}, u32[]{:S(2)}, u32[]{:S(2)}) collective-permute-start(bf16[16,2048]{1,0:T(8,128)(2,1)} %param.7), channel_id=1, source_target_pairs={{0,12},{4,16},{8,20},{12,24},{16,28},{20,0},{24,4},{28,8},{1,13},{... | collective-permute-start | bytes 196616 | tf_op jit(solution)/shard_map/ppermute | solution.py:15
  11.8 9.5 %collective-permute-start = (bf16[16,2048]{1,0:T(8,128)(2,1)}, bf16[16,2048]{1,0:T(8,128)(2,1)S(1)}, u32[]{:S(2)}, u32[]{:S(2)}) collective-permute-start(bf16[16,2048]{1,0:T(8,128)(2,1)} %param.7), channel_id=1, source_target_pairs={{0,4},{4,8},{8,12},{12,16},{16,20},{20,24},{24,28},{28,0},{1,5},{5... | collective-permute-start | bytes 196616 | tf_op jit(solution)/shard_map/ppermute | solution.py:15
  21.3 5.6 %collective-permute-start.1 = (bf16[16,2048]{1,0:T(8,128)(2,1)}, bf16[16,2048]{1,0:T(8,128)(2,1)S(1)}, u32[]{:S(2)}, u32[]{:S(2)}) collective-permute-start(bf16[16,2048]{1,0:T(8,128)(2,1)} %param.7), channel_id=1, source_target_pairs={{0,8},{4,12},{8,16},{12,20},{16,24},{20,28},{24,0},{28,4},{1,9},{5... | collective-permute-start | bytes 196616 | tf_op jit(solution)/shard_map/ppermute | solution.py:15
  30.2 9.3 %collective-permute-start.7 = (bf16[128,2048]{1,0:T(8,128)(2,1)S(1)}, bf16[128,2048]{1,0:T(8,128)(2,1)S(1)}, u32[]{:S(2)}, u32[]{:S(2)}) collective-permute-start(bf16[128,2048]{1,0:T(8,128)(2,1)S(1)} %constant_dynamic-update-slice_fusion.refs_0_), channel_id=1, source_target_pairs={{0,2},{2,0},{1,3},{3,1},{4,6},{6,4},{5,7},{7,5},{8,10},{10,8},{9,1... | collective-permute-start | bytes 1572872 | tf_op jit(solution)/shard_map/ppermute | solution.py:15
  31.5 14.6 %collective-permute-start.8 = (bf16[128,2048]{1,0:T(8,128)(2,1)S(1)}, bf16[128,2048]{1,0:T(8,128)(2,1)S(1)}, u32[]{:S(2)}, u32[]{:S(2)}) collective-permute-start(bf16[128,2048]{1,0:T(8,128)(2,1)S(1)} %constant_dynamic-update-slice_fusion.refs_0_), channel_id=1, source_target_pairs={{0,1},{1,0},{2,3},{3,2},{4,5},{5,4},{6,7},{7,6},{8,9},{9,8},{10,11... | collective-permute-start | bytes 1572872 | tf_op jit(solution)/shard_map/ppermute | solution.py:15
  39.5 6.6 %collective-permute-start.9 = (bf16[128,2048]{1,0:T(8,128)(2,1)S(1)}, bf16[128,2048]{1,0:T(8,128)(2,1)S(1)}, u32[]{:S(2)}, u32[]{:S(2)}) collective-permute-start(bf16[128,2048]{1,0:T(8,128)(2,1)S(1)} %collective-permute-done.7.refs_1_), channel_id=1, source_target_pairs={{0,1},{1,0},{2,3},{3,2},{4,5},{5,4},{6,7},{7,6},{8,9},{9,8},{10,11... | collective-permute-start | bytes 1572872 | tf_op jit(solution)/shard_map/ppermute | solution.py:15
  55.2 12.0 %collective-permute-start.10 = (bf16[64,1792]{1,0:T(8,128)(2,1)S(1)}, bf16[64,1792]{1,0:T(8,128)(2,1)S(1)}, u32[]{:S(2)}, u32[]{:S(2)}) collective-permute-start(bf16[64,1792]{1,0:T(8,128)(2,1)S(1)} %get-tuple-element.16), channel_id=1, source_target_pairs={{0,32},{32,64},{64,96},{96,128},{128,160},{160,192},{192,224},{224... | collective-permute-start | bytes 688136 | tf_op jit(solution)/shard_map/ppermute | solution.py:15
  58.2 10.2 %collective-permute-start.11 = (bf16[64,1792]{1,0:T(8,128)(2,1)S(1)}, bf16[64,1792]{1,0:T(8,128)(2,1)S(1)}, u32[]{:S(2)}, u32[]{:S(2)}) collective-permute-start(bf16[64,1792]{1,0:T(8,128)(2,1)S(1)} %get-tuple-element.17), channel_id=1, source_target_pairs={{0,64},{32,96},{64,128},{96,160},{128,192},{160,224},{192,0},{224,... | collective-permute-start | bytes 688136 | tf_op jit(solution)/shard_map/ppermute | solution.py:15
  59.4 18.2 %collective-permute-start.12 = (bf16[64,1792]{1,0:T(8,128)(2,1)S(1)}, bf16[64,1792]{1,0:T(8,128)(2,1)S(1)}, u32[]{:S(2)}, u32[]{:S(2)}) collective-permute-start(bf16[64,1792]{1,0:T(8,128)(2,1)S(1)} %get-tuple-element.18), channel_id=1, source_target_pairs={{0,96},{32,128},{64,160},{96,192},{128,224},{160,0},{192,32},{224,... | collective-permute-start | bytes 688136 | tf_op jit(solution)/shard_map/ppermute | solution.py:15
  61.0 16.6 %collective-permute-start.13 = (bf16[64,1792]{1,0:T(8,128)(2,1)S(1)}, bf16[64,1792]{1,0:T(8,128)(2,1)S(1)}, u32[]{:S(2)}, u32[]{:S(2)}) collective-permute-start(bf16[64,1792]{1,0:T(8,128)(2,1)S(1)} %get-tuple-element.19), channel_id=1, source_target_pairs={{0,128},{32,160},{64,192},{96,224},{128,0},{160,32},{192,64},{224,... | collective-permute-start | bytes 688136 | tf_op jit(solution)/shard_map/ppermute | solution.py:15
  62.7 18.1 %collective-permute-start.14 = (bf16[64,1792]{1,0:T(8,128)(2,1)S(1)}, bf16[64,1792]{1,0:T(8,128)(2,1)S(1)}, u32[]{:S(2)}, u32[]{:S(2)}) collective-permute-start(bf16[64,1792]{1,0:T(8,128)(2,1)S(1)} %get-tuple-element.20), channel_id=1, source_target_pairs={{0,160},{32,192},{64,224},{96,0},{128,32},{160,64},{192,96},{224,1... | collective-permute-start | bytes 688136 | tf_op jit(solution)/shard_map/ppermute | solution.py:15
  67.2 13.6 %collective-permute-start.15 = (bf16[64,1792]{1,0:T(8,128)(2,1)S(1)}, bf16[64,1792]{1,0:T(8,128)(2,1)S(1)}, u32[]{:S(2)}, u32[]{:S(2)}) collective-permute-start(bf16[64,1792]{1,0:T(8,128)(2,1)S(1)} %get-tuple-element.21), channel_id=1, source_target_pairs={{0,192},{32,224},{64,0},{96,32},{128,64},{160,96},{192,128},{224,1... | collective-permute-start | bytes 688136 | tf_op jit(solution)/shard_map/ppermute | solution.py:15
  68.4 18.0 %collective-permute-start.16 = (bf16[64,1792]{1,0:T(8,128)(2,1)S(1)}, bf16[64,1792]{1,0:T(8,128)(2,1)S(1)}, u32[]{:S(2)}, u32[]{:S(2)}) collective-permute-start(bf16[64,1792]{1,0:T(8,128)(2,1)S(1)} %get-tuple-element.22), channel_id=1, source_target_pairs={{0,224},{32,0},{64,32},{96,64},{128,96},{160,128},{192,160},{224,1... | collective-permute-start | bytes 688136 | tf_op jit(solution)/shard_map/ppermute | solution.py:15
  86.7 8.3 %collective-permute-start.23 = (bf16[64,896]{1,0:T(8,128)(2,1)S(1)}, bf16[64,896]{1,0:T(8,128)(2,1)S(1)}, u32[]{:S(2)}, u32[]{:S(2)}) collective-permute-start(bf16[64,896]{1,0:T(8,128)(2,1)S(1)} %hidden.1.refs_0_), channel_id=1, source_target_pairs={{0,224},{32,0},{64,32},{96,64},{128,96},{160,128},{192,160},{224,1... | collective-permute-start | bytes 344072 | tf_op jit(solution)/shard_map/ppermute | solution.py:15
  89.3 5.6 %collective-permute-start.22 = (bf16[64,896]{1,0:T(8,128)(2,1)S(1)}, bf16[64,896]{1,0:T(8,128)(2,1)S(1)}, u32[]{:S(2)}, u32[]{:S(2)}) collective-permute-start(bf16[64,896]{1,0:T(8,128)(2,1)S(1)} %hidden.1.refs_0_), channel_id=1, source_target_pairs={{0,192},{32,224},{64,0},{96,32},{128,64},{160,96},{192,128},{224,1... | collective-permute-start | bytes 344072 | tf_op jit(solution)/shard_map/ppermute | solution.py:15
  89.5 7.6 %collective-permute-start.21 = (bf16[64,896]{1,0:T(8,128)(2,1)S(1)}, bf16[64,896]{1,0:T(8,128)(2,1)S(1)}, u32[]{:S(2)}, u32[]{:S(2)}) collective-permute-start(bf16[64,896]{1,0:T(8,128)(2,1)S(1)} %hidden.1.refs_0_), channel_id=1, source_target_pairs={{0,160},{32,192},{64,224},{96,0},{128,32},{160,64},{192,96},{224,1... | collective-permute-start | bytes 344072 | tf_op jit(solution)/shard_map/ppermute | solution.py:15
  90.6 6.5 %collective-permute-start.20 = (bf16[64,896]{1,0:T(8,128)(2,1)S(1)}, bf16[64,896]{1,0:T(8,128)(2,1)S(1)}, u32[]{:S(2)}, u32[]{:S(2)}) collective-permute-start(bf16[64,896]{1,0:T(8,128)(2,1)S(1)} %hidden.1.refs_0_), channel_id=1, source_target_pairs={{0,128},{32,160},{64,192},{96,224},{128,0},{160,32},{192,64},{224,... | collective-permute-start | bytes 344072 | tf_op jit(solution)/shard_map/ppermute | solution.py:15
  92.4 8.6 %collective-permute-start.19 = (bf16[64,896]{1,0:T(8,128)(2,1)S(1)}, bf16[64,896]{1,0:T(8,128)(2,1)S(1)}, u32[]{:S(2)}, u32[]{:S(2)}) collective-permute-start(bf16[64,896]{1,0:T(8,128)(2,1)S(1)} %hidden.1.refs_0_), channel_id=1, source_target_pairs={{0,96},{32,128},{64,160},{96,192},{128,224},{160,0},{192,32},{224,... | collective-permute-start | bytes 344072 | tf_op jit(solution)/shard_map/ppermute | solution.py:15
  94.9 6.1 %collective-permute-start.18 = (bf16[64,896]{1,0:T(8,128)(2,1)S(1)}, bf16[64,896]{1,0:T(8,128)(2,1)S(1)}, u32[]{:S(2)}, u32[]{:S(2)}) collective-permute-start(bf16[64,896]{1,0:T(8,128)(2,1)S(1)} %hidden.1.refs_0_), channel_id=1, source_target_pairs={{0,64},{32,96},{64,128},{96,160},{128,192},{160,224},{192,0},{224,... | collective-permute-start | bytes 344072 | tf_op jit(solution)/shard_map/ppermute | solution.py:15
  95.0 11.5 %collective-permute-start.17 = (bf16[64,896]{1,0:T(8,128)(2,1)S(1)}, bf16[64,896]{1,0:T(8,128)(2,1)S(1)}, u32[]{:S(2)}, u32[]{:S(2)}) collective-permute-start(bf16[64,896]{1,0:T(8,128)(2,1)S(1)} %hidden.1.refs_0_), channel_id=1, source_target_pairs={{0,32},{32,64},{64,96},{96,128},{128,160},{160,192},{192,224},{224... | collective-permute-start | bytes 344072 | tf_op jit(solution)/shard_map/ppermute | solution.py:15
  113.8 4.0 %collective-permute-start.24 = (bf16[256,2048]{1,0:T(8,128)(2,1)S(1)}, bf16[256,2048]{1,0:T(8,128)(2,1)S(1)}, u32[]{:S(2)}, u32[]{:S(2)}) collective-permute-start(bf16[256,2048]{1,0:T(8,128)(2,1)S(1)} %get-tuple-element.24), channel_id=1, source_target_pairs={{0,1},{1,0},{2,3},{3,2},{4,5},{5,4},{6,7},{7,6},{8,9},{9,8},{10,11... | collective-permute-start | bytes 3145736 | tf_op jit(solution)/shard_map/ppermute | solution.py:15
  117.9 13.2 %collective-permute-start.25 = (bf16[128,2048]{1,0:T(8,128)(2,1)S(1)}, bf16[128,2048]{1,0:T(8,128)(2,1)S(1)}, u32[]{:S(2)}, u32[]{:S(2)}) collective-permute-start(bf16[128,2048]{1,0:T(8,128)(2,1)S(1)} %add_convert_fusion.1), channel_id=1, source_target_pairs={{0,2},{2,0},{1,3},{3,1},{4,6},{6,4},{5,7},{7,5},{8,10},{10,8},{9,1... | collective-permute-start | bytes 1572872 | tf_op jit(solution)/shard_map/ppermute | solution.py:15
  131.4 8.3 %collective-permute-start.26 = (bf16[16,2048]{1,0:T(8,128)(2,1)S(1)}, bf16[16,2048]{1,0:T(8,128)(2,1)S(1)}, u32[]{:S(2)}, u32[]{:S(2)}) collective-permute-start(bf16[16,2048]{1,0:T(8,128)(2,1)S(1)} %get-tuple-element.25), channel_id=1, source_target_pairs={{0,28},{4,0},{8,4},{12,8},{16,12},{20,16},{24,20},{28,24},{1,29},{... | collective-permute-start | bytes 196616 | tf_op jit(solution)/shard_map/ppermute | solution.py:15
  132.9 8.3 %collective-permute-start.32 = (bf16[16,2048]{1,0:T(8,128)(2,1)S(1)}, bf16[16,2048]{1,0:T(8,128)(2,1)S(1)}, u32[]{:S(2)}, u32[]{:S(2)}) collective-permute-start(bf16[16,2048]{1,0:T(8,128)(2,1)S(1)} %get-tuple-element.26), channel_id=1, source_target_pairs={{0,4},{4,8},{8,12},{12,16},{16,20},{20,24},{24,28},{28,0},{1,5},{5... | collective-permute-start | bytes 196616 | tf_op jit(solution)/shard_map/ppermute | solution.py:15
  132.9 11.8 %collective-permute-start.31 = (bf16[16,2048]{1,0:T(8,128)(2,1)S(1)}, bf16[16,2048]{1,0:T(8,128)(2,1)S(1)}, u32[]{:S(2)}, u32[]{:S(2)}) collective-permute-start(bf16[16,2048]{1,0:T(8,128)(2,1)S(1)} %get-tuple-element.27), channel_id=1, source_target_pairs={{0,8},{4,12},{8,16},{12,20},{16,24},{20,28},{24,0},{28,4},{1,9},{5... | collective-permute-start | bytes 196616 | tf_op jit(solution)/shard_map/ppermute | solution.py:15
  135.2 9.5 %collective-permute-start.30 = (bf16[16,2048]{1,0:T(8,128)(2,1)S(1)}, bf16[16,2048]{1,0:T(8,128)(2,1)S(1)}, u32[]{:S(2)}, u32[]{:S(2)}) collective-permute-start(bf16[16,2048]{1,0:T(8,128)(2,1)S(1)} %get-tuple-element.28), channel_id=1, source_target_pairs={{0,12},{4,16},{8,20},{12,24},{16,28},{20,0},{24,4},{28,8},{1,13},{... | collective-permute-start | bytes 196616 | tf_op jit(solution)/shard_map/ppermute | solution.py:15
  136.7 9.7 %collective-permute-start.29 = (bf16[16,2048]{1,0:T(8,128)(2,1)S(1)}, bf16[16,2048]{1,0:T(8,128)(2,1)S(1)}, u32[]{:S(2)}, u32[]{:S(2)}) collective-permute-start(bf16[16,2048]{1,0:T(8,128)(2,1)S(1)} %get-tuple-element.29), channel_id=1, source_target_pairs={{0,16},{4,20},{8,24},{12,28},{16,0},{20,4},{24,8},{28,12},{1,17},{... | collective-permute-start | bytes 196616 | tf_op jit(solution)/shard_map/ppermute | solution.py:15
  139.6 6.8 %collective-permute-start.28 = (bf16[16,2048]{1,0:T(8,128)(2,1)S(1)}, bf16[16,2048]{1,0:T(8,128)(2,1)S(1)}, u32[]{:S(2)}, u32[]{:S(2)}) collective-permute-start(bf16[16,2048]{1,0:T(8,128)(2,1)S(1)} %get-tuple-element.30), channel_id=1, source_target_pairs={{0,20},{4,24},{8,28},{12,0},{16,4},{20,8},{24,12},{28,16},{1,21},{... | collective-permute-start | bytes 196616 | tf_op jit(solution)/shard_map/ppermute | solution.py:15
  141.2 10.7 %collective-permute-start.27 = (bf16[16,2048]{1,0:T(8,128)(2,1)S(1)}, bf16[16,2048]{1,0:T(8,128)(2,1)S(1)}, u32[]{:S(2)}, u32[]{:S(2)}) collective-permute-start(bf16[16,2048]{1,0:T(8,128)(2,1)S(1)} %get-tuple-element.31), channel_id=1, source_target_pairs={{0,24},{4,28},{8,0},{12,4},{16,8},{20,12},{24,16},{28,20},{1,25},{... | collective-permute-start | bytes 196616 | tf_op jit(solution)/shard_map/ppermute | solution.py:15
  (2 other events, 63.6 us)

commit v2 on v0

v2 whole, which is shorter than its diff:
```python
import jax
import jax.numpy as jnp
from jax import lax
from jax.experimental import pallas as pl
from jax.experimental.pallas import tpu as pltpu
from jax.sharding import Mesh, PartitionSpec as P

BLOCK = 128
WIDE = 256
COL = ("z", "yl", "core")
ROW = ("x", "yh")
LIMIT = 24 * 1024 * 1024
F32 = jnp.float32
BF16 = jnp.bfloat16


def swap(value, axis):
    return lax.ppermute(value, axis, [(0, 1), (1, 0)])


def shift_x(value, by):
    return lax.ppermute(value, "x", [(i, (i + by) % 4) for i in range(4)])


def shift_z(value, by):
    pairs = []
    for z in range(8):
        pairs.append((2 * z, 2 * ((z + by) % 8)))
        pairs.append((2 * z + 1, 2 * ((z - by) % 8) + 1))
    return lax.ppermute(value, ("z", "core"), pairs)


def call(name, body, outs, ins, scalars=(), later=(), scratch=(), limit=LIMIT // 2):
    counts = [len(scalars), len(ins), len(later), len(outs)]

    def kernel(*refs):
        groups, at = [], 0
        for count in counts:
            groups.append(refs[at : at + count])
            at += count
        numbers, inputs, _, results = groups
        body(numbers, inputs, results, refs[at:])

    vmem = pl.BlockSpec(memory_space=pltpu.VMEM)
    return pl.pallas_call(
        kernel,
        in_specs=[pl.BlockSpec(memory_space=pltpu.SMEM)] * counts[0]
        + [vmem] * counts[1]
        + [pl.BlockSpec(memory_space=pl.ANY)] * counts[2],
        out_specs=[vmem] * counts[3],
        out_shape=[jax.ShapeDtypeStruct(shape, dtype) for shape, dtype in outs],
        scratch_shapes=list(scratch),
        compiler_params=pltpu.CompilerParams(vmem_limit_bytes=limit),
        cost_estimate=pl.CostEstimate(flops=1024, bytes_accessed=1024, transcendentals=0),
        name=name,
    )(*scalars, *ins, *later)


def columns(j, width):
    return pl.ds(pl.multiple_of(j * width, width), width)


def down_weight(quant, scale):
    depth, width = quant.shape

    def body(scales, quants, outs, _):
        def step(i, carry):
            rows = pl.ds(pl.multiple_of(i * BLOCK, BLOCK), BLOCK)
            for j in range(width // BLOCK):
                at = slice(j * BLOCK, (j + 1) * BLOCK)
                block = quants[0][rows, at].astype(F32)
                outs[0][rows, at] = (block * scales[0][j, i]).astype(BF16)
            return carry

        lax.fori_loop(0, depth // BLOCK, step, 0)

    outs = [((depth, width), BF16)]
    return call("down_weight", body, outs, [quant], scalars=[scale.T], limit=LIMIT)[0]


def joined(parts, later=()):
    def body(_, ins, outs, __):
        at = 0
        for part in ins:
            outs[0][at : at + part.shape[0], :] = part[...]
            at += part.shape[0]

    shape = (sum(part.shape[0] for part in parts), parts[0].shape[1])
    return call("joined", body, [(shape, BF16)], parts, later=later)[0]


def gate_up(me, pieces, gate, gate_scale, up, up_scale, later=()):
    depth, width = gate.shape
    count = 2 * width // WIDE

    def body(numbers, ins, outs, scratch):
        features, held = scratch
        quants, scales = ins[2:], numbers[1:]

        def fill(j):
            for side in range(2):
                for i in range(depth // BLOCK):
                    rows = slice(i * BLOCK, (i + 1) * BLOCK)
                    block = quants[side][rows, j * BLOCK : (j + 1) * BLOCK].astype(F32)
                    block = (block * scales[side][j, i]).astype(BF16)
                    held[j % 2, rows, side * BLOCK : (side + 1) * BLOCK] = block

        for chunk in range(4):
            at = pl.multiple_of(lax.rem(chunk + 4 - numbers[0][0], 4) * 64, 64)
            rows = slice(64 * (chunk % 2), 64 * (chunk % 2 + 1))
            features[pl.ds(at, 64), :] = ins[chunk // 2][rows, :]
        fill(0)
        for j in range(count):
            if j + 1 < count:
                fill(j + 1)
            total = jnp.dot(features[...], held[j % 2], preferred_element_type=F32)
            for k, out in enumerate(outs):
                out[:, j * WIDE : (j + 1) * WIDE] = total[64 * k : 64 * (k + 1)].astype(BF16)

    return call(
        "gate_up",
        body,
        [((64, 2 * width), BF16)] * 4,
        [*pieces, gate, up],
        scalars=[me, gate_scale.T, up_scale.T],
        later=later,
        scratch=[pltpu.VMEM((256, depth), BF16), pltpu.VMEM((2, depth, WIDE), BF16)],
        limit=LIMIT,
    )


def sum_x(outs, arrived, later=()):
    def body(_, ins, results, __):
        total = ins[0][...].astype(F32)
        for part in ins[1:]:
            total = total + part[...].astype(F32)
        results[0][...] = total
        results[1][...] = total.astype(BF16)

    shape = outs[0].shape
    return call("sum_x", body, [(shape, F32), (shape, BF16)], [outs[0], *arrived], later=later)


def silu(own, other, out):
    for j in range(out.shape[1] // BLOCK):
        at = slice(j * WIDE, (j + 1) * WIDE)
        total = own[:, at] + other[:, at].astype(F32)
        gate, up = total[:, :BLOCK], total[:, BLOCK:]
        hidden = gate / (1.0 + jnp.exp(-gate)) * up
        out[:, j * BLOCK : (j + 1) * BLOCK] = hidden.astype(BF16)


def hidden_and_sum(own, other, outs, arrived):
    rows, width = own.shape

    def body(_, ins, results, __):
        silu(ins[-2], ins[-1], results[0])
        total = ins[0][...].astype(F32)
        for part in ins[1:-2]:
            total = total + part[...].astype(F32)
        results[1][...] = total
        results[2][...] = total.astype(BF16)

    results = [((rows, width // 2), BF16), ((rows, width), F32), ((rows, width), BF16)]
    return call("hidden_and_sum", body, results, [outs[0], *arrived, own, other])


def hidden_of(own, other, later=()):
    rows, width = own.shape

    def body(_, ins, outs, __):
        silu(ins[0], ins[1], outs[0])

    return call("hidden", body, [((rows, width // 2), BF16)], [own, other], later=later)[0]


def down(me, pieces, weight, later=()):
    depth, width = weight.shape

    def body(numbers, ins, outs, scratch):
        hidden = scratch[0]
        for k in range(4):
            at = pl.multiple_of(lax.rem(numbers[0][0] + 4 - k, 4) * 64, 64)
            hidden[pl.ds(at, 64), :] = ins[k][...]

        def step(j, carry):
            at = columns(j, WIDE)
            total = jnp.dot(hidden[...], ins[4][:, at], preferred_element_type=F32)
            outs[0][:, at] = total[:128]
            outs[1][:, at] = total[128:].astype(BF16)
            return carry

        lax.fori_loop(0, width // WIDE, step, 0)

    return call(
        "down",
        body,
        [((128, width), F32), ((128, width), BF16)],
        [*pieces, weight],
        scalars=[me],
        later=later,
        scratch=[pltpu.VMEM((256, depth), BF16)],
    )


def sum_far(near, got):
    def body(_, ins, outs, __):
        total = (ins[0][...] + ins[1][...].astype(F32)).astype(BF16)
        outs[0][...] = total[:80]
        outs[1][...] = total[80:]

    width = near.shape[1]
    return call("sum_far", body, [((80, width), BF16), ((48, width), BF16)], [near, got])


def sum_near(near, got, other, low, parts):
    def body(_, ins, outs, __):
        at = 0
        for out in outs:
            rows = slice(low + at, low + at + out.shape[0])
            total = ins[0][rows] + ins[1][rows].astype(F32)
            total = total + ins[2][at : at + out.shape[0]].astype(F32)
            out[...] = total.astype(out.dtype)
            at += out.shape[0]

    outs = [((rows, near.shape[1]), kind) for rows, kind in parts]
    return call("sum_near", body, outs, [near, got, other])


def relay(own, arrived):
    def body(_, ins, outs, __):
        outs[0][:16] = (ins[0][:16] + ins[1][32:].astype(F32)).astype(BF16)
        outs[0][16:] = ins[0][16:].astype(BF16)

    return call("relay", body, [(own.shape, BF16)], [own, arrived])[0]


def sum_z(own, third, second, first):
    def body(_, ins, outs, __):
        total = ins[1][:32].astype(F32) + ins[2][...].astype(F32) + ins[3][...].astype(F32)
        outs[0][...] = ins[0][...] + total[:16]
        outs[1][...] = total[16:]

    return call("sum_z", body, [(own.shape, F32)] * 2, [own, third, second, first])


def spread_x(value):
    x1, x3, x2 = (shift_x(value, k) for k in (1, 3, 2))
    return [value, x1, x2, x3]


def local(tokens, gate_quant, gate_scale, up_quant, up_scale, down_quant, down_scale):
    me = lax.axis_index("x").astype(jnp.int32).reshape(1)
    both = (gate_quant, gate_scale, up_quant, up_scale)
    last_weight = down_weight(down_quant, down_scale)

    chip = joined([tokens, swap(tokens, "core")])
    z4 = shift_z(tokens, 4)
    z3, z2, z1 = (shift_z(chip, j) for j in (3, 2, 1))
    a = joined([tokens, z1, z2, z3, z4])
    b, c = swap(a, "core"), swap(a, "yl")

    outs_a = gate_up(me, [a, b], *both)
    parts_a = [shift_x(outs_a[k], k) for k in (2, 1, 3)]
    c = joined([c], later=[outs_a[0]])
    outs_c = gate_up(me, [c, swap(c, "core")], *both)
    total_a, sent_a = sum_x(outs_a, parts_a, later=[outs_c[0]])
    other_a = swap(sent_a, "yh")
    parts_c = [shift_x(outs_c[k], k) for k in (2, 1, 3)]
    hidden_a, total_c, sent_c = hidden_and_sum(total_a, other_a, outs_c, parts_c)
    gathered_a = spread_x(hidden_a)
    hidden_c = hidden_of(total_c, swap(sent_c, "yh"))
    gathered_c = spread_x(hidden_c)
    near_a, far_a = down(me, gathered_a, last_weight)
    near_c, far_c = down(me, gathered_c, last_weight, later=[far_a])

    sent2, sent1 = sum_far(near_c, swap(far_c, "core"))
    got = swap(far_a, "core")
    other1, other2 = swap(sent1, "yl"), swap(sent2, "yl")
    third = shift_z(sum_near(near_a, got, other1, 80, [(48, BF16)])[0], -3)
    parts = [(16, F32), (32, F32), (32, BF16)]
    own, first, second = sum_near(near_a, got, other2, 0, parts)
    second = shift_z(second, -2)
    first = shift_z(relay(first, third), -1)
    keep, send = sum_z(own, third, second, first)
    return (keep + swap(send, "core")).astype(BF16)


def solution(mesh):
    fine = Mesh(mesh.devices.reshape(4, 2, 8, 2, 2), ROW + COL)
    placed = (
        P(COL, ROW),
        P(ROW, COL),
        P(ROW, COL),
        P(ROW, COL),
        P(ROW, COL),
        P(COL, ROW),
        P(COL, ROW),
    )
    return jax.shard_map(
        local, mesh=fine, in_specs=placed, out_specs=P(COL, ROW), check_vma=False
    )
```

time: 357 us -> 115 us (0.32); the launches traced: 353 us -> 115 us
  waiting for transfers between devices: 270 us -> 40.1 us
  starting transfers between devices: 0.08 us -> 49.7 us
  blocking collectives: 30.8 us -> 0 us
  local copies, waits for them, and re-layouts: 24.2 us -> 8.43 us
  Pallas kernels: 0 us -> 15.6 us
  between operations: 13.2 us -> 0.19 us
  matrix products: 9.92 us -> 0 us
  other arithmetic: 4.85 us -> 0.65 us
    reduce_scatter x2 -> x0, waiting for transfers between devices: 211 us -> none  [the longest x1 125 us: local(): lax.psum_scatter(jnp.dot(picked, down_weight, preferred_element_type=jnp....]
    all_gather x1 -> x0, waiting for transfers between devices: 58.5 us -> none  [local(): features = lax.all_gather(tokens, 'col', axis=0, tiled=True)]
    ppermute x0 -> x30, starting transfers between devices: none -> 49.7 us  [the longest x11 22.4 us: swap(): return lax.ppermute(value, axis, [(0, 1), (1, 0)])]
    ppermute x0 -> x30, waiting for transfers between devices: none -> 40.1 us  [the longest x11 19.4 us: swap(): return lax.ppermute(value, axis, [(0, 1), (1, 0)])]
    all_gather x1 -> x0, blocking collectives: 30.8 us -> none  [local(): hidden = lax.all_gather(local_hidden, 'row', axis=0, tiled=True)]
    pallas_call x0 -> x16, Pallas kernels: none -> 15.6 us  [call(): pl.pallas_call(kernel, in_specs=[pl.BlockSpec(memory_space=pltpu.SMEM)] *...]
    unnamed x17 -> x23, local copies, waits for them, and re-layouts: 22.6 us -> 8.43 us
    dot_general x3 -> x0, matrix products: 9.92 us -> none  [the longest x1 4.82 us: local(): jnp.dot(picked, down_weight, preferred_element_type=jnp.float32)]
  transfers between devices with their start and end apart: 3 -> 30, of which waited for: 3 -> 16; matrix products, arithmetic and copies ran while one was open for 3% -> 0% of each run, Pallas kernels for 0% -> 11%
where the time goes in v2:
time: 115 us
  starting transfers between devices  49.7 us (43%)
  waiting for transfers between devices  40.1 us (35%)
  Pallas kernels  15.6 us (14%)
  local copies, waits for them, and re-layouts  8.43 us (7%)
    ppermute x11, starting transfers between devices, swap(): return lax.ppermute(value, axis, [(0, 1), (1, 0)])  22.4 us
    ppermute x11, waiting for transfers between devices, swap(): return lax.ppermute(value, axis, [(0, 1), (1, 0)])  19.4 us
    pallas_call x16, Pallas kernels, call(): pl.pallas_call(kernel, in_specs=[pl.BlockSpec(memory_space=pltpu.SMEM)] *...  15.6 us
    ppermute x12, starting transfers between devices, shift_x(): return lax.ppermute(value, 'x', [(i, (i + by) % 4) for i in range(4)])  14.8 us
    ppermute x7, starting transfers between devices, shift_z(): return lax.ppermute(value, ('z', 'core'), pairs)  12.5 us
    ppermute x7, waiting for transfers between devices, shift_z(): return lax.ppermute(value, ('z', 'core'), pairs)  12.5 us
    unnamed x23, local copies, waits for them, and re-layouts  8.43 us
    ppermute x12, waiting for transfers between devices, shift_x(): return lax.ppermute(value, 'x', [(i, (i + by) % 4) for i in range(4)])  8.27 us
  transfers between devices with their start and end apart: 30, of which 16 were waited for; matrix products, arithmetic and copies ran while one was open for 0% of the time, Pallas kernels for 11%

profile of v2, /device:TPU:1, one launch (start us, length us, event | category | flops | bytes accessed | tf_op | source)
XLA Modules:
  0.0 114.7 jit_solution(16755952218512585639)
XLA Ops:
  0.0 3.2 %collective-permute-start = (bf16[16,2048]{1,0:T(8,128)(2,1)}, bf16[16,2048]{1,0:T(8,128)(2,1)S(1)}, u32[]{:S(2)}, u32[]{:S(2)}) collective-permute-start(bf16[16,2048]{1,0:T(8,128)(2,1)} %refs_0_.3), channel_id=1, source_target_pairs={{0,1},{1,0},{2,3},{3,2},{4,5},{5,4},{6,7},{7,6},{8,9},{9,8},{10,11... | collective-permute-start | bytes 196616 | tf_op jit(solution)/shard_map/ppermute | solution.py:18
  5.2 4.8 %collective-permute-start.3 = (bf16[32,2048]{1,0:T(8,128)(2,1)S(1)}, bf16[32,2048]{1,0:T(8,128)(2,1)S(1)}, u32[]{:S(2)}, u32[]{:S(2)}) collective-permute-start(bf16[32,2048]{1,0:T(8,128)(2,1)S(1)} %joined.3), channel_id=1, source_target_pairs={{0,12},{1,21},{4,16},{5,25},{8,20},{9,29},{12,24},{13,1},{16,28},{... | collective-permute-start | bytes 393224 | tf_op jit(solution)/shard_map/ppermute | solution.py:30
  10.7 4.5 %collective-permute-start.4 = (bf16[16,2048]{1,0:T(8,128)(2,1)S(1)}, bf16[16,2048]{1,0:T(8,128)(2,1)S(1)}, u32[]{:S(2)}, u32[]{:S(2)}) collective-permute-start(bf16[16,2048]{1,0:T(8,128)(2,1)S(1)} %copy-done.5), channel_id=1, source_target_pairs={{0,16},{1,17},{4,20},{5,21},{8,24},{9,25},{12,28},{13,29},{16,0},{... | collective-permute-start | bytes 196616 | tf_op jit(solution)/shard_map/ppermute | solution.py:30
  15.2 5.2 %collective-permute-done.4.refs_4_ = bf16[16,2048]{1,0:T(8,128)(2,1)S(1)} collective-permute-done((bf16[16,2048]{1,0:T(8,128)(2,1)S(1)}, bf16[16,2048]{1,0:T(8,128)(2,1)S(1)}, u32[]{:S(2)}, u32[]{:S(2)}) %collective-permute-start.4) | collective-permute-done | bytes 65568 | tf_op jit(solution)/shard_map/ppermute | solution.py:30
  21.8 3.5 %collective-permute-start.6 = (bf16[128,2048]{1,0:T(8,128)(2,1)S(1)}, bf16[128,2048]{1,0:T(8,128)(2,1)S(1)}, u32[]{:S(2)}, u32[]{:S(2)}) collective-permute-start(bf16[128,2048]{1,0:T(8,128)(2,1)S(1)} %joined.4.refs_3_), channel_id=1, source_target_pairs={{0,1},{1,0},{2,3},{3,2},{4,5},{5,4},{6,7},{7,6},{8,9},{9,8},{10,11... | collective-permute-start | bytes 1572872 | tf_op jit(solution)/shard_map/ppermute | solution.py:18
  26.8 2.0 %copy-done = bf16[2048,896]{1,0:T(8,128)(2,1)S(1)} copy-done((bf16[2048,896]{1,0:T(8,128)(2,1)S(1)}, bf16[2048,896]{1,0:T(8,128)(2,1)}, u32[]{:S(2)}) %copy-start) | copy-done | bytes 3670040
  28.9 2.0 %copy-done.2 = bf16[2048,896]{1,0:T(8,128)(2,1)S(1)} copy-done((bf16[2048,896]{1,0:T(8,128)(2,1)S(1)}, bf16[2048,896]{1,0:T(8,128)(2,1)}, u32[]{:S(2)}) %copy-start.2) | copy-done | bytes 3670040
  32.3 4.0 %gate_up.2 = (bf16[64,1792]{1,0:T(8,128)(2,1)S(1)}, bf16[64,1792]{1,0:T(8,128)(2,1)S(1)}, bf16[64,1792]{1,0:T(8,128)(2,1)S(1)}, bf16[64,1792]{1,0:T(8,128)(2,1)S(1)}) custom-call(s32[1]{0:T(128)} %bitcast.refs_0_, f32[7,16]{1,0:T(8,128)S(1)} %bitcast.5, f32[7,16]{1,0:T(8,128)S(1)} %bitcast.7, bf16[128,2048]{1,0:T(8,128)(2,1)S(1)} %joined.4.refs_3_, ...), custom_call_target="tpu_custom_call" | custom-call | flops 1024 | bytes 1024 | tf_op jit(solution)/shard_map/gate_up/pallas_call | solution.py:45
  36.3 2.5 %collective-permute-done.5.refs_0_ = bf16[128,2048]{1,0:T(8,128)(2,1)S(1)} collective-permute-done((bf16[128,2048]{1,0:T(8,128)(2,1)S(1)}, bf16[128,2048]{1,0:T(8,128)(2,1)S(1)}, u32[]{:S(2)}, u32[]{:S(2)}) %collective-permute-start.5) | collective-permute-done | bytes 524320 | tf_op jit(solution)/shard_map/ppermute | solution.py:18
  39.8 2.8 %collective-permute-start.11 = (bf16[64,1792]{1,0:T(8,128)(2,1)S(1)}, bf16[64,1792]{1,0:T(8,128)(2,1)S(1)}, u32[]{:S(2)}, u32[]{:S(2)}) collective-permute-start(bf16[64,1792]{1,0:T(8,128)(2,1)S(1)} %get-tuple-element.34), channel_id=1, source_target_pairs={{0,128},{64,192},{128,0},{192,64},{1,129},{65,193},{129,1},{193,65... | collective-permute-start | bytes 688136 | tf_op jit(solution)/shard_map/ppermute | solution.py:22
  42.8 2.4 %collective-permute-start.13 = (bf16[64,1792]{1,0:T(8,128)(2,1)S(1)}, bf16[64,1792]{1,0:T(8,128)(2,1)S(1)}, u32[]{:S(2)}, u32[]{:S(2)}) collective-permute-start(bf16[64,1792]{1,0:T(8,128)(2,1)S(1)} %get-tuple-element.36), channel_id=1, source_target_pairs={{0,192},{64,0},{128,64},{192,128},{1,193},{65,1},{129,65},{193,129... | collective-permute-start | bytes 688136 | tf_op jit(solution)/shard_map/ppermute | solution.py:22
  45.2 4.0 %gate_up.3 = (bf16[64,1792]{1,0:T(8,128)(2,1)S(1)}, bf16[64,1792]{1,0:T(8,128)(2,1)S(1)}, bf16[64,1792]{1,0:T(8,128)(2,1)S(1)}, bf16[64,1792]{1,0:T(8,128)(2,1)S(1)}) custom-call(s32[1]{0:T(128)} %bitcast.refs_0_, f32[7,16]{1,0:T(8,128)S(1)} %bitcast.6, f32[7,16]{1,0:T(8,128)S(1)} %bitcast.8, bf16[128,2048]{1,0:T(8,128)(2,1)S(1)} %joined.5.refs_3_, ...), custom_call_target="tpu_custom_call" | custom-call | flops 1024 | bytes 1024 | tf_op jit(solution)/shard_map/gate_up/pallas_call | solution.py:45
  49.9 2.2 %collective-permute-start.10 = (bf16[64,1792]{1,0:T(8,128)(2,1)S(1)}, bf16[64,1792]{1,0:T(8,128)(2,1)S(1)}, u32[]{:S(2)}, u32[]{:S(2)}) collective-permute-start(bf16[64,1792]{1,0:T(8,128)(2,1)S(1)} %get-tuple-element.33), channel_id=1, source_target_pairs={{0,192},{64,0},{128,64},{192,128},{1,193},{65,1},{129,65},{193,129... | collective-permute-start | bytes 688136 | tf_op jit(solution)/shard_map/ppermute | solution.py:22
  52.1 1.8 %collective-permute-done.12.refs_2_ = bf16[64,1792]{1,0:T(8,128)(2,1)S(1)} collective-permute-done((bf16[64,1792]{1,0:T(8,128)(2,1)S(1)}, bf16[64,1792]{1,0:T(8,128)(2,1)S(1)}, u32[]{:S(2)}, u32[]{:S(2)}) %collective-permute-start.12) | collective-permute-done | bytes 229408 | tf_op jit(solution)/shard_map/ppermute | solution.py:22
  54.0 3.0 %collective-permute-start.14 = (bf16[64,1792]{1,0:T(8,128)(2,1)S(1)}, bf16[64,1792]{1,0:T(8,128)(2,1)S(1)}, u32[]{:S(2)}, u32[]{:S(2)}) collective-permute-start(bf16[64,1792]{1,0:T(8,128)(2,1)S(1)} %get-tuple-element.38), channel_id=1, source_target_pairs={{0,32},{32,0},{1,33},{33,1},{2,34},{34,2},{3,35},{35,3},{4,36},{36... | collective-permute-start | bytes 688136 | tf_op jit(solution)/shard_map/ppermute | solution.py:18
  57.8 5.7 %collective-permute-done.9.refs_2_ = bf16[64,1792]{1,0:T(8,128)(2,1)S(1)} collective-permute-done((bf16[64,1792]{1,0:T(8,128)(2,1)S(1)}, bf16[64,1792]{1,0:T(8,128)(2,1)S(1)}, u32[]{:S(2)}, u32[]{:S(2)}) %collective-permute-start.9) | collective-permute-done | bytes 229408 | tf_op jit(solution)/shard_map/ppermute | solution.py:22
  63.7 3.0 %collective-permute-start.19 = (bf16[64,1792]{1,0:T(8,128)(2,1)S(1)}, bf16[64,1792]{1,0:T(8,128)(2,1)S(1)}, u32[]{:S(2)}, u32[]{:S(2)}) collective-permute-start(bf16[64,1792]{1,0:T(8,128)(2,1)S(1)} %get-tuple-element.43), channel_id=1, source_target_pairs={{0,32},{32,0},{1,33},{33,1},{2,34},{34,2},{3,35},{35,3},{4,36},{36... | collective-permute-start | bytes 688136 | tf_op jit(solution)/shard_map/ppermute | solution.py:18
  66.7 2.5 %collective-permute-start.17 = (bf16[64,896]{1,0:T(8,128)(2,1)S(1)}, bf16[64,896]{1,0:T(8,128)(2,1)S(1)}, u32[]{:S(2)}, u32[]{:S(2)}) collective-permute-start(bf16[64,896]{1,0:T(8,128)(2,1)S(1)} %get-tuple-element.39.refs_1_), channel_id=1, source_target_pairs={{0,192},{64,0},{128,64},{192,128},{1,193},{65,1},{129,65},{193,129... | collective-permute-start | bytes 344072 | tf_op jit(solution)/shard_map/ppermute | solution.py:22
  69.7 1.9 %collective-permute-done.19.refs_1_ = bf16[64,1792]{1,0:T(8,128)(2,1)S(1)} collective-permute-done((bf16[64,1792]{1,0:T(8,128)(2,1)S(1)}, bf16[64,1792]{1,0:T(8,128)(2,1)S(1)}, u32[]{:S(2)}, u32[]{:S(2)}) %collective-permute-start.19) | collective-permute-done | bytes 229408 | tf_op jit(solution)/shard_map/ppermute | solution.py:18
  71.7 2.8 %collective-permute-start.22 = (bf16[64,896]{1,0:T(8,128)(2,1)S(1)}, bf16[64,896]{1,0:T(8,128)(2,1)S(1)}, u32[]{:S(2)}, u32[]{:S(2)}) collective-permute-start(bf16[64,896]{1,0:T(8,128)(2,1)S(1)} %hidden.1.refs_1_), channel_id=1, source_target_pairs={{0,192},{64,0},{128,64},{192,128},{1,193},{65,1},{129,65},{193,129... | collective-permute-start | bytes 344072 | tf_op jit(solution)/shard_map/ppermute | solution.py:22
  75.3 2.0 %copy-done.4 = bf16[896,2048]{1,0:T(8,128)(2,1)S(1)} copy-done((bf16[896,2048]{1,0:T(8,128)(2,1)S(1)}, bf16[896,2048]{1,0:T(8,128)(2,1)}, u32[]{:S(2)}) %copy-start.4) | copy-done | bytes 3670040
  77.3 1.6 %down_weight.1.refs_5_ = bf16[896,2048]{1,0:T(8,128)(2,1)S(1)} custom-call(f32[16,7]{1,0:T(8,128)S(1)} %bitcast.4, bf16[896,2048]{1,0:T(8,128)(2,1)S(1)} %copy-done.4), custom_call_target="tpu_custom_call" | custom-call | flops 1024 | bytes 1024 | tf_op jit(solution)/shard_map/down_weight/pallas_call | solution.py:45
  79.0 2.5 %down.2 = (f32[128,2048]{1,0:T(8,128)S(1)}, bf16[128,2048]{1,0:T(8,128)(2,1)S(1)}) custom-call(s32[1]{0:T(128)} %bitcast.refs_0_, bf16[64,896]{1,0:T(8,128)(2,1)S(1)} %get-tuple-element.39.refs_1_, bf16[64,896]{1,0:T(8,128)(2,1)S(1)} %collective-permute-done.15.refs_2_, bf16[64,896]{1,0:T(8,128)(2,1)S(1)} %collective-permute-done.16.refs_3_, ...), custom_call_target="tpu_custom_call" | custom-call | flops 1024 | bytes 1024 | tf_op jit(solution)/shard_map/down/pallas_call | solution.py:45
  81.6 2.5 %down.3 = (f32[128,2048]{1,0:T(8,128)S(1)}, bf16[128,2048]{1,0:T(8,128)(2,1)S(1)}) custom-call(s32[1]{0:T(128)} %bitcast.refs_0_, bf16[64,896]{1,0:T(8,128)(2,1)S(1)} %hidden.1.refs_1_, bf16[64,896]{1,0:T(8,128)(2,1)S(1)} %collective-permute-done.20.refs_2_, bf16[64,896]{1,0:T(8,128)(2,1)S(1)} %collective-permute-done.21.refs_3_, ...), custom_call_target="tpu_custom_call" | custom-call | flops 1024 | bytes 1024 | tf_op jit(solution)/shard_map/down/pallas_call | solution.py:45
  84.1 2.5 %collective-permute-start.23 = (bf16[128,2048]{1,0:T(8,128)(2,1)S(1)}, bf16[128,2048]{1,0:T(8,128)(2,1)S(1)}, u32[]{:S(2)}, u32[]{:S(2)}) collective-permute-start(bf16[128,2048]{1,0:T(8,128)(2,1)S(1)} %get-tuple-element.45), channel_id=1, source_target_pairs={{0,1},{1,0},{2,3},{3,2},{4,5},{5,4},{6,7},{7,6},{8,9},{9,8},{10,11... | collective-permute-start | bytes 1572872 | tf_op jit(solution)/shard_map/ppermute | solution.py:18
  88.3 1.6 %collective-permute-start.25 = (bf16[48,2048]{1,0:T(8,128)(2,1)S(1)}, bf16[48,2048]{1,0:T(8,128)(2,1)S(1)}, u32[]{:S(2)}, u32[]{:S(2)}) collective-permute-start(bf16[48,2048]{1,0:T(8,128)(2,1)S(1)} %get-tuple-element.48), channel_id=1, source_target_pairs={{0,2},{2,0},{1,3},{3,1},{4,6},{6,4},{5,7},{7,5},{8,10},{10,8},{9,1... | collective-permute-start | bytes 589832 | tf_op jit(solution)/shard_map/ppermute | solution.py:18
  90.1 4.6 %collective-permute-done.25.refs_2_ = bf16[48,2048]{1,0:T(8,128)(2,1)S(1)} collective-permute-done((bf16[48,2048]{1,0:T(8,128)(2,1)S(1)}, bf16[48,2048]{1,0:T(8,128)(2,1)S(1)}, u32[]{:S(2)}, u32[]{:S(2)}) %collective-permute-start.25) | collective-permute-done | bytes 196640 | tf_op jit(solution)/shard_map/ppermute | solution.py:18
  95.1 6.6 %collective-permute-done.24.refs_2_ = bf16[80,2048]{1,0:T(8,128)(2,1)S(1)} collective-permute-done((bf16[80,2048]{1,0:T(8,128)(2,1)S(1)}, bf16[80,2048]{1,0:T(8,128)(2,1)S(1)}, u32[]{:S(2)}, u32[]{:S(2)}) %collective-permute-start.24) | collective-permute-done | bytes 327712 | tf_op jit(solution)/shard_map/ppermute | solution.py:18
  101.9 1.7 %collective-permute-done.26.refs_1_ = bf16[48,2048]{1,0:T(8,128)(2,1)S(1)} collective-permute-done((bf16[48,2048]{1,0:T(8,128)(2,1)S(1)}, bf16[48,2048]{1,0:T(8,128)(2,1)S(1)}, u32[]{:S(2)}, u32[]{:S(2)}) %collective-permute-start.26) | collective-permute-done | bytes 196640 | tf_op jit(solution)/shard_map/ppermute | solution.py:30
  103.7 2.1 %collective-permute-start.28 = (bf16[32,2048]{1,0:T(8,128)(2,1)S(1)}, bf16[32,2048]{1,0:T(8,128)(2,1)S(1)}, u32[]{:S(2)}, u32[]{:S(2)}) collective-permute-start(bf16[32,2048]{1,0:T(8,128)(2,1)S(1)} %relay.1), channel_id=1, source_target_pairs={{0,28},{1,5},{4,0},{5,9},{8,4},{9,13},{12,8},{13,17},{16,12},{17,2... | collective-permute-start | bytes 393224 | tf_op jit(solution)/shard_map/ppermute | solution.py:30
  105.8 2.9 %collective-permute-done.27.refs_2_ = bf16[32,2048]{1,0:T(8,128)(2,1)S(1)} collective-permute-done((bf16[32,2048]{1,0:T(8,128)(2,1)S(1)}, bf16[32,2048]{1,0:T(8,128)(2,1)S(1)}, u32[]{:S(2)}, u32[]{:S(2)}) %collective-permute-start.27) | collective-permute-done | bytes 131104 | tf_op jit(solution)/shard_map/ppermute | solution.py:30
  110.1 3.0 %collective-permute-start.29 = (f32[16,2048]{1,0:T(8,128)S(1)}, f32[16,2048]{1,0:T(8,128)S(1)}, u32[]{:S(2)}, u32[]{:S(2)}) collective-permute-start(f32[16,2048]{1,0:T(8,128)S(1)} %get-tuple-element.52), channel_id=1, source_target_pairs={{0,1},{1,0},{2,3},{3,2},{4,5},{5,4},{6,7},{7,6},{8,9},{9,8},{10,11... | collective-permute-start | bytes 393224 | tf_op jit(solution)/shard_map/ppermute | solution.py:18
  (68 shorter events, 16.8 us)
Async XLA Ops:
  0.0 4.4 %collective-permute-start = (bf16[16,2048]{1,0:T(8,128)(2,1)}, bf16[16,2048]{1,0:T(8,128)(2,1)S(1)}, u32[]{:S(2)}, u32[]{:S(2)}) collective-permute-start(bf16[16,2048]{1,0:T(8,128)(2,1)} %refs_0_.3), channel_id=1, source_target_pairs={{0,1},{1,0},{2,3},{3,2},{4,5},{5,4},{6,7},{7,6},{8,9},{9,8},{10,11... | collective-permute-start | bytes 196616 | tf_op jit(solution)/shard_map/ppermute | solution.py:18
  5.2 15.3 %collective-permute-start.3 = (bf16[32,2048]{1,0:T(8,128)(2,1)S(1)}, bf16[32,2048]{1,0:T(8,128)(2,1)S(1)}, u32[]{:S(2)}, u32[]{:S(2)}) collective-permute-start(bf16[32,2048]{1,0:T(8,128)(2,1)S(1)} %joined.3), channel_id=1, source_target_pairs={{0,12},{1,21},{4,16},{5,25},{8,20},{9,29},{12,24},{13,1},{16,28},{... | collective-permute-start | bytes 393224 | tf_op jit(solution)/shard_map/ppermute | solution.py:30
  10.0 10.5 %collective-permute-start.2 = (bf16[32,2048]{1,0:T(8,128)(2,1)S(1)}, bf16[32,2048]{1,0:T(8,128)(2,1)S(1)}, u32[]{:S(2)}, u32[]{:S(2)}) collective-permute-start(bf16[32,2048]{1,0:T(8,128)(2,1)S(1)} %joined.3), channel_id=1, source_target_pairs={{0,8},{1,25},{4,12},{5,29},{8,16},{9,1},{12,20},{13,5},{16,24},{17... | collective-permute-start | bytes 393224 | tf_op jit(solution)/shard_map/ppermute | solution.py:30
  10.3 11.5 %collective-permute-start.1 = (bf16[32,2048]{1,0:T(8,128)(2,1)S(1)}, bf16[32,2048]{1,0:T(8,128)(2,1)S(1)}, u32[]{:S(2)}, u32[]{:S(2)}) collective-permute-start(bf16[32,2048]{1,0:T(8,128)(2,1)S(1)} %joined.3), channel_id=1, source_target_pairs={{0,4},{1,29},{4,8},{5,1},{8,12},{9,5},{12,16},{13,9},{16,20},{17,1... | collective-permute-start | bytes 393224 | tf_op jit(solution)/shard_map/ppermute | solution.py:30
  10.7 9.7 %collective-permute-start.4 = (bf16[16,2048]{1,0:T(8,128)(2,1)S(1)}, bf16[16,2048]{1,0:T(8,128)(2,1)S(1)}, u32[]{:S(2)}, u32[]{:S(2)}) collective-permute-start(bf16[16,2048]{1,0:T(8,128)(2,1)S(1)} %copy-done.5), channel_id=1, source_target_pairs={{0,16},{1,17},{4,20},{5,21},{8,24},{9,25},{12,28},{13,29},{16,0},{... | collective-permute-start | bytes 196616 | tf_op jit(solution)/shard_map/ppermute | solution.py:30
  21.8 5.0 %collective-permute-start.6 = (bf16[128,2048]{1,0:T(8,128)(2,1)S(1)}, bf16[128,2048]{1,0:T(8,128)(2,1)S(1)}, u32[]{:S(2)}, u32[]{:S(2)}) collective-permute-start(bf16[128,2048]{1,0:T(8,128)(2,1)S(1)} %joined.4.refs_3_), channel_id=1, source_target_pairs={{0,1},{1,0},{2,3},{3,2},{4,5},{5,4},{6,7},{7,6},{8,9},{9,8},{10,11... | collective-permute-start | bytes 1572872 | tf_op jit(solution)/shard_map/ppermute | solution.py:18
  25.3 13.5 %collective-permute-start.5 = (bf16[128,2048]{1,0:T(8,128)(2,1)S(1)}, bf16[128,2048]{1,0:T(8,128)(2,1)S(1)}, u32[]{:S(2)}, u32[]{:S(2)}) collective-permute-start(bf16[128,2048]{1,0:T(8,128)(2,1)S(1)} %joined.4.refs_3_), channel_id=1, source_target_pairs={{0,2},{2,0},{1,3},{3,1},{4,6},{6,4},{5,7},{7,5},{8,10},{10,8},{9,1... | collective-permute-start | bytes 1572872 | tf_op jit(solution)/shard_map/ppermute | solution.py:18
  32.3 13.0 %copy-start.9 = (f32[16,7]{0,1:T(8,128)S(1)}, f32[16,7]{0,1:T(8,128)}, u32[]{:S(2)}) copy-start(f32[16,7]{0,1:T(8,128)} %param.11) | copy-start | bytes 1348
  38.8 6.4 %collective-permute-start.7 = (bf16[128,2048]{1,0:T(8,128)(2,1)S(1)}, bf16[128,2048]{1,0:T(8,128)(2,1)S(1)}, u32[]{:S(2)}, u32[]{:S(2)}) collective-permute-start(bf16[128,2048]{1,0:T(8,128)(2,1)S(1)} %joined.5.refs_3_), channel_id=1, source_target_pairs={{0,1},{1,0},{2,3},{3,2},{4,5},{5,4},{6,7},{7,6},{8,9},{9,8},{10,11... | collective-permute-start | bytes 1572872 | tf_op jit(solution)/shard_map/ppermute | solution.py:18
  39.8 10.1 %collective-permute-start.11 = (bf16[64,1792]{1,0:T(8,128)(2,1)S(1)}, bf16[64,1792]{1,0:T(8,128)(2,1)S(1)}, u32[]{:S(2)}, u32[]{:S(2)}) collective-permute-start(bf16[64,1792]{1,0:T(8,128)(2,1)S(1)} %get-tuple-element.34), channel_id=1, source_target_pairs={{0,128},{64,192},{128,0},{192,64},{1,129},{65,193},{129,1},{193,65... | collective-permute-start | bytes 688136 | tf_op jit(solution)/shard_map/ppermute | solution.py:22
  42.5 11.4 %collective-permute-start.12 = (bf16[64,1792]{1,0:T(8,128)(2,1)S(1)}, bf16[64,1792]{1,0:T(8,128)(2,1)S(1)}, u32[]{:S(2)}, u32[]{:S(2)}) collective-permute-start(bf16[64,1792]{1,0:T(8,128)(2,1)S(1)} %get-tuple-element.35), channel_id=1, source_target_pairs={{0,64},{64,128},{128,192},{192,0},{1,65},{65,129},{129,193},{193,1... | collective-permute-start | bytes 688136 | tf_op jit(solution)/shard_map/ppermute | solution.py:22
  42.8 32.3 %copy-start.10 = (f32[7,16]{1,0:T(8,128)S(1)}, f32[7,16]{1,0:T(8,128)}, u32[]{:S(2)}) copy-start(f32[7,16]{1,0:T(8,128)} %param.13) | copy-start | bytes 1348
  42.8 11.1 %collective-permute-start.13 = (bf16[64,1792]{1,0:T(8,128)(2,1)S(1)}, bf16[64,1792]{1,0:T(8,128)(2,1)S(1)}, u32[]{:S(2)}, u32[]{:S(2)}) collective-permute-start(bf16[64,1792]{1,0:T(8,128)(2,1)S(1)} %get-tuple-element.36), channel_id=1, source_target_pairs={{0,192},{64,0},{128,64},{192,128},{1,193},{65,1},{129,65},{193,129... | collective-permute-start | bytes 688136 | tf_op jit(solution)/shard_map/ppermute | solution.py:22
  49.2 8.5 %collective-permute-start.8 = (bf16[64,1792]{1,0:T(8,128)(2,1)S(1)}, bf16[64,1792]{1,0:T(8,128)(2,1)S(1)}, u32[]{:S(2)}, u32[]{:S(2)}) collective-permute-start(bf16[64,1792]{1,0:T(8,128)(2,1)S(1)} %get-tuple-element.31), channel_id=1, source_target_pairs={{0,128},{64,192},{128,0},{192,64},{1,129},{65,193},{129,1},{193,65... | collective-permute-start | bytes 688136 | tf_op jit(solution)/shard_map/ppermute | solution.py:22
  49.3 14.1 %collective-permute-start.9 = (bf16[64,1792]{1,0:T(8,128)(2,1)S(1)}, bf16[64,1792]{1,0:T(8,128)(2,1)S(1)}, u32[]{:S(2)}, u32[]{:S(2)}) collective-permute-start(bf16[64,1792]{1,0:T(8,128)(2,1)S(1)} %get-tuple-element.32), channel_id=1, source_target_pairs={{0,64},{64,128},{128,192},{192,0},{1,65},{65,129},{129,193},{193,1... | collective-permute-start | bytes 688136 | tf_op jit(solution)/shard_map/ppermute | solution.py:22
  49.9 13.5 %collective-permute-start.10 = (bf16[64,1792]{1,0:T(8,128)(2,1)S(1)}, bf16[64,1792]{1,0:T(8,128)(2,1)S(1)}, u32[]{:S(2)}, u32[]{:S(2)}) collective-permute-start(bf16[64,1792]{1,0:T(8,128)(2,1)S(1)} %get-tuple-element.33), channel_id=1, source_target_pairs={{0,192},{64,0},{128,64},{192,128},{1,193},{65,1},{129,65},{193,129... | collective-permute-start | bytes 688136 | tf_op jit(solution)/shard_map/ppermute | solution.py:22
  54.0 9.4 %collective-permute-start.14 = (bf16[64,1792]{1,0:T(8,128)(2,1)S(1)}, bf16[64,1792]{1,0:T(8,128)(2,1)S(1)}, u32[]{:S(2)}, u32[]{:S(2)}) collective-permute-start(bf16[64,1792]{1,0:T(8,128)(2,1)S(1)} %get-tuple-element.38), channel_id=1, source_target_pairs={{0,32},{32,0},{1,33},{33,1},{2,34},{34,2},{3,35},{35,3},{4,36},{36... | collective-permute-start | bytes 688136 | tf_op jit(solution)/shard_map/ppermute | solution.py:18
  63.7 8.0 %collective-permute-start.19 = (bf16[64,1792]{1,0:T(8,128)(2,1)S(1)}, bf16[64,1792]{1,0:T(8,128)(2,1)S(1)}, u32[]{:S(2)}, u32[]{:S(2)}) collective-permute-start(bf16[64,1792]{1,0:T(8,128)(2,1)S(1)} %get-tuple-element.43), channel_id=1, source_target_pairs={{0,32},{32,0},{1,33},{33,1},{2,34},{34,2},{3,35},{35,3},{4,36},{36... | collective-permute-start | bytes 688136 | tf_op jit(solution)/shard_map/ppermute | solution.py:18
  66.7 8.2 %collective-permute-start.17 = (bf16[64,896]{1,0:T(8,128)(2,1)S(1)}, bf16[64,896]{1,0:T(8,128)(2,1)S(1)}, u32[]{:S(2)}, u32[]{:S(2)}) collective-permute-start(bf16[64,896]{1,0:T(8,128)(2,1)S(1)} %get-tuple-element.39.refs_1_), channel_id=1, source_target_pairs={{0,192},{64,0},{128,64},{192,128},{1,193},{65,1},{129,65},{193,129... | collective-permute-start | bytes 344072 | tf_op jit(solution)/shard_map/ppermute | solution.py:22
  69.2 9.8 %collective-permute-start.16 = (bf16[64,896]{1,0:T(8,128)(2,1)S(1)}, bf16[64,896]{1,0:T(8,128)(2,1)S(1)}, u32[]{:S(2)}, u32[]{:S(2)}) collective-permute-start(bf16[64,896]{1,0:T(8,128)(2,1)S(1)} %get-tuple-element.39.refs_1_), channel_id=1, source_target_pairs={{0,128},{64,192},{128,0},{192,64},{1,129},{65,193},{129,1},{193,65... | collective-permute-start | bytes 344072 | tf_op jit(solution)/shard_map/ppermute | solution.py:22
  69.7 9.3 %collective-permute-start.15 = (bf16[64,896]{1,0:T(8,128)(2,1)S(1)}, bf16[64,896]{1,0:T(8,128)(2,1)S(1)}, u32[]{:S(2)}, u32[]{:S(2)}) collective-permute-start(bf16[64,896]{1,0:T(8,128)(2,1)S(1)} %get-tuple-element.39.refs_1_), channel_id=1, source_target_pairs={{0,64},{64,128},{128,192},{192,0},{1,65},{65,129},{129,193},{193,1... | collective-permute-start | bytes 344072 | tf_op jit(solution)/shard_map/ppermute | solution.py:22
  71.7 9.8 %collective-permute-start.22 = (bf16[64,896]{1,0:T(8,128)(2,1)S(1)}, bf16[64,896]{1,0:T(8,128)(2,1)S(1)}, u32[]{:S(2)}, u32[]{:S(2)}) collective-permute-start(bf16[64,896]{1,0:T(8,128)(2,1)S(1)} %hidden.1.refs_1_), channel_id=1, source_target_pairs={{0,192},{64,0},{128,64},{192,128},{1,193},{65,1},{129,65},{193,129... | collective-permute-start | bytes 344072 | tf_op jit(solution)/shard_map/ppermute | solution.py:22
  74.5 7.0 %collective-permute-start.21 = (bf16[64,896]{1,0:T(8,128)(2,1)S(1)}, bf16[64,896]{1,0:T(8,128)(2,1)S(1)}, u32[]{:S(2)}, u32[]{:S(2)}) collective-permute-start(bf16[64,896]{1,0:T(8,128)(2,1)S(1)} %hidden.1.refs_1_), channel_id=1, source_target_pairs={{0,128},{64,192},{128,0},{192,64},{1,129},{65,193},{129,1},{193,65... | collective-permute-start | bytes 344072 | tf_op jit(solution)/shard_map/ppermute | solution.py:22
  74.9 6.7 %collective-permute-start.20 = (bf16[64,896]{1,0:T(8,128)(2,1)S(1)}, bf16[64,896]{1,0:T(8,128)(2,1)S(1)}, u32[]{:S(2)}, u32[]{:S(2)}) collective-permute-start(bf16[64,896]{1,0:T(8,128)(2,1)S(1)} %hidden.1.refs_1_), channel_id=1, source_target_pairs={{0,64},{64,128},{128,192},{192,0},{1,65},{65,129},{129,193},{193,1... | collective-permute-start | bytes 344072 | tf_op jit(solution)/shard_map/ppermute | solution.py:22
  84.1 4.1 %collective-permute-start.23 = (bf16[128,2048]{1,0:T(8,128)(2,1)S(1)}, bf16[128,2048]{1,0:T(8,128)(2,1)S(1)}, u32[]{:S(2)}, u32[]{:S(2)}) collective-permute-start(bf16[128,2048]{1,0:T(8,128)(2,1)S(1)} %get-tuple-element.45), channel_id=1, source_target_pairs={{0,1},{1,0},{2,3},{3,2},{4,5},{5,4},{6,7},{7,6},{8,9},{9,8},{10,11... | collective-permute-start | bytes 1572872 | tf_op jit(solution)/shard_map/ppermute | solution.py:18
  86.7 3.4 %collective-permute-start.18 = (bf16[128,2048]{1,0:T(8,128)(2,1)S(1)}, bf16[128,2048]{1,0:T(8,128)(2,1)S(1)}, u32[]{:S(2)}, u32[]{:S(2)}) collective-permute-start(bf16[128,2048]{1,0:T(8,128)(2,1)S(1)} %get-tuple-element.41.refs_6_), channel_id=1, source_target_pairs={{0,1},{1,0},{2,3},{3,2},{4,5},{5,4},{6,7},{7,6},{8,9},{9,8},{10,11... | collective-permute-start | bytes 1572872 | tf_op jit(solution)/shard_map/ppermute | solution.py:18
  88.3 6.4 %collective-permute-start.25 = (bf16[48,2048]{1,0:T(8,128)(2,1)S(1)}, bf16[48,2048]{1,0:T(8,128)(2,1)S(1)}, u32[]{:S(2)}, u32[]{:S(2)}) collective-permute-start(bf16[48,2048]{1,0:T(8,128)(2,1)S(1)} %get-tuple-element.48), channel_id=1, source_target_pairs={{0,2},{2,0},{1,3},{3,1},{4,6},{6,4},{5,7},{7,5},{8,10},{10,8},{9,1... | collective-permute-start | bytes 589832 | tf_op jit(solution)/shard_map/ppermute | solution.py:18
  89.9 11.9 %collective-permute-start.24 = (bf16[80,2048]{1,0:T(8,128)(2,1)S(1)}, bf16[80,2048]{1,0:T(8,128)(2,1)S(1)}, u32[]{:S(2)}, u32[]{:S(2)}) collective-permute-start(bf16[80,2048]{1,0:T(8,128)(2,1)S(1)} %get-tuple-element.46), channel_id=1, source_target_pairs={{0,2},{2,0},{1,3},{3,1},{4,6},{6,4},{5,7},{7,5},{8,10},{10,8},{9,1... | collective-permute-start | bytes 983048 | tf_op jit(solution)/shard_map/ppermute | solution.py:18
  94.8 8.8 %collective-permute-start.26 = (bf16[48,2048]{1,0:T(8,128)(2,1)S(1)}, bf16[48,2048]{1,0:T(8,128)(2,1)S(1)}, u32[]{:S(2)}, u32[]{:S(2)}) collective-permute-start(bf16[48,2048]{1,0:T(8,128)(2,1)S(1)} %sum_near.3), channel_id=1, source_target_pairs={{0,20},{1,13},{4,24},{5,17},{8,28},{9,21},{12,0},{13,25},{16,4},{1... | collective-permute-start | bytes 589832 | tf_op jit(solution)/shard_map/ppermute | solution.py:30
  101.8 6.9 %collective-permute-start.27 = (bf16[32,2048]{1,0:T(8,128)(2,1)S(1)}, bf16[32,2048]{1,0:T(8,128)(2,1)S(1)}, u32[]{:S(2)}, u32[]{:S(2)}) collective-permute-start(bf16[32,2048]{1,0:T(8,128)(2,1)S(1)} %get-tuple-element.49), channel_id=1, source_target_pairs={{0,24},{1,9},{4,28},{5,13},{8,0},{9,17},{12,4},{13,21},{16,8},{17,... | collective-permute-start | bytes 393224 | tf_op jit(solution)/shard_map/ppermute | solution.py:30
  103.7 6.3 %collective-permute-start.28 = (bf16[32,2048]{1,0:T(8,128)(2,1)S(1)}, bf16[32,2048]{1,0:T(8,128)(2,1)S(1)}, u32[]{:S(2)}, u32[]{:S(2)}) collective-permute-start(bf16[32,2048]{1,0:T(8,128)(2,1)S(1)} %relay.1), channel_id=1, source_target_pairs={{0,28},{1,5},{4,0},{5,9},{8,4},{9,13},{12,8},{13,17},{16,12},{17,2... | collective-permute-start | bytes 393224 | tf_op jit(solution)/shard_map/ppermute | solution.py:30
  110.1 4.0 %collective-permute-start.29 = (f32[16,2048]{1,0:T(8,128)S(1)}, f32[16,2048]{1,0:T(8,128)S(1)}, u32[]{:S(2)}, u32[]{:S(2)}) collective-permute-start(f32[16,2048]{1,0:T(8,128)S(1)} %get-tuple-element.52), channel_id=1, source_target_pairs={{0,1},{1,0},{2,3},{3,2},{4,5},{5,4},{6,7},{7,6},{8,9},{9,8},{10,11... | collective-permute-start | bytes 393224 | tf_op jit(solution)/shard_map/ppermute | solution.py:18
  (9 other events, 47.2 us)

commit v3 on v2

--- a/solution.py
+++ b/solution.py
@@ -95,7 +95,7 @@
 
     def body(numbers, ins, outs, scratch):
         features, held = scratch
-        quants, scales = ins[2:], numbers[1:]
+        quants, scales = ins[-2:], numbers[1:]
 
         def fill(j):
             for side in range(2):
@@ -105,10 +105,13 @@
                     block = (block * scales[side][j, i]).astype(BF16)
                     held[j % 2, rows, side * BLOCK : (side + 1) * BLOCK] = block
 
-        for chunk in range(4):
-            at = pl.multiple_of(lax.rem(chunk + 4 - numbers[0][0], 4) * 64, 64)
-            rows = slice(64 * (chunk % 2), 64 * (chunk % 2 + 1))
-            features[pl.ds(at, 64), :] = ins[chunk // 2][rows, :]
+        row = 0
+        for piece in ins[:-2]:
+            for low in range(0, piece.shape[0], 16):
+                slot = lax.rem(row // 64 + 4 - numbers[0][0], 4)
+                at = pl.multiple_of(slot * 64 + row % 64, 16)
+                features[pl.ds(at, 16), :] = piece[low : low + 16, :]
+                row += 16
         fill(0)
         for j in range(count):
             if j + 1 < count:
@@ -254,16 +257,17 @@
     both = (gate_quant, gate_scale, up_quant, up_scale)
     last_weight = down_weight(down_quant, down_scale)
 
-    chip = joined([tokens, swap(tokens, "core")])
+    chip = jnp.concatenate([tokens, swap(tokens, "core")])
     z4 = shift_z(tokens, 4)
     z3, z2, z1 = (shift_z(chip, j) for j in (3, 2, 1))
-    a = joined([tokens, z1, z2, z3, z4])
-    b, c = swap(a, "core"), swap(a, "yl")
-
-    outs_a = gate_up(me, [a, b], *both)
+    a1, a2 = jnp.concatenate([tokens, z1]), jnp.concatenate([z2, z3, z4])
+    c1, c2 = swap(a1, "yl"), swap(a2, "yl")
+    b1, b2 = swap(a1, "core"), swap(a2, "core")
+
+    outs_a = gate_up(me, [a1, a2, b1, b2], *both)
     parts_a = [shift_x(outs_a[k], k) for k in (2, 1, 3)]
-    c = joined([c], later=[outs_a[0]])
-    outs_c = gate_up(me, [c, swap(c, "core")], *both)
+    c1, c2 = joined([c1], later=[outs_a[0]]), joined([c2], later=[outs_a[0]])
+    outs_c = gate_up(me, [c1, c2, swap(c1, "core"), swap(c2, "core")], *both)
     total_a, sent_a = sum_x(outs_a, parts_a, later=[outs_c[0]])
     other_a = swap(sent_a, "yh")
     parts_c = [shift_x(outs_c[k], k) for k in (2, 1, 3)]

time: 115 us -> 111 us (0.965)
  waiting for transfers between devices: 40.1 us -> 35.9 us
    ppermute x7, waiting for transfers between devices: 12.5 us -> 8.82 us  [shift_z(): return lax.ppermute(value, ('z', 'core'), pairs)]
    ppermute x12, starting transfers between devices: 14.8 us -> 12.6 us  [shift_x(): return lax.ppermute(value, 'x', [(i, (i + by) % 4) for i in range(4)])]
    ppermute x7, starting transfers between devices: 12.5 us -> 14 us  [shift_z(): return lax.ppermute(value, ('z', 'core'), pairs)]
    ppermute x11 -> x14, starting transfers between devices: 22.4 us -> 23.1 us  [swap(): return lax.ppermute(value, axis, [(0, 1), (1, 0)])]
    ppermute x11 -> x14, waiting for transfers between devices: 19.4 us -> 19.2 us  [swap(): return lax.ppermute(value, axis, [(0, 1), (1, 0)])]
    pallas_call x16 -> x15, Pallas kernels: 15.6 us -> 15.5 us  [call(): pl.pallas_call(kernel, in_specs=[pl.BlockSpec(memory_space=pltpu.SMEM)] *...]
    unnamed x23 -> x22, local copies, waits for them, and re-layouts: 8.43 us -> 8.46 us
  transfers between devices with their start and end apart: 30 -> 33, of which waited for: 16 -> 15; matrix products, arithmetic and copies ran while one was open for 0% -> 1% of each run, Pallas kernels for 11% -> 11%
where the time goes in v3:
time: 111 us
  starting transfers between devices  49.7 us (45%)
  waiting for transfers between devices  35.9 us (32%)
  Pallas kernels  15.5 us (14%)
  local copies, waits for them, and re-layouts  8.48 us (8%)
    ppermute x14, starting transfers between devices, swap(): return lax.ppermute(value, axis, [(0, 1), (1, 0)])  23.1 us
    ppermute x14, waiting for transfers between devices, swap(): return lax.ppermute(value, axis, [(0, 1), (1, 0)])  19.2 us
    pallas_call x15, Pallas kernels, call(): pl.pallas_call(kernel, in_specs=[pl.BlockSpec(memory_space=pltpu.SMEM)] *...  15.5 us
    ppermute x7, starting transfers between devices, shift_z(): return lax.ppermute(value, ('z', 'core'), pairs)  14 us
    ppermute x12, starting transfers between devices, shift_x(): return lax.ppermute(value, 'x', [(i, (i + by) % 4) for i in range(4)])  12.6 us
    ppermute x7, waiting for transfers between devices, shift_z(): return lax.ppermute(value, ('z', 'core'), pairs)  8.82 us
    unnamed x22, local copies, waits for them, and re-layouts  8.46 us
    ppermute x12, waiting for transfers between devices, shift_x(): return lax.ppermute(value, 'x', [(i, (i + by) % 4) for i in range(4)])  7.95 us
  transfers between devices with their start and end apart: 33, of which 15 were waited for; matrix products, arithmetic and copies ran while one was open for 1% of the time, Pallas kernels for 11%

profile of v3, /device:TPU:1, one launch (start us, length us, event | category | flops | bytes accessed | tf_op | source)
XLA Modules:
  0.0 110.5 jit_solution(4368954109359457329)
XLA Ops:
  0.0 3.2 %collective-permute-start = (bf16[16,2048]{1,0:T(8,128)(2,1)}, bf16[16,2048]{1,0:T(8,128)(2,1)S(1)}, u32[]{:S(2)}, u32[]{:S(2)}) collective-permute-start(bf16[16,2048]{1,0:T(8,128)(2,1)} %param.7), channel_id=1, source_target_pairs={{0,1},{1,0},{2,3},{3,2},{4,5},{5,4},{6,7},{7,6},{8,9},{9,8},{10,11... | collective-permute-start | bytes 196616 | tf_op jit(solution)/shard_map/ppermute | solution.py:18
  4.4 4.3 %collective-permute-start.3 = (bf16[32,2048]{1,0:T(8,128)(2,1)S(1)}, bf16[32,2048]{1,0:T(8,128)(2,1)S(1)}, u32[]{:S(2)}, u32[]{:S(2)}) collective-permute-start(bf16[32,2048]{1,0:T(8,128)(2,1)S(1)} %constant_dynamic-update-slice_fusion), channel_id=1, source_target_pairs={{0,8},{1,25},{4,12},{5,29},{8,16},{9,1},{12,20},{13,5},{16,24},{17... | collective-permute-start | bytes 393224 | tf_op jit(solution)/shard_map/ppermute | solution.py:30
  9.6 3.9 %collective-permute-start.4 = (bf16[32,2048]{1,0:T(8,128)(2,1)S(1)}, bf16[32,2048]{1,0:T(8,128)(2,1)S(1)}, u32[]{:S(2)}, u32[]{:S(2)}) collective-permute-start(bf16[32,2048]{1,0:T(8,128)(2,1)S(1)} %constant_dynamic-update-slice_fusion), channel_id=1, source_target_pairs={{0,12},{1,21},{4,16},{5,25},{8,20},{9,29},{12,24},{13,1},{16,28},{... | collective-permute-start | bytes 393224 | tf_op jit(solution)/shard_map/ppermute | solution.py:30
  15.0 4.1 %collective-permute-done.4 = bf16[32,2048]{1,0:T(8,128)(2,1)S(1)} collective-permute-done((bf16[32,2048]{1,0:T(8,128)(2,1)S(1)}, bf16[32,2048]{1,0:T(8,128)(2,1)S(1)}, u32[]{:S(2)}, u32[]{:S(2)}) %collective-permute-start.4) | collective-permute-done | bytes 131104 | tf_op jit(solution)/shard_map/ppermute | solution.py:30
  19.1 1.4 %collective-permute-start.8 = (bf16[80,2048]{1,0:T(8,128)(2,1)S(1)}, bf16[80,2048]{1,0:T(8,128)(2,1)S(1)}, u32[]{:S(2)}, u32[]{:S(2)}) collective-permute-start(bf16[80,2048]{1,0:T(8,128)(2,1)S(1)} %constant_dynamic-update-slice_fusion.4.refs_4_), channel_id=1, source_target_pairs={{0,2},{2,0},{1,3},{3,1},{4,6},{6,4},{5,7},{7,5},{8,10},{10,8},{9,1... | collective-permute-start | bytes 983048 | tf_op jit(solution)/shard_map/ppermute | solution.py:18
  20.4 3.5 %collective-permute-start.7 = (bf16[80,2048]{1,0:T(8,128)(2,1)S(1)}, bf16[80,2048]{1,0:T(8,128)(2,1)S(1)}, u32[]{:S(2)}, u32[]{:S(2)}) collective-permute-start(bf16[80,2048]{1,0:T(8,128)(2,1)S(1)} %constant_dynamic-update-slice_fusion.4.refs_4_), channel_id=1, source_target_pairs={{0,1},{1,0},{2,3},{3,2},{4,5},{5,4},{6,7},{7,6},{8,9},{9,8},{10,11... | collective-permute-start | bytes 983048 | tf_op jit(solution)/shard_map/ppermute | solution.py:18
  25.5 2.0 %copy-done = bf16[2048,896]{1,0:T(8,128)(2,1)S(1)} copy-done((bf16[2048,896]{1,0:T(8,128)(2,1)S(1)}, bf16[2048,896]{1,0:T(8,128)(2,1)}, u32[]{:S(2)}) %copy-start) | copy-done | bytes 3670040
  27.6 2.0 %copy-done.2 = bf16[2048,896]{1,0:T(8,128)(2,1)S(1)} copy-done((bf16[2048,896]{1,0:T(8,128)(2,1)S(1)}, bf16[2048,896]{1,0:T(8,128)(2,1)}, u32[]{:S(2)}) %copy-start.2) | copy-done | bytes 3670040
  31.0 4.0 %gate_up.2 = (bf16[64,1792]{1,0:T(8,128)(2,1)S(1)}, bf16[64,1792]{1,0:T(8,128)(2,1)S(1)}, bf16[64,1792]{1,0:T(8,128)(2,1)S(1)}, bf16[64,1792]{1,0:T(8,128)(2,1)S(1)}) custom-call(s32[1]{0:T(128)} %bitcast.refs_0_, f32[7,16]{1,0:T(8,128)S(1)} %bitcast.5, f32[7,16]{1,0:T(8,128)S(1)} %bitcast.7, ...), custom_call_target="tpu_custom_call" | custom-call | flops 1024 | bytes 1024 | tf_op jit(solution)/shard_map/gate_up/pallas_call | solution.py:45
  35.5 2.7 %collective-permute-start.14 = (bf16[64,1792]{1,0:T(8,128)(2,1)S(1)}, bf16[64,1792]{1,0:T(8,128)(2,1)S(1)}, u32[]{:S(2)}, u32[]{:S(2)}) collective-permute-start(bf16[64,1792]{1,0:T(8,128)(2,1)S(1)} %get-tuple-element.34), channel_id=1, source_target_pairs={{0,128},{64,192},{128,0},{192,64},{1,129},{65,193},{129,1},{193,65... | collective-permute-start | bytes 688136 | tf_op jit(solution)/shard_map/ppermute | solution.py:22
  38.5 2.4 %collective-permute-start.16 = (bf16[64,1792]{1,0:T(8,128)(2,1)S(1)}, bf16[64,1792]{1,0:T(8,128)(2,1)S(1)}, u32[]{:S(2)}, u32[]{:S(2)}) collective-permute-start(bf16[64,1792]{1,0:T(8,128)(2,1)S(1)} %get-tuple-element.36), channel_id=1, source_target_pairs={{0,192},{64,0},{128,64},{192,128},{1,193},{65,1},{129,65},{193,129... | collective-permute-start | bytes 688136 | tf_op jit(solution)/shard_map/ppermute | solution.py:22
  40.9 1.3 %collective-permute-start.9 = (bf16[48,2048]{1,0:T(8,128)(2,1)S(1)}, bf16[48,2048]{1,0:T(8,128)(2,1)S(1)}, u32[]{:S(2)}, u32[]{:S(2)}) collective-permute-start(bf16[48,2048]{1,0:T(8,128)(2,1)S(1)} %joined.2.refs_3_), channel_id=1, source_target_pairs={{0,1},{1,0},{2,3},{3,2},{4,5},{5,4},{6,7},{7,6},{8,9},{9,8},{10,11... | collective-permute-start | bytes 589832 | tf_op jit(solution)/shard_map/ppermute | solution.py:18
  43.3 4.0 %gate_up.3 = (bf16[64,1792]{1,0:T(8,128)(2,1)S(1)}, bf16[64,1792]{1,0:T(8,128)(2,1)S(1)}, bf16[64,1792]{1,0:T(8,128)(2,1)S(1)}, bf16[64,1792]{1,0:T(8,128)(2,1)S(1)}) custom-call(s32[1]{0:T(128)} %bitcast.refs_0_, f32[7,16]{1,0:T(8,128)S(1)} %bitcast.6, f32[7,16]{1,0:T(8,128)S(1)} %bitcast.8, bf16[48,2048]{1,0:T(8,128)(2,1)S(1)} %joined.2.refs_3_, ...), custom_call_target="tpu_custom_call" | custom-call | flops 1024 | bytes 1024 | tf_op jit(solution)/shard_map/gate_up/pallas_call | solution.py:45
  47.6 2.5 %collective-permute-start.13 = (bf16[64,1792]{1,0:T(8,128)(2,1)S(1)}, bf16[64,1792]{1,0:T(8,128)(2,1)S(1)}, u32[]{:S(2)}, u32[]{:S(2)}) collective-permute-start(bf16[64,1792]{1,0:T(8,128)(2,1)S(1)} %get-tuple-element.33), channel_id=1, source_target_pairs={{0,192},{64,0},{128,64},{192,128},{1,193},{65,1},{129,65},{193,129... | collective-permute-start | bytes 688136 | tf_op jit(solution)/shard_map/ppermute | solution.py:22
  50.2 2.7 %collective-permute-start.17 = (bf16[64,1792]{1,0:T(8,128)(2,1)S(1)}, bf16[64,1792]{1,0:T(8,128)(2,1)S(1)}, u32[]{:S(2)}, u32[]{:S(2)}) collective-permute-start(bf16[64,1792]{1,0:T(8,128)(2,1)S(1)} %get-tuple-element.38), channel_id=1, source_target_pairs={{0,32},{32,0},{1,33},{33,1},{2,34},{34,2},{3,35},{35,3},{4,36},{36... | collective-permute-start | bytes 688136 | tf_op jit(solution)/shard_map/ppermute | solution.py:18
  52.9 2.7 %collective-permute-done.11.refs_1_ = bf16[64,1792]{1,0:T(8,128)(2,1)S(1)} collective-permute-done((bf16[64,1792]{1,0:T(8,128)(2,1)S(1)}, bf16[64,1792]{1,0:T(8,128)(2,1)S(1)}, u32[]{:S(2)}, u32[]{:S(2)}) %collective-permute-start.11) | collective-permute-done | bytes 229408 | tf_op jit(solution)/shard_map/ppermute | solution.py:22
  55.7 5.2 %collective-permute-done.12.refs_2_ = bf16[64,1792]{1,0:T(8,128)(2,1)S(1)} collective-permute-done((bf16[64,1792]{1,0:T(8,128)(2,1)S(1)}, bf16[64,1792]{1,0:T(8,128)(2,1)S(1)}, u32[]{:S(2)}, u32[]{:S(2)}) %collective-permute-start.12) | collective-permute-done | bytes 229408 | tf_op jit(solution)/shard_map/ppermute | solution.py:22
  61.1 2.7 %collective-permute-start.22 = (bf16[64,1792]{1,0:T(8,128)(2,1)S(1)}, bf16[64,1792]{1,0:T(8,128)(2,1)S(1)}, u32[]{:S(2)}, u32[]{:S(2)}) collective-permute-start(bf16[64,1792]{1,0:T(8,128)(2,1)S(1)} %get-tuple-element.43), channel_id=1, source_target_pairs={{0,32},{32,0},{1,33},{33,1},{2,34},{34,2},{3,35},{35,3},{4,36},{36... | collective-permute-start | bytes 688136 | tf_op jit(solution)/shard_map/ppermute | solution.py:18
  65.8 3.3 %collective-permute-done.22.refs_1_ = bf16[64,1792]{1,0:T(8,128)(2,1)S(1)} collective-permute-done((bf16[64,1792]{1,0:T(8,128)(2,1)S(1)}, bf16[64,1792]{1,0:T(8,128)(2,1)S(1)}, u32[]{:S(2)}, u32[]{:S(2)}) %collective-permute-start.22) | collective-permute-done | bytes 229408 | tf_op jit(solution)/shard_map/ppermute | solution.py:18
  69.2 1.2 %collective-permute-start.25 = (bf16[64,896]{1,0:T(8,128)(2,1)S(1)}, bf16[64,896]{1,0:T(8,128)(2,1)S(1)}, u32[]{:S(2)}, u32[]{:S(2)}) collective-permute-start(bf16[64,896]{1,0:T(8,128)(2,1)S(1)} %hidden.1.refs_1_), channel_id=1, source_target_pairs={{0,192},{64,0},{128,64},{192,128},{1,193},{65,1},{129,65},{193,129... | collective-permute-start | bytes 344072 | tf_op jit(solution)/shard_map/ppermute | solution.py:22
  71.7 2.0 %copy-done.4 = bf16[896,2048]{1,0:T(8,128)(2,1)S(1)} copy-done((bf16[896,2048]{1,0:T(8,128)(2,1)S(1)}, bf16[896,2048]{1,0:T(8,128)(2,1)}, u32[]{:S(2)}) %copy-start.4) | copy-done | bytes 3670040
  73.7 1.6 %down_weight.1.refs_5_ = bf16[896,2048]{1,0:T(8,128)(2,1)S(1)} custom-call(f32[16,7]{1,0:T(8,128)S(1)} %bitcast.4, bf16[896,2048]{1,0:T(8,128)(2,1)S(1)} %copy-done.4), custom_call_target="tpu_custom_call" | custom-call | flops 1024 | bytes 1024 | tf_op jit(solution)/shard_map/down_weight/pallas_call | solution.py:45
  75.4 2.5 %down.2 = (f32[128,2048]{1,0:T(8,128)S(1)}, bf16[128,2048]{1,0:T(8,128)(2,1)S(1)}) custom-call(s32[1]{0:T(128)} %bitcast.refs_0_, bf16[64,896]{1,0:T(8,128)(2,1)S(1)} %get-tuple-element.39.refs_1_, bf16[64,896]{1,0:T(8,128)(2,1)S(1)} %collective-permute-done.18.refs_2_, bf16[64,896]{1,0:T(8,128)(2,1)S(1)} %collective-permute-done.19.refs_3_, ...), custom_call_target="tpu_custom_call" | custom-call | flops 1024 | bytes 1024 | tf_op jit(solution)/shard_map/down/pallas_call | solution.py:45
  77.9 2.5 %down.3 = (f32[128,2048]{1,0:T(8,128)S(1)}, bf16[128,2048]{1,0:T(8,128)(2,1)S(1)}) custom-call(s32[1]{0:T(128)} %bitcast.refs_0_, bf16[64,896]{1,0:T(8,128)(2,1)S(1)} %hidden.1.refs_1_, bf16[64,896]{1,0:T(8,128)(2,1)S(1)} %collective-permute-done.23.refs_2_, bf16[64,896]{1,0:T(8,128)(2,1)S(1)} %collective-permute-done.24.refs_3_, ...), custom_call_target="tpu_custom_call" | custom-call | flops 1024 | bytes 1024 | tf_op jit(solution)/shard_map/down/pallas_call | solution.py:45
  80.5 2.3 %collective-permute-start.26 = (bf16[128,2048]{1,0:T(8,128)(2,1)S(1)}, bf16[128,2048]{1,0:T(8,128)(2,1)S(1)}, u32[]{:S(2)}, u32[]{:S(2)}) collective-permute-start(bf16[128,2048]{1,0:T(8,128)(2,1)S(1)} %get-tuple-element.45), channel_id=1, source_target_pairs={{0,1},{1,0},{2,3},{3,2},{4,5},{5,4},{6,7},{7,6},{8,9},{9,8},{10,11... | collective-permute-start | bytes 1572872 | tf_op jit(solution)/shard_map/ppermute | solution.py:18
  82.9 1.4 %collective-permute-done.26.refs_1_ = bf16[128,2048]{1,0:T(8,128)(2,1)S(1)} collective-permute-done((bf16[128,2048]{1,0:T(8,128)(2,1)S(1)}, bf16[128,2048]{1,0:T(8,128)(2,1)S(1)}, u32[]{:S(2)}, u32[]{:S(2)}) %collective-permute-start.26) | collective-permute-done | bytes 524320 | tf_op jit(solution)/shard_map/ppermute | solution.py:18
  86.2 4.6 %collective-permute-done.28.refs_2_ = bf16[48,2048]{1,0:T(8,128)(2,1)S(1)} collective-permute-done((bf16[48,2048]{1,0:T(8,128)(2,1)S(1)}, bf16[48,2048]{1,0:T(8,128)(2,1)S(1)}, u32[]{:S(2)}, u32[]{:S(2)}) %collective-permute-start.28) | collective-permute-done | bytes 196640 | tf_op jit(solution)/shard_map/ppermute | solution.py:18
  91.1 6.7 %collective-permute-done.27.refs_2_ = bf16[80,2048]{1,0:T(8,128)(2,1)S(1)} collective-permute-done((bf16[80,2048]{1,0:T(8,128)(2,1)S(1)}, bf16[80,2048]{1,0:T(8,128)(2,1)S(1)}, u32[]{:S(2)}, u32[]{:S(2)}) %collective-permute-start.27) | collective-permute-done | bytes 327712 | tf_op jit(solution)/shard_map/ppermute | solution.py:18
  99.1 3.6 %collective-permute-start.31 = (bf16[32,2048]{1,0:T(8,128)(2,1)S(1)}, bf16[32,2048]{1,0:T(8,128)(2,1)S(1)}, u32[]{:S(2)}, u32[]{:S(2)}) collective-permute-start(bf16[32,2048]{1,0:T(8,128)(2,1)S(1)} %relay.1), channel_id=1, source_target_pairs={{0,28},{1,5},{4,0},{5,9},{8,4},{9,13},{12,8},{13,17},{16,12},{17,2... | collective-permute-start | bytes 393224 | tf_op jit(solution)/shard_map/ppermute | solution.py:30
  102.7 1.7 %collective-permute-done.30.refs_2_ = bf16[32,2048]{1,0:T(8,128)(2,1)S(1)} collective-permute-done((bf16[32,2048]{1,0:T(8,128)(2,1)S(1)}, bf16[32,2048]{1,0:T(8,128)(2,1)S(1)}, u32[]{:S(2)}, u32[]{:S(2)}) %collective-permute-start.30) | collective-permute-done | bytes 131104 | tf_op jit(solution)/shard_map/ppermute | solution.py:30
  104.4 1.5 %collective-permute-done.31.refs_3_ = bf16[32,2048]{1,0:T(8,128)(2,1)S(1)} collective-permute-done((bf16[32,2048]{1,0:T(8,128)(2,1)S(1)}, bf16[32,2048]{1,0:T(8,128)(2,1)S(1)}, u32[]{:S(2)}, u32[]{:S(2)}) %collective-permute-start.31) | collective-permute-done | bytes 131104 | tf_op jit(solution)/shard_map/ppermute | solution.py:30
  106.0 2.9 %collective-permute-start.32 = (f32[16,2048]{1,0:T(8,128)S(1)}, f32[16,2048]{1,0:T(8,128)S(1)}, u32[]{:S(2)}, u32[]{:S(2)}) collective-permute-start(f32[16,2048]{1,0:T(8,128)S(1)} %get-tuple-element.52), channel_id=1, source_target_pairs={{0,1},{1,0},{2,3},{3,2},{4,5},{5,4},{6,7},{7,6},{8,9},{9,8},{10,11... | collective-permute-start | bytes 393224 | tf_op jit(solution)/shard_map/ppermute | solution.py:18
  (75 shorter events, 17.6 us)
Async XLA Ops:
  0.0 4.4 %collective-permute-start = (bf16[16,2048]{1,0:T(8,128)(2,1)}, bf16[16,2048]{1,0:T(8,128)(2,1)S(1)}, u32[]{:S(2)}, u32[]{:S(2)}) collective-permute-start(bf16[16,2048]{1,0:T(8,128)(2,1)} %param.7), channel_id=1, source_target_pairs={{0,1},{1,0},{2,3},{3,2},{4,5},{5,4},{6,7},{7,6},{8,9},{9,8},{10,11... | collective-permute-start | bytes 196616 | tf_op jit(solution)/shard_map/ppermute | solution.py:18
  4.4 10.6 %collective-permute-start.3 = (bf16[32,2048]{1,0:T(8,128)(2,1)S(1)}, bf16[32,2048]{1,0:T(8,128)(2,1)S(1)}, u32[]{:S(2)}, u32[]{:S(2)}) collective-permute-start(bf16[32,2048]{1,0:T(8,128)(2,1)S(1)} %constant_dynamic-update-slice_fusion), channel_id=1, source_target_pairs={{0,8},{1,25},{4,12},{5,29},{8,16},{9,1},{12,20},{13,5},{16,24},{17... | collective-permute-start | bytes 393224 | tf_op jit(solution)/shard_map/ppermute | solution.py:30
  8.6 10.4 %collective-permute-start.5 = (bf16[16,2048]{1,0:T(8,128)(2,1)}, bf16[16,2048]{1,0:T(8,128)(2,1)S(1)}, u32[]{:S(2)}, u32[]{:S(2)}) collective-permute-start(bf16[16,2048]{1,0:T(8,128)(2,1)} %param.7), channel_id=1, source_target_pairs={{0,16},{1,17},{4,20},{5,21},{8,24},{9,25},{12,28},{13,29},{16,0},{... | collective-permute-start | bytes 196616 | tf_op jit(solution)/shard_map/ppermute | solution.py:30
  9.6 9.4 %collective-permute-start.4 = (bf16[32,2048]{1,0:T(8,128)(2,1)S(1)}, bf16[32,2048]{1,0:T(8,128)(2,1)S(1)}, u32[]{:S(2)}, u32[]{:S(2)}) collective-permute-start(bf16[32,2048]{1,0:T(8,128)(2,1)S(1)} %constant_dynamic-update-slice_fusion), channel_id=1, source_target_pairs={{0,12},{1,21},{4,16},{5,25},{8,20},{9,29},{12,24},{13,1},{16,28},{... | collective-permute-start | bytes 393224 | tf_op jit(solution)/shard_map/ppermute | solution.py:30
  13.6 10.4 %collective-permute-start.1 = (bf16[32,2048]{1,0:T(8,128)(2,1)S(1)}, bf16[32,2048]{1,0:T(8,128)(2,1)S(1)}, u32[]{:S(2)}, u32[]{:S(2)}) collective-permute-start(bf16[32,2048]{1,0:T(8,128)(2,1)S(1)} %constant_dynamic-update-slice_fusion), channel_id=1, source_target_pairs={{0,4},{1,29},{4,8},{5,1},{8,12},{9,5},{12,16},{13,9},{16,20},{17,1... | collective-permute-start | bytes 393224 | tf_op jit(solution)/shard_map/ppermute | solution.py:30
  19.1 15.9 %collective-permute-start.8 = (bf16[80,2048]{1,0:T(8,128)(2,1)S(1)}, bf16[80,2048]{1,0:T(8,128)(2,1)S(1)}, u32[]{:S(2)}, u32[]{:S(2)}) collective-permute-start(bf16[80,2048]{1,0:T(8,128)(2,1)S(1)} %constant_dynamic-update-slice_fusion.4.refs_4_), channel_id=1, source_target_pairs={{0,2},{2,0},{1,3},{3,1},{4,6},{6,4},{5,7},{7,5},{8,10},{10,8},{9,1... | collective-permute-start | bytes 983048 | tf_op jit(solution)/shard_map/ppermute | solution.py:18
  20.4 5.1 %collective-permute-start.7 = (bf16[80,2048]{1,0:T(8,128)(2,1)S(1)}, bf16[80,2048]{1,0:T(8,128)(2,1)S(1)}, u32[]{:S(2)}, u32[]{:S(2)}) collective-permute-start(bf16[80,2048]{1,0:T(8,128)(2,1)S(1)} %constant_dynamic-update-slice_fusion.4.refs_4_), channel_id=1, source_target_pairs={{0,1},{1,0},{2,3},{3,2},{4,5},{5,4},{6,7},{7,6},{8,9},{9,8},{10,11... | collective-permute-start | bytes 983048 | tf_op jit(solution)/shard_map/ppermute | solution.py:18
  24.1 16.8 %collective-permute-start.2 = (bf16[48,2048]{1,0:T(8,128)(2,1)S(1)}, bf16[48,2048]{1,0:T(8,128)(2,1)S(1)}, u32[]{:S(2)}, u32[]{:S(2)}) collective-permute-start(bf16[48,2048]{1,0:T(8,128)(2,1)S(1)} %constant_dynamic-update-slice_fusion.2.refs_3_), channel_id=1, source_target_pairs={{0,2},{2,0},{1,3},{3,1},{4,6},{6,4},{5,7},{7,5},{8,10},{10,8},{9,1... | collective-permute-start | bytes 589832 | tf_op jit(solution)/shard_map/ppermute | solution.py:18
  35.0 8.2 %collective-permute-start.10 = (bf16[80,2048]{1,0:T(8,128)(2,1)S(1)}, bf16[80,2048]{1,0:T(8,128)(2,1)S(1)}, u32[]{:S(2)}, u32[]{:S(2)}) collective-permute-start(bf16[80,2048]{1,0:T(8,128)(2,1)S(1)} %joined.3.refs_4_), channel_id=1, source_target_pairs={{0,1},{1,0},{2,3},{3,2},{4,5},{5,4},{6,7},{7,6},{8,9},{9,8},{10,11... | collective-permute-start | bytes 983048 | tf_op jit(solution)/shard_map/ppermute | solution.py:18
  35.5 12.2 %collective-permute-start.14 = (bf16[64,1792]{1,0:T(8,128)(2,1)S(1)}, bf16[64,1792]{1,0:T(8,128)(2,1)S(1)}, u32[]{:S(2)}, u32[]{:S(2)}) collective-permute-start(bf16[64,1792]{1,0:T(8,128)(2,1)S(1)} %get-tuple-element.34), channel_id=1, source_target_pairs={{0,128},{64,192},{128,0},{192,64},{1,129},{65,193},{129,1},{193,65... | collective-permute-start | bytes 688136 | tf_op jit(solution)/shard_map/ppermute | solution.py:22
  38.2 11.9 %collective-permute-start.15 = (bf16[64,1792]{1,0:T(8,128)(2,1)S(1)}, bf16[64,1792]{1,0:T(8,128)(2,1)S(1)}, u32[]{:S(2)}, u32[]{:S(2)}) collective-permute-start(bf16[64,1792]{1,0:T(8,128)(2,1)S(1)} %get-tuple-element.35), channel_id=1, source_target_pairs={{0,64},{64,128},{128,192},{192,0},{1,65},{65,129},{129,193},{193,1... | collective-permute-start | bytes 688136 | tf_op jit(solution)/shard_map/ppermute | solution.py:22
  38.5 11.6 %collective-permute-start.16 = (bf16[64,1792]{1,0:T(8,128)(2,1)S(1)}, bf16[64,1792]{1,0:T(8,128)(2,1)S(1)}, u32[]{:S(2)}, u32[]{:S(2)}) collective-permute-start(bf16[64,1792]{1,0:T(8,128)(2,1)S(1)} %get-tuple-element.36), channel_id=1, source_target_pairs={{0,192},{64,0},{128,64},{192,128},{1,193},{65,1},{129,65},{193,129... | collective-permute-start | bytes 688136 | tf_op jit(solution)/shard_map/ppermute | solution.py:22
  40.9 2.3 %collective-permute-start.9 = (bf16[48,2048]{1,0:T(8,128)(2,1)S(1)}, bf16[48,2048]{1,0:T(8,128)(2,1)S(1)}, u32[]{:S(2)}, u32[]{:S(2)}) collective-permute-start(bf16[48,2048]{1,0:T(8,128)(2,1)S(1)} %joined.2.refs_3_), channel_id=1, source_target_pairs={{0,1},{1,0},{2,3},{3,2},{4,5},{5,4},{6,7},{7,6},{8,9},{9,8},{10,11... | collective-permute-start | bytes 589832 | tf_op jit(solution)/shard_map/ppermute | solution.py:18
  47.2 8.4 %collective-permute-start.11 = (bf16[64,1792]{1,0:T(8,128)(2,1)S(1)}, bf16[64,1792]{1,0:T(8,128)(2,1)S(1)}, u32[]{:S(2)}, u32[]{:S(2)}) collective-permute-start(bf16[64,1792]{1,0:T(8,128)(2,1)S(1)} %get-tuple-element.31), channel_id=1, source_target_pairs={{0,128},{64,192},{128,0},{192,64},{1,129},{65,193},{129,1},{193,65... | collective-permute-start | bytes 688136 | tf_op jit(solution)/shard_map/ppermute | solution.py:22
  47.3 13.5 %collective-permute-start.12 = (bf16[64,1792]{1,0:T(8,128)(2,1)S(1)}, bf16[64,1792]{1,0:T(8,128)(2,1)S(1)}, u32[]{:S(2)}, u32[]{:S(2)}) collective-permute-start(bf16[64,1792]{1,0:T(8,128)(2,1)S(1)} %get-tuple-element.32), channel_id=1, source_target_pairs={{0,64},{64,128},{128,192},{192,0},{1,65},{65,129},{129,193},{193,1... | collective-permute-start | bytes 688136 | tf_op jit(solution)/shard_map/ppermute | solution.py:22
  47.6 13.2 %collective-permute-start.13 = (bf16[64,1792]{1,0:T(8,128)(2,1)S(1)}, bf16[64,1792]{1,0:T(8,128)(2,1)S(1)}, u32[]{:S(2)}, u32[]{:S(2)}) collective-permute-start(bf16[64,1792]{1,0:T(8,128)(2,1)S(1)} %get-tuple-element.33), channel_id=1, source_target_pairs={{0,192},{64,0},{128,64},{192,128},{1,193},{65,1},{129,65},{193,129... | collective-permute-start | bytes 688136 | tf_op jit(solution)/shard_map/ppermute | solution.py:22
  50.2 10.6 %collective-permute-start.17 = (bf16[64,1792]{1,0:T(8,128)(2,1)S(1)}, bf16[64,1792]{1,0:T(8,128)(2,1)S(1)}, u32[]{:S(2)}, u32[]{:S(2)}) collective-permute-start(bf16[64,1792]{1,0:T(8,128)(2,1)S(1)} %get-tuple-element.38), channel_id=1, source_target_pairs={{0,32},{32,0},{1,33},{33,1},{2,34},{34,2},{3,35},{35,3},{4,36},{36... | collective-permute-start | bytes 688136 | tf_op jit(solution)/shard_map/ppermute | solution.py:18
  61.1 8.0 %collective-permute-start.22 = (bf16[64,1792]{1,0:T(8,128)(2,1)S(1)}, bf16[64,1792]{1,0:T(8,128)(2,1)S(1)}, u32[]{:S(2)}, u32[]{:S(2)}) collective-permute-start(bf16[64,1792]{1,0:T(8,128)(2,1)S(1)} %get-tuple-element.43), channel_id=1, source_target_pairs={{0,32},{32,0},{1,33},{33,1},{2,34},{34,2},{3,35},{35,3},{4,36},{36... | collective-permute-start | bytes 688136 | tf_op jit(solution)/shard_map/ppermute | solution.py:18
  63.8 7.1 %collective-permute-start.20 = (bf16[64,896]{1,0:T(8,128)(2,1)S(1)}, bf16[64,896]{1,0:T(8,128)(2,1)S(1)}, u32[]{:S(2)}, u32[]{:S(2)}) collective-permute-start(bf16[64,896]{1,0:T(8,128)(2,1)S(1)} %get-tuple-element.39.refs_1_), channel_id=1, source_target_pairs={{0,192},{64,0},{128,64},{192,128},{1,193},{65,1},{129,65},{193,129... | collective-permute-start | bytes 344072 | tf_op jit(solution)/shard_map/ppermute | solution.py:22
  64.7 10.7 %collective-permute-start.19 = (bf16[64,896]{1,0:T(8,128)(2,1)S(1)}, bf16[64,896]{1,0:T(8,128)(2,1)S(1)}, u32[]{:S(2)}, u32[]{:S(2)}) collective-permute-start(bf16[64,896]{1,0:T(8,128)(2,1)S(1)} %get-tuple-element.39.refs_1_), channel_id=1, source_target_pairs={{0,128},{64,192},{128,0},{192,64},{1,129},{65,193},{129,1},{193,65... | collective-permute-start | bytes 344072 | tf_op jit(solution)/shard_map/ppermute | solution.py:22
  65.2 10.1 %collective-permute-start.18 = (bf16[64,896]{1,0:T(8,128)(2,1)S(1)}, bf16[64,896]{1,0:T(8,128)(2,1)S(1)}, u32[]{:S(2)}, u32[]{:S(2)}) collective-permute-start(bf16[64,896]{1,0:T(8,128)(2,1)S(1)} %get-tuple-element.39.refs_1_), channel_id=1, source_target_pairs={{0,64},{64,128},{128,192},{192,0},{1,65},{65,129},{129,193},{193,1... | collective-permute-start | bytes 344072 | tf_op jit(solution)/shard_map/ppermute | solution.py:22
  69.2 8.7 %collective-permute-start.25 = (bf16[64,896]{1,0:T(8,128)(2,1)S(1)}, bf16[64,896]{1,0:T(8,128)(2,1)S(1)}, u32[]{:S(2)}, u32[]{:S(2)}) collective-permute-start(bf16[64,896]{1,0:T(8,128)(2,1)S(1)} %hidden.1.refs_1_), channel_id=1, source_target_pairs={{0,192},{64,0},{128,64},{192,128},{1,193},{65,1},{129,65},{193,129... | collective-permute-start | bytes 344072 | tf_op jit(solution)/shard_map/ppermute | solution.py:22
  70.4 7.5 %collective-permute-start.24 = (bf16[64,896]{1,0:T(8,128)(2,1)S(1)}, bf16[64,896]{1,0:T(8,128)(2,1)S(1)}, u32[]{:S(2)}, u32[]{:S(2)}) collective-permute-start(bf16[64,896]{1,0:T(8,128)(2,1)S(1)} %hidden.1.refs_1_), channel_id=1, source_target_pairs={{0,128},{64,192},{128,0},{192,64},{1,129},{65,193},{129,1},{193,65... | collective-permute-start | bytes 344072 | tf_op jit(solution)/shard_map/ppermute | solution.py:22
  70.9 7.1 %collective-permute-start.23 = (bf16[64,896]{1,0:T(8,128)(2,1)S(1)}, bf16[64,896]{1,0:T(8,128)(2,1)S(1)}, u32[]{:S(2)}, u32[]{:S(2)}) collective-permute-start(bf16[64,896]{1,0:T(8,128)(2,1)S(1)} %hidden.1.refs_1_), channel_id=1, source_target_pairs={{0,64},{64,128},{128,192},{192,0},{1,65},{65,129},{129,193},{193,1... | collective-permute-start | bytes 344072 | tf_op jit(solution)/shard_map/ppermute | solution.py:22
  80.5 3.8 %collective-permute-start.26 = (bf16[128,2048]{1,0:T(8,128)(2,1)S(1)}, bf16[128,2048]{1,0:T(8,128)(2,1)S(1)}, u32[]{:S(2)}, u32[]{:S(2)}) collective-permute-start(bf16[128,2048]{1,0:T(8,128)(2,1)S(1)} %get-tuple-element.45), channel_id=1, source_target_pairs={{0,1},{1,0},{2,3},{3,2},{4,5},{5,4},{6,7},{7,6},{8,9},{9,8},{10,11... | collective-permute-start | bytes 1572872 | tf_op jit(solution)/shard_map/ppermute | solution.py:18
  82.8 3.4 %collective-permute-start.21 = (bf16[128,2048]{1,0:T(8,128)(2,1)S(1)}, bf16[128,2048]{1,0:T(8,128)(2,1)S(1)}, u32[]{:S(2)}, u32[]{:S(2)}) collective-permute-start(bf16[128,2048]{1,0:T(8,128)(2,1)S(1)} %get-tuple-element.41.refs_6_), channel_id=1, source_target_pairs={{0,1},{1,0},{2,3},{3,2},{4,5},{5,4},{6,7},{7,6},{8,9},{9,8},{10,11... | collective-permute-start | bytes 1572872 | tf_op jit(solution)/shard_map/ppermute | solution.py:18
  84.4 6.4 %collective-permute-start.28 = (bf16[48,2048]{1,0:T(8,128)(2,1)S(1)}, bf16[48,2048]{1,0:T(8,128)(2,1)S(1)}, u32[]{:S(2)}, u32[]{:S(2)}) collective-permute-start(bf16[48,2048]{1,0:T(8,128)(2,1)S(1)} %get-tuple-element.48), channel_id=1, source_target_pairs={{0,2},{2,0},{1,3},{3,1},{4,6},{6,4},{5,7},{7,5},{8,10},{10,8},{9,1... | collective-permute-start | bytes 589832 | tf_op jit(solution)/shard_map/ppermute | solution.py:18
  85.2 12.7 %collective-permute-start.27 = (bf16[80,2048]{1,0:T(8,128)(2,1)S(1)}, bf16[80,2048]{1,0:T(8,128)(2,1)S(1)}, u32[]{:S(2)}, u32[]{:S(2)}) collective-permute-start(bf16[80,2048]{1,0:T(8,128)(2,1)S(1)} %get-tuple-element.46), channel_id=1, source_target_pairs={{0,2},{2,0},{1,3},{3,1},{4,6},{6,4},{5,7},{7,5},{8,10},{10,8},{9,1... | collective-permute-start | bytes 983048 | tf_op jit(solution)/shard_map/ppermute | solution.py:18
  90.9 8.2 %collective-permute-start.29 = (bf16[48,2048]{1,0:T(8,128)(2,1)S(1)}, bf16[48,2048]{1,0:T(8,128)(2,1)S(1)}, u32[]{:S(2)}, u32[]{:S(2)}) collective-permute-start(bf16[48,2048]{1,0:T(8,128)(2,1)S(1)} %sum_near.3), channel_id=1, source_target_pairs={{0,20},{1,13},{4,24},{5,17},{8,28},{9,21},{12,0},{13,25},{16,4},{1... | collective-permute-start | bytes 589832 | tf_op jit(solution)/shard_map/ppermute | solution.py:30
  97.9 6.5 %collective-permute-start.30 = (bf16[32,2048]{1,0:T(8,128)(2,1)S(1)}, bf16[32,2048]{1,0:T(8,128)(2,1)S(1)}, u32[]{:S(2)}, u32[]{:S(2)}) collective-permute-start(bf16[32,2048]{1,0:T(8,128)(2,1)S(1)} %get-tuple-element.49), channel_id=1, source_target_pairs={{0,24},{1,9},{4,28},{5,13},{8,0},{9,17},{12,4},{13,21},{16,8},{17,... | collective-permute-start | bytes 393224 | tf_op jit(solution)/shard_map/ppermute | solution.py:30
  99.1 6.8 %collective-permute-start.31 = (bf16[32,2048]{1,0:T(8,128)(2,1)S(1)}, bf16[32,2048]{1,0:T(8,128)(2,1)S(1)}, u32[]{:S(2)}, u32[]{:S(2)}) collective-permute-start(bf16[32,2048]{1,0:T(8,128)(2,1)S(1)} %relay.1), channel_id=1, source_target_pairs={{0,28},{1,5},{4,0},{5,9},{8,4},{9,13},{12,8},{13,17},{16,12},{17,2... | collective-permute-start | bytes 393224 | tf_op jit(solution)/shard_map/ppermute | solution.py:30
  106.0 3.9 %collective-permute-start.32 = (f32[16,2048]{1,0:T(8,128)S(1)}, f32[16,2048]{1,0:T(8,128)S(1)}, u32[]{:S(2)}, u32[]{:S(2)}) collective-permute-start(f32[16,2048]{1,0:T(8,128)S(1)} %get-tuple-element.52), channel_id=1, source_target_pairs={{0,1},{1,0},{2,3},{3,2},{4,5},{5,4},{6,7},{7,6},{8,9},{9,8},{10,11... | collective-permute-start | bytes 393224 | tf_op jit(solution)/shard_map/ppermute | solution.py:18
  (10 other events, 76.6 us)

commit v4 on v3

--- a/solution.py
+++ b/solution.py
@@ -89,20 +89,20 @@
     return call("joined", body, [(shape, BF16)], parts, later=later)[0]
 
 
-def gate_up(me, pieces, gate, gate_scale, up, up_scale, later=()):
+def gate_up(me, pieces, gate, up, scale, later=()):
     depth, width = gate.shape
     count = 2 * width // WIDE
 
     def body(numbers, ins, outs, scratch):
         features, held = scratch
-        quants, scales = ins[-2:], numbers[1:]
+        quants, scale = ins[-2:], numbers[1]
 
         def fill(j):
             for side in range(2):
                 for i in range(depth // BLOCK):
                     rows = slice(i * BLOCK, (i + 1) * BLOCK)
                     block = quants[side][rows, j * BLOCK : (j + 1) * BLOCK].astype(F32)
-                    block = (block * scales[side][j, i]).astype(BF16)
+                    block = (block * scale[side * count + j, i]).astype(BF16)
                     held[j % 2, rows, side * BLOCK : (side + 1) * BLOCK] = block
 
         row = 0
@@ -125,7 +125,7 @@
         body,
         [((64, 2 * width), BF16)] * 4,
         [*pieces, gate, up],
-        scalars=[me, gate_scale.T, up_scale.T],
+        scalars=[me, scale],
         later=later,
         scratch=[pltpu.VMEM((256, depth), BF16), pltpu.VMEM((2, depth, WIDE), BF16)],
         limit=LIMIT,
@@ -254,7 +254,7 @@
 
 def local(tokens, gate_quant, gate_scale, up_quant, up_scale, down_quant, down_scale):
     me = lax.axis_index("x").astype(jnp.int32).reshape(1)
-    both = (gate_quant, gate_scale, up_quant, up_scale)
+    both = (gate_quant, up_quant, jnp.concatenate([gate_scale.T, up_scale.T]))
     last_weight = down_weight(down_quant, down_scale)
 
     chip = jnp.concatenate([tokens, swap(tokens, "core")])
@@ -265,12 +265,12 @@
     b1, b2 = swap(a1, "core"), swap(a2, "core")
 
     outs_a = gate_up(me, [a1, a2, b1, b2], *both)
-    parts_a = [shift_x(outs_a[k], k) for k in (2, 1, 3)]
+    parts_a = [shift_x(outs_a[k], k) for k in (1, 3, 2)]
     c1, c2 = joined([c1], later=[outs_a[0]]), joined([c2], later=[outs_a[0]])
     outs_c = gate_up(me, [c1, c2, swap(c1, "core"), swap(c2, "core")], *both)
     total_a, sent_a = sum_x(outs_a, parts_a, later=[outs_c[0]])
     other_a = swap(sent_a, "yh")
-    parts_c = [shift_x(outs_c[k], k) for k in (2, 1, 3)]
+    parts_c = [shift_x(outs_c[k], k) for k in (1, 3, 2)]
     hidden_a, total_c, sent_c = hidden_and_sum(total_a, other_a, outs_c, parts_c)
     gathered_a = spread_x(hidden_a)
     hidden_c = hidden_of(total_c, swap(sent_c, "yh"))

time: 111 us -> 109 us (0.982)
  waiting for transfers between devices: 35.9 us -> 33.2 us
  starting transfers between devices: 49.7 us -> 51.1 us
  local copies, waits for them, and re-layouts: 8.48 us -> 7.1 us
    ppermute x14, waiting for transfers between devices: 19.2 us -> 16.4 us  [swap(): return lax.ppermute(value, axis, [(0, 1), (1, 0)])]
    unnamed x22 -> x16, local copies, waits for them, and re-layouts: 8.46 us -> 7.07 us
  transfers between devices with their start and end apart: 33 -> 33, of which waited for: 15 -> 15; matrix products, arithmetic and copies ran while one was open for 1% -> 2% of each run, Pallas kernels for 11% -> 12%
where the time goes in v4:
time: 109 us
  starting transfers between devices  51.1 us (47%)
  waiting for transfers between devices  33.2 us (30%)
  Pallas kernels  15.5 us (14%)
  local copies, waits for them, and re-layouts  7.1 us (7%)
  other arithmetic  1.36 us (1%)
    ppermute x14, starting transfers between devices, swap(): return lax.ppermute(value, axis, [(0, 1), (1, 0)])  23.5 us
    ppermute x14, waiting for transfers between devices, swap(): return lax.ppermute(value, axis, [(0, 1), (1, 0)])  16.4 us
    pallas_call x15, Pallas kernels, call(): pl.pallas_call(kernel, in_specs=[pl.BlockSpec(memory_space=pltpu.SMEM)] *...  15.5 us
    ppermute x7, starting transfers between devices, shift_z(): return lax.ppermute(value, ('z', 'core'), pairs)  14.5 us
    ppermute x12, starting transfers between devices, shift_x(): return lax.ppermute(value, 'x', [(i, (i + by) % 4) for i in range(4)])  13.1 us
    ppermute x7, waiting for transfers between devices, shift_z(): return lax.ppermute(value, ('z', 'core'), pairs)  9.39 us
    ppermute x12, waiting for transfers between devices, shift_x(): return lax.ppermute(value, 'x', [(i, (i + by) % 4) for i in range(4)])  7.38 us
    unnamed x16, local copies, waits for them, and re-layouts  7.07 us
  transfers between devices with their start and end apart: 33, of which 15 were waited for; matrix products, arithmetic and copies ran while one was open for 2% of the time, Pallas kernels for 12%

profile of v4, /device:TPU:1, one launch (start us, length us, event | category | flops | bytes accessed | tf_op | source)
XLA Modules:
  0.0 108.5 jit_solution(12450432745707501371)
XLA Ops:
  0.0 3.2 %collective-permute-start = (bf16[16,2048]{1,0:T(8,128)(2,1)}, bf16[16,2048]{1,0:T(8,128)(2,1)S(1)}, u32[]{:S(2)}, u32[]{:S(2)}) collective-permute-start(bf16[16,2048]{1,0:T(8,128)(2,1)} %param.7), channel_id=1, source_target_pairs={{0,1},{1,0},{2,3},{3,2},{4,5},{5,4},{6,7},{7,6},{8,9},{9,8},{10,11... | collective-permute-start | bytes 196616 | tf_op jit(solution)/shard_map/ppermute | solution.py:18
  4.4 4.3 %collective-permute-start.3 = (bf16[32,2048]{1,0:T(8,128)(2,1)S(1)}, bf16[32,2048]{1,0:T(8,128)(2,1)S(1)}, u32[]{:S(2)}, u32[]{:S(2)}) collective-permute-start(bf16[32,2048]{1,0:T(8,128)(2,1)S(1)} %constant_dynamic-update-slice_fusion), channel_id=1, source_target_pairs={{0,8},{1,25},{4,12},{5,29},{8,16},{9,1},{12,20},{13,5},{16,24},{17... | collective-permute-start | bytes 393224 | tf_op jit(solution)/shard_map/ppermute | solution.py:30
  9.6 3.9 %collective-permute-start.4 = (bf16[32,2048]{1,0:T(8,128)(2,1)S(1)}, bf16[32,2048]{1,0:T(8,128)(2,1)S(1)}, u32[]{:S(2)}, u32[]{:S(2)}) collective-permute-start(bf16[32,2048]{1,0:T(8,128)(2,1)S(1)} %constant_dynamic-update-slice_fusion), channel_id=1, source_target_pairs={{0,12},{1,21},{4,16},{5,25},{8,20},{9,29},{12,24},{13,1},{16,28},{... | collective-permute-start | bytes 393224 | tf_op jit(solution)/shard_map/ppermute | solution.py:30
  15.0 4.1 %collective-permute-done.4 = bf16[32,2048]{1,0:T(8,128)(2,1)S(1)} collective-permute-done((bf16[32,2048]{1,0:T(8,128)(2,1)S(1)}, bf16[32,2048]{1,0:T(8,128)(2,1)S(1)}, u32[]{:S(2)}, u32[]{:S(2)}) %collective-permute-start.4) | collective-permute-done | bytes 131104 | tf_op jit(solution)/shard_map/ppermute | solution.py:30
  20.4 3.5 %collective-permute-start.7 = (bf16[80,2048]{1,0:T(8,128)(2,1)S(1)}, bf16[80,2048]{1,0:T(8,128)(2,1)S(1)}, u32[]{:S(2)}, u32[]{:S(2)}) collective-permute-start(bf16[80,2048]{1,0:T(8,128)(2,1)S(1)} %constant_dynamic-update-slice_fusion.4.refs_3_), channel_id=1, source_target_pairs={{0,1},{1,0},{2,3},{3,2},{4,5},{5,4},{6,7},{7,6},{8,9},{9,8},{10,11... | collective-permute-start | bytes 983048 | tf_op jit(solution)/shard_map/ppermute | solution.py:18
  25.5 2.0 %copy-done = bf16[2048,896]{1,0:T(8,128)(2,1)S(1)} copy-done((bf16[2048,896]{1,0:T(8,128)(2,1)S(1)}, bf16[2048,896]{1,0:T(8,128)(2,1)}, u32[]{:S(2)}) %copy-start) | copy-done | bytes 3670040
  27.6 2.0 %copy-done.2 = bf16[2048,896]{1,0:T(8,128)(2,1)S(1)} copy-done((bf16[2048,896]{1,0:T(8,128)(2,1)S(1)}, bf16[2048,896]{1,0:T(8,128)(2,1)}, u32[]{:S(2)}) %copy-start.2) | copy-done | bytes 3670040
  29.6 4.0 %gate_up.2 = (bf16[64,1792]{1,0:T(8,128)(2,1)S(1)}, bf16[64,1792]{1,0:T(8,128)(2,1)S(1)}, bf16[64,1792]{1,0:T(8,128)(2,1)S(1)}, bf16[64,1792]{1,0:T(8,128)(2,1)S(1)}) custom-call(s32[1]{0:T(128)} %bitcast.refs_0_, f32[14,16]{1,0:T(8,128)S(1)} %pad_maximum_fusion.refs_1_, bf16[48,2048]{1,0:T(8,128)(2,1)S(1)} %constant_dynamic-update-slice_fusion.2.refs_2_, ...), custom_call_target="tpu_custom_call" | custom-call | flops 1024 | bytes 1024 | tf_op jit(solution)/shard_map/gate_up/pallas_call | solution.py:45
  35.3 1.5 %collective-permute-start.15 = (bf16[64,1792]{1,0:T(8,128)(2,1)S(1)}, bf16[64,1792]{1,0:T(8,128)(2,1)S(1)}, u32[]{:S(2)}, u32[]{:S(2)}) collective-permute-start(bf16[64,1792]{1,0:T(8,128)(2,1)S(1)} %get-tuple-element.35), channel_id=1, source_target_pairs={{0,192},{64,0},{128,64},{192,128},{1,193},{65,1},{129,65},{193,129... | collective-permute-start | bytes 688136 | tf_op jit(solution)/shard_map/ppermute | solution.py:22
  36.8 1.5 %collective-permute-start.16 = (bf16[64,1792]{1,0:T(8,128)(2,1)S(1)}, bf16[64,1792]{1,0:T(8,128)(2,1)S(1)}, u32[]{:S(2)}, u32[]{:S(2)}) collective-permute-start(bf16[64,1792]{1,0:T(8,128)(2,1)S(1)} %get-tuple-element.36), channel_id=1, source_target_pairs={{0,128},{64,192},{128,0},{192,64},{1,129},{65,193},{129,1},{193,65... | collective-permute-start | bytes 688136 | tf_op jit(solution)/shard_map/ppermute | solution.py:22
  40.7 4.0 %gate_up.3 = (bf16[64,1792]{1,0:T(8,128)(2,1)S(1)}, bf16[64,1792]{1,0:T(8,128)(2,1)S(1)}, bf16[64,1792]{1,0:T(8,128)(2,1)S(1)}, bf16[64,1792]{1,0:T(8,128)(2,1)S(1)}) custom-call(s32[1]{0:T(128)} %bitcast.refs_0_, f32[14,16]{1,0:T(8,128)S(1)} %pad_maximum_fusion.refs_1_, bf16[48,2048]{1,0:T(8,128)(2,1)S(1)} %joined.2.refs_2_, ...), custom_call_target="tpu_custom_call" | custom-call | flops 1024 | bytes 1024 | tf_op jit(solution)/shard_map/gate_up/pallas_call | solution.py:45
  45.1 2.4 %collective-permute-start.12 = (bf16[64,1792]{1,0:T(8,128)(2,1)S(1)}, bf16[64,1792]{1,0:T(8,128)(2,1)S(1)}, u32[]{:S(2)}, u32[]{:S(2)}) collective-permute-start(bf16[64,1792]{1,0:T(8,128)(2,1)S(1)} %get-tuple-element.32), channel_id=1, source_target_pairs={{0,192},{64,0},{128,64},{192,128},{1,193},{65,1},{129,65},{193,129... | collective-permute-start | bytes 688136 | tf_op jit(solution)/shard_map/ppermute | solution.py:22
  48.4 3.0 %collective-permute-start.17 = (bf16[64,1792]{1,0:T(8,128)(2,1)S(1)}, bf16[64,1792]{1,0:T(8,128)(2,1)S(1)}, u32[]{:S(2)}, u32[]{:S(2)}) collective-permute-start(bf16[64,1792]{1,0:T(8,128)(2,1)S(1)} %get-tuple-element.38), channel_id=1, source_target_pairs={{0,32},{32,0},{1,33},{33,1},{2,34},{34,2},{3,35},{35,3},{4,36},{36... | collective-permute-start | bytes 688136 | tf_op jit(solution)/shard_map/ppermute | solution.py:18
  51.4 2.4 %collective-permute-done.11.refs_1_ = bf16[64,1792]{1,0:T(8,128)(2,1)S(1)} collective-permute-done((bf16[64,1792]{1,0:T(8,128)(2,1)S(1)}, bf16[64,1792]{1,0:T(8,128)(2,1)S(1)}, u32[]{:S(2)}, u32[]{:S(2)}) %collective-permute-start.11) | collective-permute-done | bytes 229408 | tf_op jit(solution)/shard_map/ppermute | solution.py:22
  53.8 4.3 %collective-permute-done.13.refs_3_ = bf16[64,1792]{1,0:T(8,128)(2,1)S(1)} collective-permute-done((bf16[64,1792]{1,0:T(8,128)(2,1)S(1)}, bf16[64,1792]{1,0:T(8,128)(2,1)S(1)}, u32[]{:S(2)}, u32[]{:S(2)}) %collective-permute-start.13) | collective-permute-done | bytes 229408 | tf_op jit(solution)/shard_map/ppermute | solution.py:22
  58.3 3.0 %collective-permute-start.22 = (bf16[64,1792]{1,0:T(8,128)(2,1)S(1)}, bf16[64,1792]{1,0:T(8,128)(2,1)S(1)}, u32[]{:S(2)}, u32[]{:S(2)}) collective-permute-start(bf16[64,1792]{1,0:T(8,128)(2,1)S(1)} %get-tuple-element.43), channel_id=1, source_target_pairs={{0,32},{32,0},{1,33},{33,1},{2,34},{34,2},{3,35},{35,3},{4,36},{36... | collective-permute-start | bytes 688136 | tf_op jit(solution)/shard_map/ppermute | solution.py:18
  62.3 1.6 %collective-permute-start.19 = (bf16[64,896]{1,0:T(8,128)(2,1)S(1)}, bf16[64,896]{1,0:T(8,128)(2,1)S(1)}, u32[]{:S(2)}, u32[]{:S(2)}) collective-permute-start(bf16[64,896]{1,0:T(8,128)(2,1)S(1)} %get-tuple-element.39.refs_1_), channel_id=1, source_target_pairs={{0,128},{64,192},{128,0},{192,64},{1,129},{65,193},{129,1},{193,65... | collective-permute-start | bytes 344072 | tf_op jit(solution)/shard_map/ppermute | solution.py:22
  63.9 1.9 %collective-permute-done.22.refs_1_ = bf16[64,1792]{1,0:T(8,128)(2,1)S(1)} collective-permute-done((bf16[64,1792]{1,0:T(8,128)(2,1)S(1)}, bf16[64,1792]{1,0:T(8,128)(2,1)S(1)}, u32[]{:S(2)}, u32[]{:S(2)}) %collective-permute-start.22) | collective-permute-done | bytes 229408 | tf_op jit(solution)/shard_map/ppermute | solution.py:18
  66.8 2.5 %collective-permute-start.24 = (bf16[64,896]{1,0:T(8,128)(2,1)S(1)}, bf16[64,896]{1,0:T(8,128)(2,1)S(1)}, u32[]{:S(2)}, u32[]{:S(2)}) collective-permute-start(bf16[64,896]{1,0:T(8,128)(2,1)S(1)} %hidden.1.refs_1_), channel_id=1, source_target_pairs={{0,128},{64,192},{128,0},{192,64},{1,129},{65,193},{129,1},{193,65... | collective-permute-start | bytes 344072 | tf_op jit(solution)/shard_map/ppermute | solution.py:22
  69.4 2.0 %copy-done.4 = bf16[896,2048]{1,0:T(8,128)(2,1)S(1)} copy-done((bf16[896,2048]{1,0:T(8,128)(2,1)S(1)}, bf16[896,2048]{1,0:T(8,128)(2,1)}, u32[]{:S(2)}) %copy-start.4) | copy-done | bytes 3670040
  71.4 1.6 %down_weight.1.refs_5_ = bf16[896,2048]{1,0:T(8,128)(2,1)S(1)} custom-call(f32[16,7]{1,0:T(8,128)S(1)} %bitcast.4, bf16[896,2048]{1,0:T(8,128)(2,1)S(1)} %copy-done.4), custom_call_target="tpu_custom_call" | custom-call | flops 1024 | bytes 1024 | tf_op jit(solution)/shard_map/down_weight/pallas_call | solution.py:45
  73.1 2.5 %down.2 = (f32[128,2048]{1,0:T(8,128)S(1)}, bf16[128,2048]{1,0:T(8,128)(2,1)S(1)}) custom-call(s32[1]{0:T(128)} %bitcast.refs_0_, bf16[64,896]{1,0:T(8,128)(2,1)S(1)} %get-tuple-element.39.refs_1_, bf16[64,896]{1,0:T(8,128)(2,1)S(1)} %collective-permute-done.18.refs_2_, bf16[64,896]{1,0:T(8,128)(2,1)S(1)} %collective-permute-done.19.refs_3_, ...), custom_call_target="tpu_custom_call" | custom-call | flops 1024 | bytes 1024 | tf_op jit(solution)/shard_map/down/pallas_call | solution.py:45
  75.7 2.5 %down.3 = (f32[128,2048]{1,0:T(8,128)S(1)}, bf16[128,2048]{1,0:T(8,128)(2,1)S(1)}) custom-call(s32[1]{0:T(128)} %bitcast.refs_0_, bf16[64,896]{1,0:T(8,128)(2,1)S(1)} %hidden.1.refs_1_, bf16[64,896]{1,0:T(8,128)(2,1)S(1)} %collective-permute-done.23.refs_2_, bf16[64,896]{1,0:T(8,128)(2,1)S(1)} %collective-permute-done.24.refs_3_, ...), custom_call_target="tpu_custom_call" | custom-call | flops 1024 | bytes 1024 | tf_op jit(solution)/shard_map/down/pallas_call | solution.py:45
  78.2 2.3 %collective-permute-start.26 = (bf16[128,2048]{1,0:T(8,128)(2,1)S(1)}, bf16[128,2048]{1,0:T(8,128)(2,1)S(1)}, u32[]{:S(2)}, u32[]{:S(2)}) collective-permute-start(bf16[128,2048]{1,0:T(8,128)(2,1)S(1)} %get-tuple-element.45), channel_id=1, source_target_pairs={{0,1},{1,0},{2,3},{3,2},{4,5},{5,4},{6,7},{7,6},{8,9},{9,8},{10,11... | collective-permute-start | bytes 1572872 | tf_op jit(solution)/shard_map/ppermute | solution.py:18
  80.6 1.4 %collective-permute-done.26.refs_1_ = bf16[128,2048]{1,0:T(8,128)(2,1)S(1)} collective-permute-done((bf16[128,2048]{1,0:T(8,128)(2,1)S(1)}, bf16[128,2048]{1,0:T(8,128)(2,1)S(1)}, u32[]{:S(2)}, u32[]{:S(2)}) %collective-permute-start.26) | collective-permute-done | bytes 524320 | tf_op jit(solution)/shard_map/ppermute | solution.py:18
  82.2 1.4 %collective-permute-start.28 = (bf16[48,2048]{1,0:T(8,128)(2,1)S(1)}, bf16[48,2048]{1,0:T(8,128)(2,1)S(1)}, u32[]{:S(2)}, u32[]{:S(2)}) collective-permute-start(bf16[48,2048]{1,0:T(8,128)(2,1)S(1)} %get-tuple-element.48), channel_id=1, source_target_pairs={{0,2},{2,0},{1,3},{3,1},{4,6},{6,4},{5,7},{7,5},{8,10},{10,8},{9,1... | collective-permute-start | bytes 589832 | tf_op jit(solution)/shard_map/ppermute | solution.py:18
  83.9 4.6 %collective-permute-done.28.refs_2_ = bf16[48,2048]{1,0:T(8,128)(2,1)S(1)} collective-permute-done((bf16[48,2048]{1,0:T(8,128)(2,1)S(1)}, bf16[48,2048]{1,0:T(8,128)(2,1)S(1)}, u32[]{:S(2)}, u32[]{:S(2)}) %collective-permute-start.28) | collective-permute-done | bytes 196640 | tf_op jit(solution)/shard_map/ppermute | solution.py:18
  89.5 6.1 %collective-permute-done.27.refs_2_ = bf16[80,2048]{1,0:T(8,128)(2,1)S(1)} collective-permute-done((bf16[80,2048]{1,0:T(8,128)(2,1)S(1)}, bf16[80,2048]{1,0:T(8,128)(2,1)S(1)}, u32[]{:S(2)}, u32[]{:S(2)}) %collective-permute-start.27) | collective-permute-done | bytes 327712 | tf_op jit(solution)/shard_map/ppermute | solution.py:18
  95.8 1.7 %collective-permute-done.29.refs_1_ = bf16[48,2048]{1,0:T(8,128)(2,1)S(1)} collective-permute-done((bf16[48,2048]{1,0:T(8,128)(2,1)S(1)}, bf16[48,2048]{1,0:T(8,128)(2,1)S(1)}, u32[]{:S(2)}, u32[]{:S(2)}) %collective-permute-start.29) | collective-permute-done | bytes 196640 | tf_op jit(solution)/shard_map/ppermute | solution.py:30
  97.5 3.6 %collective-permute-start.31 = (bf16[32,2048]{1,0:T(8,128)(2,1)S(1)}, bf16[32,2048]{1,0:T(8,128)(2,1)S(1)}, u32[]{:S(2)}, u32[]{:S(2)}) collective-permute-start(bf16[32,2048]{1,0:T(8,128)(2,1)S(1)} %relay.1), channel_id=1, source_target_pairs={{0,28},{1,5},{4,0},{5,9},{8,4},{9,13},{12,8},{13,17},{16,12},{17,2... | collective-permute-start | bytes 393224 | tf_op jit(solution)/shard_map/ppermute | solution.py:30
  101.1 1.7 %collective-permute-done.30.refs_2_ = bf16[32,2048]{1,0:T(8,128)(2,1)S(1)} collective-permute-done((bf16[32,2048]{1,0:T(8,128)(2,1)S(1)}, bf16[32,2048]{1,0:T(8,128)(2,1)S(1)}, u32[]{:S(2)}, u32[]{:S(2)}) %collective-permute-start.30) | collective-permute-done | bytes 131104 | tf_op jit(solution)/shard_map/ppermute | solution.py:30
  104.1 2.7 %collective-permute-start.32 = (f32[16,2048]{1,0:T(8,128)S(1)}, f32[16,2048]{1,0:T(8,128)S(1)}, u32[]{:S(2)}, u32[]{:S(2)}) collective-permute-start(f32[16,2048]{1,0:T(8,128)S(1)} %get-tuple-element.52), channel_id=1, source_target_pairs={{0,1},{1,0},{2,3},{3,2},{4,5},{5,4},{6,7},{7,6},{8,9},{9,8},{10,11... | collective-permute-start | bytes 393224 | tf_op jit(solution)/shard_map/ppermute | solution.py:18
  (70 shorter events, 18.8 us)
Async XLA Ops:
  0.0 4.4 %collective-permute-start = (bf16[16,2048]{1,0:T(8,128)(2,1)}, bf16[16,2048]{1,0:T(8,128)(2,1)S(1)}, u32[]{:S(2)}, u32[]{:S(2)}) collective-permute-start(bf16[16,2048]{1,0:T(8,128)(2,1)} %param.7), channel_id=1, source_target_pairs={{0,1},{1,0},{2,3},{3,2},{4,5},{5,4},{6,7},{7,6},{8,9},{9,8},{10,11... | collective-permute-start | bytes 196616 | tf_op jit(solution)/shard_map/ppermute | solution.py:18
  4.4 10.6 %collective-permute-start.3 = (bf16[32,2048]{1,0:T(8,128)(2,1)S(1)}, bf16[32,2048]{1,0:T(8,128)(2,1)S(1)}, u32[]{:S(2)}, u32[]{:S(2)}) collective-permute-start(bf16[32,2048]{1,0:T(8,128)(2,1)S(1)} %constant_dynamic-update-slice_fusion), channel_id=1, source_target_pairs={{0,8},{1,25},{4,12},{5,29},{8,16},{9,1},{12,20},{13,5},{16,24},{17... | collective-permute-start | bytes 393224 | tf_op jit(solution)/shard_map/ppermute | solution.py:30
  8.6 10.4 %collective-permute-start.5 = (bf16[16,2048]{1,0:T(8,128)(2,1)}, bf16[16,2048]{1,0:T(8,128)(2,1)S(1)}, u32[]{:S(2)}, u32[]{:S(2)}) collective-permute-start(bf16[16,2048]{1,0:T(8,128)(2,1)} %param.7), channel_id=1, source_target_pairs={{0,16},{1,17},{4,20},{5,21},{8,24},{9,25},{12,28},{13,29},{16,0},{... | collective-permute-start | bytes 196616 | tf_op jit(solution)/shard_map/ppermute | solution.py:30
  9.6 9.4 %collective-permute-start.4 = (bf16[32,2048]{1,0:T(8,128)(2,1)S(1)}, bf16[32,2048]{1,0:T(8,128)(2,1)S(1)}, u32[]{:S(2)}, u32[]{:S(2)}) collective-permute-start(bf16[32,2048]{1,0:T(8,128)(2,1)S(1)} %constant_dynamic-update-slice_fusion), channel_id=1, source_target_pairs={{0,12},{1,21},{4,16},{5,25},{8,20},{9,29},{12,24},{13,1},{16,28},{... | collective-permute-start | bytes 393224 | tf_op jit(solution)/shard_map/ppermute | solution.py:30
  13.6 10.4 %collective-permute-start.1 = (bf16[32,2048]{1,0:T(8,128)(2,1)S(1)}, bf16[32,2048]{1,0:T(8,128)(2,1)S(1)}, u32[]{:S(2)}, u32[]{:S(2)}) collective-permute-start(bf16[32,2048]{1,0:T(8,128)(2,1)S(1)} %constant_dynamic-update-slice_fusion), channel_id=1, source_target_pairs={{0,4},{1,29},{4,8},{5,1},{8,12},{9,5},{12,16},{13,9},{16,20},{17,1... | collective-permute-start | bytes 393224 | tf_op jit(solution)/shard_map/ppermute | solution.py:30
  19.1 14.5 %collective-permute-start.8 = (bf16[80,2048]{1,0:T(8,128)(2,1)S(1)}, bf16[80,2048]{1,0:T(8,128)(2,1)S(1)}, u32[]{:S(2)}, u32[]{:S(2)}) collective-permute-start(bf16[80,2048]{1,0:T(8,128)(2,1)S(1)} %constant_dynamic-update-slice_fusion.4.refs_3_), channel_id=1, source_target_pairs={{0,2},{2,0},{1,3},{3,1},{4,6},{6,4},{5,7},{7,5},{8,10},{10,8},{9,1... | collective-permute-start | bytes 983048 | tf_op jit(solution)/shard_map/ppermute | solution.py:18
  20.4 5.1 %collective-permute-start.7 = (bf16[80,2048]{1,0:T(8,128)(2,1)S(1)}, bf16[80,2048]{1,0:T(8,128)(2,1)S(1)}, u32[]{:S(2)}, u32[]{:S(2)}) collective-permute-start(bf16[80,2048]{1,0:T(8,128)(2,1)S(1)} %constant_dynamic-update-slice_fusion.4.refs_3_), channel_id=1, source_target_pairs={{0,1},{1,0},{2,3},{3,2},{4,5},{5,4},{6,7},{7,6},{8,9},{9,8},{10,11... | collective-permute-start | bytes 983048 | tf_op jit(solution)/shard_map/ppermute | solution.py:18
  24.1 14.2 %collective-permute-start.2 = (bf16[48,2048]{1,0:T(8,128)(2,1)S(1)}, bf16[48,2048]{1,0:T(8,128)(2,1)S(1)}, u32[]{:S(2)}, u32[]{:S(2)}) collective-permute-start(bf16[48,2048]{1,0:T(8,128)(2,1)S(1)} %constant_dynamic-update-slice_fusion.2.refs_2_), channel_id=1, source_target_pairs={{0,2},{2,0},{1,3},{3,1},{4,6},{6,4},{5,7},{7,5},{8,10},{10,8},{9,1... | collective-permute-start | bytes 589832 | tf_op jit(solution)/shard_map/ppermute | solution.py:18
  33.6 7.0 %collective-permute-start.10 = (bf16[80,2048]{1,0:T(8,128)(2,1)S(1)}, bf16[80,2048]{1,0:T(8,128)(2,1)S(1)}, u32[]{:S(2)}, u32[]{:S(2)}) collective-permute-start(bf16[80,2048]{1,0:T(8,128)(2,1)S(1)} %joined.3.refs_3_), channel_id=1, source_target_pairs={{0,1},{1,0},{2,3},{3,2},{4,5},{5,4},{6,7},{7,6},{8,9},{9,8},{10,11... | collective-permute-start | bytes 983048 | tf_op jit(solution)/shard_map/ppermute | solution.py:18
  34.1 13.3 %collective-permute-start.14 = (bf16[64,1792]{1,0:T(8,128)(2,1)S(1)}, bf16[64,1792]{1,0:T(8,128)(2,1)S(1)}, u32[]{:S(2)}, u32[]{:S(2)}) collective-permute-start(bf16[64,1792]{1,0:T(8,128)(2,1)S(1)} %get-tuple-element.34), channel_id=1, source_target_pairs={{0,64},{64,128},{128,192},{192,0},{1,65},{65,129},{129,193},{193,1... | collective-permute-start | bytes 688136 | tf_op jit(solution)/shard_map/ppermute | solution.py:22
  35.3 12.4 %collective-permute-start.15 = (bf16[64,1792]{1,0:T(8,128)(2,1)S(1)}, bf16[64,1792]{1,0:T(8,128)(2,1)S(1)}, u32[]{:S(2)}, u32[]{:S(2)}) collective-permute-start(bf16[64,1792]{1,0:T(8,128)(2,1)S(1)} %get-tuple-element.35), channel_id=1, source_target_pairs={{0,192},{64,0},{128,64},{192,128},{1,193},{65,1},{129,65},{193,129... | collective-permute-start | bytes 688136 | tf_op jit(solution)/shard_map/ppermute | solution.py:22
  36.8 11.5 %collective-permute-start.16 = (bf16[64,1792]{1,0:T(8,128)(2,1)S(1)}, bf16[64,1792]{1,0:T(8,128)(2,1)S(1)}, u32[]{:S(2)}, u32[]{:S(2)}) collective-permute-start(bf16[64,1792]{1,0:T(8,128)(2,1)S(1)} %get-tuple-element.36), channel_id=1, source_target_pairs={{0,128},{64,192},{128,0},{192,64},{1,129},{65,193},{129,1},{193,65... | collective-permute-start | bytes 688136 | tf_op jit(solution)/shard_map/ppermute | solution.py:22
  38.3 2.3 %collective-permute-start.9 = (bf16[48,2048]{1,0:T(8,128)(2,1)S(1)}, bf16[48,2048]{1,0:T(8,128)(2,1)S(1)}, u32[]{:S(2)}, u32[]{:S(2)}) collective-permute-start(bf16[48,2048]{1,0:T(8,128)(2,1)S(1)} %joined.2.refs_2_), channel_id=1, source_target_pairs={{0,1},{1,0},{2,3},{3,2},{4,5},{5,4},{6,7},{7,6},{8,9},{9,8},{10,11... | collective-permute-start | bytes 589832 | tf_op jit(solution)/shard_map/ppermute | solution.py:18
  44.7 9.1 %collective-permute-start.11 = (bf16[64,1792]{1,0:T(8,128)(2,1)S(1)}, bf16[64,1792]{1,0:T(8,128)(2,1)S(1)}, u32[]{:S(2)}, u32[]{:S(2)}) collective-permute-start(bf16[64,1792]{1,0:T(8,128)(2,1)S(1)} %get-tuple-element.31), channel_id=1, source_target_pairs={{0,64},{64,128},{128,192},{192,0},{1,65},{65,129},{129,193},{193,1... | collective-permute-start | bytes 688136 | tf_op jit(solution)/shard_map/ppermute | solution.py:22
  45.1 8.8 %collective-permute-start.12 = (bf16[64,1792]{1,0:T(8,128)(2,1)S(1)}, bf16[64,1792]{1,0:T(8,128)(2,1)S(1)}, u32[]{:S(2)}, u32[]{:S(2)}) collective-permute-start(bf16[64,1792]{1,0:T(8,128)(2,1)S(1)} %get-tuple-element.32), channel_id=1, source_target_pairs={{0,192},{64,0},{128,64},{192,128},{1,193},{65,1},{129,65},{193,129... | collective-permute-start | bytes 688136 | tf_op jit(solution)/shard_map/ppermute | solution.py:22
  47.4 10.7 %collective-permute-start.13 = (bf16[64,1792]{1,0:T(8,128)(2,1)S(1)}, bf16[64,1792]{1,0:T(8,128)(2,1)S(1)}, u32[]{:S(2)}, u32[]{:S(2)}) collective-permute-start(bf16[64,1792]{1,0:T(8,128)(2,1)S(1)} %get-tuple-element.33), channel_id=1, source_target_pairs={{0,128},{64,192},{128,0},{192,64},{1,129},{65,193},{129,1},{193,65... | collective-permute-start | bytes 688136 | tf_op jit(solution)/shard_map/ppermute | solution.py:22
  48.4 9.8 %collective-permute-start.17 = (bf16[64,1792]{1,0:T(8,128)(2,1)S(1)}, bf16[64,1792]{1,0:T(8,128)(2,1)S(1)}, u32[]{:S(2)}, u32[]{:S(2)}) collective-permute-start(bf16[64,1792]{1,0:T(8,128)(2,1)S(1)} %get-tuple-element.38), channel_id=1, source_target_pairs={{0,32},{32,0},{1,33},{33,1},{2,34},{34,2},{3,35},{35,3},{4,36},{36... | collective-permute-start | bytes 688136 | tf_op jit(solution)/shard_map/ppermute | solution.py:18
  58.3 7.5 %collective-permute-start.22 = (bf16[64,1792]{1,0:T(8,128)(2,1)S(1)}, bf16[64,1792]{1,0:T(8,128)(2,1)S(1)}, u32[]{:S(2)}, u32[]{:S(2)}) collective-permute-start(bf16[64,1792]{1,0:T(8,128)(2,1)S(1)} %get-tuple-element.43), channel_id=1, source_target_pairs={{0,32},{32,0},{1,33},{33,1},{2,34},{34,2},{3,35},{35,3},{4,36},{36... | collective-permute-start | bytes 688136 | tf_op jit(solution)/shard_map/ppermute | solution.py:18
  61.3 8.0 %collective-permute-start.20 = (bf16[64,896]{1,0:T(8,128)(2,1)S(1)}, bf16[64,896]{1,0:T(8,128)(2,1)S(1)}, u32[]{:S(2)}, u32[]{:S(2)}) collective-permute-start(bf16[64,896]{1,0:T(8,128)(2,1)S(1)} %get-tuple-element.39.refs_1_), channel_id=1, source_target_pairs={{0,192},{64,0},{128,64},{192,128},{1,193},{65,1},{129,65},{193,129... | collective-permute-start | bytes 344072 | tf_op jit(solution)/shard_map/ppermute | solution.py:22
  62.3 10.7 %collective-permute-start.19 = (bf16[64,896]{1,0:T(8,128)(2,1)S(1)}, bf16[64,896]{1,0:T(8,128)(2,1)S(1)}, u32[]{:S(2)}, u32[]{:S(2)}) collective-permute-start(bf16[64,896]{1,0:T(8,128)(2,1)S(1)} %get-tuple-element.39.refs_1_), channel_id=1, source_target_pairs={{0,128},{64,192},{128,0},{192,64},{1,129},{65,193},{129,1},{193,65... | collective-permute-start | bytes 344072 | tf_op jit(solution)/shard_map/ppermute | solution.py:22
  63.9 9.1 %collective-permute-start.18 = (bf16[64,896]{1,0:T(8,128)(2,1)S(1)}, bf16[64,896]{1,0:T(8,128)(2,1)S(1)}, u32[]{:S(2)}, u32[]{:S(2)}) collective-permute-start(bf16[64,896]{1,0:T(8,128)(2,1)S(1)} %get-tuple-element.39.refs_1_), channel_id=1, source_target_pairs={{0,64},{64,128},{128,192},{192,0},{1,65},{65,129},{129,193},{193,1... | collective-permute-start | bytes 344072 | tf_op jit(solution)/shard_map/ppermute | solution.py:22
  66.0 9.6 %collective-permute-start.25 = (bf16[64,896]{1,0:T(8,128)(2,1)S(1)}, bf16[64,896]{1,0:T(8,128)(2,1)S(1)}, u32[]{:S(2)}, u32[]{:S(2)}) collective-permute-start(bf16[64,896]{1,0:T(8,128)(2,1)S(1)} %hidden.1.refs_1_), channel_id=1, source_target_pairs={{0,192},{64,0},{128,64},{192,128},{1,193},{65,1},{129,65},{193,129... | collective-permute-start | bytes 344072 | tf_op jit(solution)/shard_map/ppermute | solution.py:22
  66.8 8.8 %collective-permute-start.24 = (bf16[64,896]{1,0:T(8,128)(2,1)S(1)}, bf16[64,896]{1,0:T(8,128)(2,1)S(1)}, u32[]{:S(2)}, u32[]{:S(2)}) collective-permute-start(bf16[64,896]{1,0:T(8,128)(2,1)S(1)} %hidden.1.refs_1_), channel_id=1, source_target_pairs={{0,128},{64,192},{128,0},{192,64},{1,129},{65,193},{129,1},{193,65... | collective-permute-start | bytes 344072 | tf_op jit(solution)/shard_map/ppermute | solution.py:22
  69.3 6.4 %collective-permute-start.23 = (bf16[64,896]{1,0:T(8,128)(2,1)S(1)}, bf16[64,896]{1,0:T(8,128)(2,1)S(1)}, u32[]{:S(2)}, u32[]{:S(2)}) collective-permute-start(bf16[64,896]{1,0:T(8,128)(2,1)S(1)} %hidden.1.refs_1_), channel_id=1, source_target_pairs={{0,64},{64,128},{128,192},{192,0},{1,65},{65,129},{129,193},{193,1... | collective-permute-start | bytes 344072 | tf_op jit(solution)/shard_map/ppermute | solution.py:22
  78.2 3.8 %collective-permute-start.26 = (bf16[128,2048]{1,0:T(8,128)(2,1)S(1)}, bf16[128,2048]{1,0:T(8,128)(2,1)S(1)}, u32[]{:S(2)}, u32[]{:S(2)}) collective-permute-start(bf16[128,2048]{1,0:T(8,128)(2,1)S(1)} %get-tuple-element.45), channel_id=1, source_target_pairs={{0,1},{1,0},{2,3},{3,2},{4,5},{5,4},{6,7},{7,6},{8,9},{9,8},{10,11... | collective-permute-start | bytes 1572872 | tf_op jit(solution)/shard_map/ppermute | solution.py:18
  80.5 3.4 %collective-permute-start.21 = (bf16[128,2048]{1,0:T(8,128)(2,1)S(1)}, bf16[128,2048]{1,0:T(8,128)(2,1)S(1)}, u32[]{:S(2)}, u32[]{:S(2)}) collective-permute-start(bf16[128,2048]{1,0:T(8,128)(2,1)S(1)} %get-tuple-element.41.refs_6_), channel_id=1, source_target_pairs={{0,1},{1,0},{2,3},{3,2},{4,5},{5,4},{6,7},{7,6},{8,9},{9,8},{10,11... | collective-permute-start | bytes 1572872 | tf_op jit(solution)/shard_map/ppermute | solution.py:18
  82.2 6.4 %collective-permute-start.28 = (bf16[48,2048]{1,0:T(8,128)(2,1)S(1)}, bf16[48,2048]{1,0:T(8,128)(2,1)S(1)}, u32[]{:S(2)}, u32[]{:S(2)}) collective-permute-start(bf16[48,2048]{1,0:T(8,128)(2,1)S(1)} %get-tuple-element.48), channel_id=1, source_target_pairs={{0,2},{2,0},{1,3},{3,1},{4,6},{6,4},{5,7},{7,5},{8,10},{10,8},{9,1... | collective-permute-start | bytes 589832 | tf_op jit(solution)/shard_map/ppermute | solution.py:18
  83.6 12.0 %collective-permute-start.27 = (bf16[80,2048]{1,0:T(8,128)(2,1)S(1)}, bf16[80,2048]{1,0:T(8,128)(2,1)S(1)}, u32[]{:S(2)}, u32[]{:S(2)}) collective-permute-start(bf16[80,2048]{1,0:T(8,128)(2,1)S(1)} %get-tuple-element.46), channel_id=1, source_target_pairs={{0,2},{2,0},{1,3},{3,1},{4,6},{6,4},{5,7},{7,5},{8,10},{10,8},{9,1... | collective-permute-start | bytes 983048 | tf_op jit(solution)/shard_map/ppermute | solution.py:18
  88.7 8.8 %collective-permute-start.29 = (bf16[48,2048]{1,0:T(8,128)(2,1)S(1)}, bf16[48,2048]{1,0:T(8,128)(2,1)S(1)}, u32[]{:S(2)}, u32[]{:S(2)}) collective-permute-start(bf16[48,2048]{1,0:T(8,128)(2,1)S(1)} %sum_near.3), channel_id=1, source_target_pairs={{0,20},{1,13},{4,24},{5,17},{8,28},{9,21},{12,0},{13,25},{16,4},{1... | collective-permute-start | bytes 589832 | tf_op jit(solution)/shard_map/ppermute | solution.py:30
  95.7 7.1 %collective-permute-start.30 = (bf16[32,2048]{1,0:T(8,128)(2,1)S(1)}, bf16[32,2048]{1,0:T(8,128)(2,1)S(1)}, u32[]{:S(2)}, u32[]{:S(2)}) collective-permute-start(bf16[32,2048]{1,0:T(8,128)(2,1)S(1)} %get-tuple-element.49), channel_id=1, source_target_pairs={{0,24},{1,9},{4,28},{5,13},{8,0},{9,17},{12,4},{13,21},{16,8},{17,... | collective-permute-start | bytes 393224 | tf_op jit(solution)/shard_map/ppermute | solution.py:30
  97.5 6.6 %collective-permute-start.31 = (bf16[32,2048]{1,0:T(8,128)(2,1)S(1)}, bf16[32,2048]{1,0:T(8,128)(2,1)S(1)}, u32[]{:S(2)}, u32[]{:S(2)}) collective-permute-start(bf16[32,2048]{1,0:T(8,128)(2,1)S(1)} %relay.1), channel_id=1, source_target_pairs={{0,28},{1,5},{4,0},{5,9},{8,4},{9,13},{12,8},{13,17},{16,12},{17,2... | collective-permute-start | bytes 393224 | tf_op jit(solution)/shard_map/ppermute | solution.py:30
  104.1 3.7 %collective-permute-start.32 = (f32[16,2048]{1,0:T(8,128)S(1)}, f32[16,2048]{1,0:T(8,128)S(1)}, u32[]{:S(2)}, u32[]{:S(2)}) collective-permute-start(f32[16,2048]{1,0:T(8,128)S(1)} %get-tuple-element.52), channel_id=1, source_target_pairs={{0,1},{1,0},{2,3},{3,2},{4,5},{5,4},{6,7},{7,6},{8,9},{9,8},{10,11... | collective-permute-start | bytes 393224 | tf_op jit(solution)/shard_map/ppermute | solution.py:18
  (7 other events, 60.8 us)

commit v5 on v4

--- a/solution.py
+++ b/solution.py
@@ -177,7 +177,7 @@
     return call("hidden", body, [((rows, width // 2), BF16)], [own, other], later=later)[0]
 
 
-def down(me, pieces, weight, later=()):
+def down(me, pieces, weight, cut=128, later=()):
     depth, width = weight.shape
 
     def body(numbers, ins, outs, scratch):
@@ -190,7 +190,9 @@
             at = columns(j, WIDE)
             total = jnp.dot(hidden[...], ins[4][:, at], preferred_element_type=F32)
             outs[0][:, at] = total[:128]
-            outs[1][:, at] = total[128:].astype(BF16)
+            outs[1][:, at] = total[128 : 128 + cut].astype(BF16)
+            if cut < 128:
+                outs[2][:, at] = total[128 + cut :].astype(BF16)
             return carry
 
         lax.fori_loop(0, width // WIDE, step, 0)
@@ -198,7 +200,8 @@
     return call(
         "down",
         body,
-        [((128, width), F32), ((128, width), BF16)],
+        [((128, width), F32), ((cut, width), BF16)]
+        + [((128 - cut, width), BF16)] * (cut < 128),
         [*pieces, weight],
         scalars=[me],
         later=later,
@@ -206,14 +209,12 @@
     )
 
 
-def sum_far(near, got):
-    def body(_, ins, outs, __):
-        total = (ins[0][...] + ins[1][...].astype(F32)).astype(BF16)
-        outs[0][...] = total[:80]
-        outs[1][...] = total[80:]
-
-    width = near.shape[1]
-    return call("sum_far", body, [((80, width), BF16), ((48, width), BF16)], [near, got])
+def sum_far(near, got, low):
+    def body(_, ins, outs, __):
+        rows = slice(low, low + ins[1].shape[0])
+        outs[0][...] = (ins[0][rows] + ins[1][...].astype(F32)).astype(BF16)
+
+    return call("sum_far", body, [(got.shape, BF16)], [near, got])[0]
 
 
 def sum_near(near, got, other, low, parts):
@@ -276,9 +277,10 @@
     hidden_c = hidden_of(total_c, swap(sent_c, "yh"))
     gathered_c = spread_x(hidden_c)
     near_a, far_a = down(me, gathered_a, last_weight)
-    near_c, far_c = down(me, gathered_c, last_weight, later=[far_a])
-
-    sent2, sent1 = sum_far(near_c, swap(far_c, "core"))
+    near_c, far2, far1 = down(me, gathered_c, last_weight, cut=80, later=[far_a])
+
+    sent1 = sum_far(near_c, swap(far1, "core"), 80)
+    sent2 = sum_far(near_c, swap(far2, "core"), 0)
     got = swap(far_a, "core")
     other1, other2 = swap(sent1, "yl"), swap(sent2, "yl")
     third = shift_z(sum_near(near_a, got, other1, 80, [(48, BF16)])[0], -3)

time: 109 us -> 109 us (level)
    ppermute x14 -> x15, waiting for transfers between devices: 16.4 us -> 16.5 us  [swap(): return lax.ppermute(value, axis, [(0, 1), (1, 0)])]
    pallas_call x15 -> x16, Pallas kernels: 15.5 us -> 15.5 us  [call(): pl.pallas_call(kernel, in_specs=[pl.BlockSpec(memory_space=pltpu.SMEM)] *...]
    ppermute x14 -> x15, starting transfers between devices: 23.5 us -> 23.5 us  [swap(): return lax.ppermute(value, axis, [(0, 1), (1, 0)])]
  transfers between devices with their start and end apart: 33 -> 34, of which waited for: 15 -> 15; matrix products, arithmetic and copies ran while one was open for 2% -> 2% of each run, Pallas kernels for 12% -> 14%
where the time goes in v5:
time: 109 us; the launch traced here: 108 us
  starting transfers between devices  51.1 us (47%)
  waiting for transfers between devices  33.1 us (30%)
  Pallas kernels  15.5 us (14%)
  local copies, waits for them, and re-layouts  7.1 us (7%)
  other arithmetic  1.36 us (1%)
    ppermute x15, starting transfers between devices, swap(): return lax.ppermute(value, axis, [(0, 1), (1, 0)])  23.5 us
    ppermute x15, waiting for transfers between devices, swap(): return lax.ppermute(value, axis, [(0, 1), (1, 0)])  16.5 us
    pallas_call x16, Pallas kernels, call(): pl.pallas_call(kernel, in_specs=[pl.BlockSpec(memory_space=pltpu.SMEM)] *...  15.5 us
    ppermute x7, starting transfers between devices, shift_z(): return lax.ppermute(value, ('z', 'core'), pairs)  14.5 us
    ppermute x12, starting transfers between devices, shift_x(): return lax.ppermute(value, 'x', [(i, (i + by) % 4) for i in range(4)])  13.1 us
    ppermute x7, waiting for transfers between devices, shift_z(): return lax.ppermute(value, ('z', 'core'), pairs)  9.25 us
    ppermute x12, waiting for transfers between devices, shift_x(): return lax.ppermute(value, 'x', [(i, (i + by) % 4) for i in range(4)])  7.38 us
    unnamed x16, local copies, waits for them, and re-layouts  7.07 us
  transfers between devices with their start and end apart: 34, of which 15 were waited for; matrix products, arithmetic and copies ran while one was open for 2% of the time, Pallas kernels for 14%

profile of v5, /device:TPU:1, one launch (start us, length us, event | category | flops | bytes accessed | tf_op | source)
XLA Modules:
  0.0 108.4 jit_solution(1490486240425288757)
XLA Ops:
  0.0 3.2 %collective-permute-start = (bf16[16,2048]{1,0:T(8,128)(2,1)}, bf16[16,2048]{1,0:T(8,128)(2,1)S(1)}, u32[]{:S(2)}, u32[]{:S(2)}) collective-permute-start(bf16[16,2048]{1,0:T(8,128)(2,1)} %param.7), channel_id=1, source_target_pairs={{0,1},{1,0},{2,3},{3,2},{4,5},{5,4},{6,7},{7,6},{8,9},{9,8},{10,11... | collective-permute-start | bytes 196616 | tf_op jit(solution)/shard_map/ppermute | solution.py:18
  4.4 4.3 %collective-permute-start.3 = (bf16[32,2048]{1,0:T(8,128)(2,1)S(1)}, bf16[32,2048]{1,0:T(8,128)(2,1)S(1)}, u32[]{:S(2)}, u32[]{:S(2)}) collective-permute-start(bf16[32,2048]{1,0:T(8,128)(2,1)S(1)} %constant_dynamic-update-slice_fusion), channel_id=1, source_target_pairs={{0,8},{1,25},{4,12},{5,29},{8,16},{9,1},{12,20},{13,5},{16,24},{17... | collective-permute-start | bytes 393224 | tf_op jit(solution)/shard_map/ppermute | solution.py:30
  9.6 3.9 %collective-permute-start.4 = (bf16[32,2048]{1,0:T(8,128)(2,1)S(1)}, bf16[32,2048]{1,0:T(8,128)(2,1)S(1)}, u32[]{:S(2)}, u32[]{:S(2)}) collective-permute-start(bf16[32,2048]{1,0:T(8,128)(2,1)S(1)} %constant_dynamic-update-slice_fusion), channel_id=1, source_target_pairs={{0,12},{1,21},{4,16},{5,25},{8,20},{9,29},{12,24},{13,1},{16,28},{... | collective-permute-start | bytes 393224 | tf_op jit(solution)/shard_map/ppermute | solution.py:30
  15.0 4.1 %collective-permute-done.4 = bf16[32,2048]{1,0:T(8,128)(2,1)S(1)} collective-permute-done((bf16[32,2048]{1,0:T(8,128)(2,1)S(1)}, bf16[32,2048]{1,0:T(8,128)(2,1)S(1)}, u32[]{:S(2)}, u32[]{:S(2)}) %collective-permute-start.4) | collective-permute-done | bytes 131104 | tf_op jit(solution)/shard_map/ppermute | solution.py:30
  19.1 1.4 %collective-permute-start.8 = (bf16[80,2048]{1,0:T(8,128)(2,1)S(1)}, bf16[80,2048]{1,0:T(8,128)(2,1)S(1)}, u32[]{:S(2)}, u32[]{:S(2)}) collective-permute-start(bf16[80,2048]{1,0:T(8,128)(2,1)S(1)} %constant_dynamic-update-slice_fusion.4.refs_3_), channel_id=1, source_target_pairs={{0,2},{2,0},{1,3},{3,1},{4,6},{6,4},{5,7},{7,5},{8,10},{10,8},{9,1... | collective-permute-start | bytes 983048 | tf_op jit(solution)/shard_map/ppermute | solution.py:18
  20.4 3.5 %collective-permute-start.7 = (bf16[80,2048]{1,0:T(8,128)(2,1)S(1)}, bf16[80,2048]{1,0:T(8,128)(2,1)S(1)}, u32[]{:S(2)}, u32[]{:S(2)}) collective-permute-start(bf16[80,2048]{1,0:T(8,128)(2,1)S(1)} %constant_dynamic-update-slice_fusion.4.refs_3_), channel_id=1, source_target_pairs={{0,1},{1,0},{2,3},{3,2},{4,5},{5,4},{6,7},{7,6},{8,9},{9,8},{10,11... | collective-permute-start | bytes 983048 | tf_op jit(solution)/shard_map/ppermute | solution.py:18
  25.5 2.0 %copy-done = bf16[2048,896]{1,0:T(8,128)(2,1)S(1)} copy-done((bf16[2048,896]{1,0:T(8,128)(2,1)S(1)}, bf16[2048,896]{1,0:T(8,128)(2,1)}, u32[]{:S(2)}) %copy-start) | copy-done | bytes 3670040
  27.6 2.0 %copy-done.2 = bf16[2048,896]{1,0:T(8,128)(2,1)S(1)} copy-done((bf16[2048,896]{1,0:T(8,128)(2,1)S(1)}, bf16[2048,896]{1,0:T(8,128)(2,1)}, u32[]{:S(2)}) %copy-start.2) | copy-done | bytes 3670040
  29.6 4.0 %gate_up.2 = (bf16[64,1792]{1,0:T(8,128)(2,1)S(1)}, bf16[64,1792]{1,0:T(8,128)(2,1)S(1)}, bf16[64,1792]{1,0:T(8,128)(2,1)S(1)}, bf16[64,1792]{1,0:T(8,128)(2,1)S(1)}) custom-call(s32[1]{0:T(128)} %bitcast.refs_0_, f32[14,16]{1,0:T(8,128)S(1)} %pad_maximum_fusion.refs_1_, bf16[48,2048]{1,0:T(8,128)(2,1)S(1)} %constant_dynamic-update-slice_fusion.2.refs_2_, ...), custom_call_target="tpu_custom_call" | custom-call | flops 1024 | bytes 1024 | tf_op jit(solution)/shard_map/gate_up/pallas_call | solution.py:45
  35.3 1.5 %collective-permute-start.15 = (bf16[64,1792]{1,0:T(8,128)(2,1)S(1)}, bf16[64,1792]{1,0:T(8,128)(2,1)S(1)}, u32[]{:S(2)}, u32[]{:S(2)}) collective-permute-start(bf16[64,1792]{1,0:T(8,128)(2,1)S(1)} %get-tuple-element.34), channel_id=1, source_target_pairs={{0,192},{64,0},{128,64},{192,128},{1,193},{65,1},{129,65},{193,129... | collective-permute-start | bytes 688136 | tf_op jit(solution)/shard_map/ppermute | solution.py:22
  36.8 1.5 %collective-permute-start.16 = (bf16[64,1792]{1,0:T(8,128)(2,1)S(1)}, bf16[64,1792]{1,0:T(8,128)(2,1)S(1)}, u32[]{:S(2)}, u32[]{:S(2)}) collective-permute-start(bf16[64,1792]{1,0:T(8,128)(2,1)S(1)} %get-tuple-element.35), channel_id=1, source_target_pairs={{0,128},{64,192},{128,0},{192,64},{1,129},{65,193},{129,1},{193,65... | collective-permute-start | bytes 688136 | tf_op jit(solution)/shard_map/ppermute | solution.py:22
  40.7 4.0 %gate_up.3 = (bf16[64,1792]{1,0:T(8,128)(2,1)S(1)}, bf16[64,1792]{1,0:T(8,128)(2,1)S(1)}, bf16[64,1792]{1,0:T(8,128)(2,1)S(1)}, bf16[64,1792]{1,0:T(8,128)(2,1)S(1)}) custom-call(s32[1]{0:T(128)} %bitcast.refs_0_, f32[14,16]{1,0:T(8,128)S(1)} %pad_maximum_fusion.refs_1_, bf16[48,2048]{1,0:T(8,128)(2,1)S(1)} %joined.2.refs_2_, ...), custom_call_target="tpu_custom_call" | custom-call | flops 1024 | bytes 1024 | tf_op jit(solution)/shard_map/gate_up/pallas_call | solution.py:45
  45.1 2.4 %collective-permute-start.12 = (bf16[64,1792]{1,0:T(8,128)(2,1)S(1)}, bf16[64,1792]{1,0:T(8,128)(2,1)S(1)}, u32[]{:S(2)}, u32[]{:S(2)}) collective-permute-start(bf16[64,1792]{1,0:T(8,128)(2,1)S(1)} %get-tuple-element.31), channel_id=1, source_target_pairs={{0,192},{64,0},{128,64},{192,128},{1,193},{65,1},{129,65},{193,129... | collective-permute-start | bytes 688136 | tf_op jit(solution)/shard_map/ppermute | solution.py:22
  48.4 3.0 %collective-permute-start.17 = (bf16[64,1792]{1,0:T(8,128)(2,1)S(1)}, bf16[64,1792]{1,0:T(8,128)(2,1)S(1)}, u32[]{:S(2)}, u32[]{:S(2)}) collective-permute-start(bf16[64,1792]{1,0:T(8,128)(2,1)S(1)} %get-tuple-element.37), channel_id=1, source_target_pairs={{0,32},{32,0},{1,33},{33,1},{2,34},{34,2},{3,35},{35,3},{4,36},{36... | collective-permute-start | bytes 688136 | tf_op jit(solution)/shard_map/ppermute | solution.py:18
  51.4 2.4 %collective-permute-done.11.refs_1_ = bf16[64,1792]{1,0:T(8,128)(2,1)S(1)} collective-permute-done((bf16[64,1792]{1,0:T(8,128)(2,1)S(1)}, bf16[64,1792]{1,0:T(8,128)(2,1)S(1)}, u32[]{:S(2)}, u32[]{:S(2)}) %collective-permute-start.11) | collective-permute-done | bytes 229408 | tf_op jit(solution)/shard_map/ppermute | solution.py:22
  53.8 4.3 %collective-permute-done.13.refs_3_ = bf16[64,1792]{1,0:T(8,128)(2,1)S(1)} collective-permute-done((bf16[64,1792]{1,0:T(8,128)(2,1)S(1)}, bf16[64,1792]{1,0:T(8,128)(2,1)S(1)}, u32[]{:S(2)}, u32[]{:S(2)}) %collective-permute-start.13) | collective-permute-done | bytes 229408 | tf_op jit(solution)/shard_map/ppermute | solution.py:22
  58.3 3.0 %collective-permute-start.22 = (bf16[64,1792]{1,0:T(8,128)(2,1)S(1)}, bf16[64,1792]{1,0:T(8,128)(2,1)S(1)}, u32[]{:S(2)}, u32[]{:S(2)}) collective-permute-start(bf16[64,1792]{1,0:T(8,128)(2,1)S(1)} %get-tuple-element.42), channel_id=1, source_target_pairs={{0,32},{32,0},{1,33},{33,1},{2,34},{34,2},{3,35},{35,3},{4,36},{36... | collective-permute-start | bytes 688136 | tf_op jit(solution)/shard_map/ppermute | solution.py:18
  62.3 1.6 %collective-permute-start.19 = (bf16[64,896]{1,0:T(8,128)(2,1)S(1)}, bf16[64,896]{1,0:T(8,128)(2,1)S(1)}, u32[]{:S(2)}, u32[]{:S(2)}) collective-permute-start(bf16[64,896]{1,0:T(8,128)(2,1)S(1)} %get-tuple-element.38.refs_1_), channel_id=1, source_target_pairs={{0,128},{64,192},{128,0},{192,64},{1,129},{65,193},{129,1},{193,65... | collective-permute-start | bytes 344072 | tf_op jit(solution)/shard_map/ppermute | solution.py:22
  63.9 1.9 %collective-permute-done.22.refs_1_ = bf16[64,1792]{1,0:T(8,128)(2,1)S(1)} collective-permute-done((bf16[64,1792]{1,0:T(8,128)(2,1)S(1)}, bf16[64,1792]{1,0:T(8,128)(2,1)S(1)}, u32[]{:S(2)}, u32[]{:S(2)}) %collective-permute-start.22) | collective-permute-done | bytes 229408 | tf_op jit(solution)/shard_map/ppermute | solution.py:18
  66.8 2.5 %collective-permute-start.24 = (bf16[64,896]{1,0:T(8,128)(2,1)S(1)}, bf16[64,896]{1,0:T(8,128)(2,1)S(1)}, u32[]{:S(2)}, u32[]{:S(2)}) collective-permute-start(bf16[64,896]{1,0:T(8,128)(2,1)S(1)} %hidden.1.refs_1_), channel_id=1, source_target_pairs={{0,128},{64,192},{128,0},{192,64},{1,129},{65,193},{129,1},{193,65... | collective-permute-start | bytes 344072 | tf_op jit(solution)/shard_map/ppermute | solution.py:22
  69.4 2.0 %copy-done.4 = bf16[896,2048]{1,0:T(8,128)(2,1)S(1)} copy-done((bf16[896,2048]{1,0:T(8,128)(2,1)S(1)}, bf16[896,2048]{1,0:T(8,128)(2,1)}, u32[]{:S(2)}) %copy-start.4) | copy-done | bytes 3670040
  71.4 1.6 %down_weight.1.refs_5_ = bf16[896,2048]{1,0:T(8,128)(2,1)S(1)} custom-call(f32[16,7]{1,0:T(8,128)S(1)} %bitcast.4, bf16[896,2048]{1,0:T(8,128)(2,1)S(1)} %copy-done.4), custom_call_target="tpu_custom_call" | custom-call | flops 1024 | bytes 1024 | tf_op jit(solution)/shard_map/down_weight/pallas_call | solution.py:45
  73.1 2.5 %down.2 = (f32[128,2048]{1,0:T(8,128)S(1)}, bf16[128,2048]{1,0:T(8,128)(2,1)S(1)}) custom-call(s32[1]{0:T(128)} %bitcast.refs_0_, bf16[64,896]{1,0:T(8,128)(2,1)S(1)} %get-tuple-element.38.refs_1_, bf16[64,896]{1,0:T(8,128)(2,1)S(1)} %collective-permute-done.18.refs_2_, bf16[64,896]{1,0:T(8,128)(2,1)S(1)} %collective-permute-done.19.refs_3_, ...), custom_call_target="tpu_custom_call" | custom-call | flops 1024 | bytes 1024 | tf_op jit(solution)/shard_map/down/pallas_call | solution.py:45
  75.6 2.3 %collective-permute-start.21 = (bf16[128,2048]{1,0:T(8,128)(2,1)S(1)}, bf16[128,2048]{1,0:T(8,128)(2,1)S(1)}, u32[]{:S(2)}, u32[]{:S(2)}) collective-permute-start(bf16[128,2048]{1,0:T(8,128)(2,1)S(1)} %get-tuple-element.40.refs_6_), channel_id=1, source_target_pairs={{0,1},{1,0},{2,3},{3,2},{4,5},{5,4},{6,7},{7,6},{8,9},{9,8},{10,11... | collective-permute-start | bytes 1572872 | tf_op jit(solution)/shard_map/ppermute | solution.py:18
  78.0 2.5 %down.3 = (f32[128,2048]{1,0:T(8,128)S(1)}, bf16[80,2048]{1,0:T(8,128)(2,1)S(1)}, bf16[48,2048]{1,0:T(8,128)(2,1)S(1)}) custom-call(s32[1]{0:T(128)} %bitcast.refs_0_, bf16[64,896]{1,0:T(8,128)(2,1)S(1)} %hidden.1.refs_1_, bf16[64,896]{1,0:T(8,128)(2,1)S(1)} %collective-permute-done.23.refs_2_, bf16[64,896]{1,0:T(8,128)(2,1)S(1)} %collective-permute-done.24.refs_3_, ...), custom_call_target="tpu_custom_call" | custom-call | flops 1024 | bytes 1024 | tf_op jit(solution)/shard_map/down/pallas_call | solution.py:45
  81.1 1.4 %collective-permute-done.28.refs_1_ = bf16[48,2048]{1,0:T(8,128)(2,1)S(1)} collective-permute-done((bf16[48,2048]{1,0:T(8,128)(2,1)S(1)}, bf16[48,2048]{1,0:T(8,128)(2,1)S(1)}, u32[]{:S(2)}, u32[]{:S(2)}) %collective-permute-start.28) | collective-permute-done | bytes 196640 | tf_op jit(solution)/shard_map/ppermute | solution.py:18
  84.3 4.7 %collective-permute-done.29.refs_2_ = bf16[48,2048]{1,0:T(8,128)(2,1)S(1)} collective-permute-done((bf16[48,2048]{1,0:T(8,128)(2,1)S(1)}, bf16[48,2048]{1,0:T(8,128)(2,1)S(1)}, u32[]{:S(2)}, u32[]{:S(2)}) %collective-permute-start.29) | collective-permute-done | bytes 196640 | tf_op jit(solution)/shard_map/ppermute | solution.py:18
  89.9 6.1 %collective-permute-done.27.refs_2_ = bf16[80,2048]{1,0:T(8,128)(2,1)S(1)} collective-permute-done((bf16[80,2048]{1,0:T(8,128)(2,1)S(1)}, bf16[80,2048]{1,0:T(8,128)(2,1)S(1)}, u32[]{:S(2)}, u32[]{:S(2)}) %collective-permute-start.27) | collective-permute-done | bytes 327712 | tf_op jit(solution)/shard_map/ppermute | solution.py:18
  96.2 1.7 %collective-permute-done.30.refs_1_ = bf16[48,2048]{1,0:T(8,128)(2,1)S(1)} collective-permute-done((bf16[48,2048]{1,0:T(8,128)(2,1)S(1)}, bf16[48,2048]{1,0:T(8,128)(2,1)S(1)}, u32[]{:S(2)}, u32[]{:S(2)}) %collective-permute-start.30) | collective-permute-done | bytes 196640 | tf_op jit(solution)/shard_map/ppermute | solution.py:30
  97.9 3.6 %collective-permute-start.32 = (bf16[32,2048]{1,0:T(8,128)(2,1)S(1)}, bf16[32,2048]{1,0:T(8,128)(2,1)S(1)}, u32[]{:S(2)}, u32[]{:S(2)}) collective-permute-start(bf16[32,2048]{1,0:T(8,128)(2,1)S(1)} %relay.1), channel_id=1, source_target_pairs={{0,28},{1,5},{4,0},{5,9},{8,4},{9,13},{12,8},{13,17},{16,12},{17,2... | collective-permute-start | bytes 393224 | tf_op jit(solution)/shard_map/ppermute | solution.py:30
  101.5 1.7 %collective-permute-done.31.refs_2_ = bf16[32,2048]{1,0:T(8,128)(2,1)S(1)} collective-permute-done((bf16[32,2048]{1,0:T(8,128)(2,1)S(1)}, bf16[32,2048]{1,0:T(8,128)(2,1)S(1)}, u32[]{:S(2)}, u32[]{:S(2)}) %collective-permute-start.31) | collective-permute-done | bytes 131104 | tf_op jit(solution)/shard_map/ppermute | solution.py:30
  104.4 2.4 %collective-permute-start.33 = (f32[16,2048]{1,0:T(8,128)S(1)}, f32[16,2048]{1,0:T(8,128)S(1)}, u32[]{:S(2)}, u32[]{:S(2)}) collective-permute-start(f32[16,2048]{1,0:T(8,128)S(1)} %get-tuple-element.50), channel_id=1, source_target_pairs={{0,1},{1,0},{2,3},{3,2},{4,5},{5,4},{6,7},{7,6},{8,9},{9,8},{10,11... | collective-permute-start | bytes 393224 | tf_op jit(solution)/shard_map/ppermute | solution.py:18
  (73 shorter events, 19.0 us)
Async XLA Ops:
  0.0 4.4 %collective-permute-start = (bf16[16,2048]{1,0:T(8,128)(2,1)}, bf16[16,2048]{1,0:T(8,128)(2,1)S(1)}, u32[]{:S(2)}, u32[]{:S(2)}) collective-permute-start(bf16[16,2048]{1,0:T(8,128)(2,1)} %param.7), channel_id=1, source_target_pairs={{0,1},{1,0},{2,3},{3,2},{4,5},{5,4},{6,7},{7,6},{8,9},{9,8},{10,11... | collective-permute-start | bytes 196616 | tf_op jit(solution)/shard_map/ppermute | solution.py:18
  4.4 10.6 %collective-permute-start.3 = (bf16[32,2048]{1,0:T(8,128)(2,1)S(1)}, bf16[32,2048]{1,0:T(8,128)(2,1)S(1)}, u32[]{:S(2)}, u32[]{:S(2)}) collective-permute-start(bf16[32,2048]{1,0:T(8,128)(2,1)S(1)} %constant_dynamic-update-slice_fusion), channel_id=1, source_target_pairs={{0,8},{1,25},{4,12},{5,29},{8,16},{9,1},{12,20},{13,5},{16,24},{17... | collective-permute-start | bytes 393224 | tf_op jit(solution)/shard_map/ppermute | solution.py:30
  8.6 10.4 %collective-permute-start.5 = (bf16[16,2048]{1,0:T(8,128)(2,1)}, bf16[16,2048]{1,0:T(8,128)(2,1)S(1)}, u32[]{:S(2)}, u32[]{:S(2)}) collective-permute-start(bf16[16,2048]{1,0:T(8,128)(2,1)} %param.7), channel_id=1, source_target_pairs={{0,16},{1,17},{4,20},{5,21},{8,24},{9,25},{12,28},{13,29},{16,0},{... | collective-permute-start | bytes 196616 | tf_op jit(solution)/shard_map/ppermute | solution.py:30
  9.6 9.4 %collective-permute-start.4 = (bf16[32,2048]{1,0:T(8,128)(2,1)S(1)}, bf16[32,2048]{1,0:T(8,128)(2,1)S(1)}, u32[]{:S(2)}, u32[]{:S(2)}) collective-permute-start(bf16[32,2048]{1,0:T(8,128)(2,1)S(1)} %constant_dynamic-update-slice_fusion), channel_id=1, source_target_pairs={{0,12},{1,21},{4,16},{5,25},{8,20},{9,29},{12,24},{13,1},{16,28},{... | collective-permute-start | bytes 393224 | tf_op jit(solution)/shard_map/ppermute | solution.py:30
  13.6 10.4 %collective-permute-start.1 = (bf16[32,2048]{1,0:T(8,128)(2,1)S(1)}, bf16[32,2048]{1,0:T(8,128)(2,1)S(1)}, u32[]{:S(2)}, u32[]{:S(2)}) collective-permute-start(bf16[32,2048]{1,0:T(8,128)(2,1)S(1)} %constant_dynamic-update-slice_fusion), channel_id=1, source_target_pairs={{0,4},{1,29},{4,8},{5,1},{8,12},{9,5},{12,16},{13,9},{16,20},{17,1... | collective-permute-start | bytes 393224 | tf_op jit(solution)/shard_map/ppermute | solution.py:30
  19.1 14.5 %collective-permute-start.8 = (bf16[80,2048]{1,0:T(8,128)(2,1)S(1)}, bf16[80,2048]{1,0:T(8,128)(2,1)S(1)}, u32[]{:S(2)}, u32[]{:S(2)}) collective-permute-start(bf16[80,2048]{1,0:T(8,128)(2,1)S(1)} %constant_dynamic-update-slice_fusion.4.refs_3_), channel_id=1, source_target_pairs={{0,2},{2,0},{1,3},{3,1},{4,6},{6,4},{5,7},{7,5},{8,10},{10,8},{9,1... | collective-permute-start | bytes 983048 | tf_op jit(solution)/shard_map/ppermute | solution.py:18
  20.4 5.1 %collective-permute-start.7 = (bf16[80,2048]{1,0:T(8,128)(2,1)S(1)}, bf16[80,2048]{1,0:T(8,128)(2,1)S(1)}, u32[]{:S(2)}, u32[]{:S(2)}) collective-permute-start(bf16[80,2048]{1,0:T(8,128)(2,1)S(1)} %constant_dynamic-update-slice_fusion.4.refs_3_), channel_id=1, source_target_pairs={{0,1},{1,0},{2,3},{3,2},{4,5},{5,4},{6,7},{7,6},{8,9},{9,8},{10,11... | collective-permute-start | bytes 983048 | tf_op jit(solution)/shard_map/ppermute | solution.py:18
  24.1 14.2 %collective-permute-start.2 = (bf16[48,2048]{1,0:T(8,128)(2,1)S(1)}, bf16[48,2048]{1,0:T(8,128)(2,1)S(1)}, u32[]{:S(2)}, u32[]{:S(2)}) collective-permute-start(bf16[48,2048]{1,0:T(8,128)(2,1)S(1)} %constant_dynamic-update-slice_fusion.2.refs_2_), channel_id=1, source_target_pairs={{0,2},{2,0},{1,3},{3,1},{4,6},{6,4},{5,7},{7,5},{8,10},{10,8},{9,1... | collective-permute-start | bytes 589832 | tf_op jit(solution)/shard_map/ppermute | solution.py:18
  33.6 7.0 %collective-permute-start.10 = (bf16[80,2048]{1,0:T(8,128)(2,1)S(1)}, bf16[80,2048]{1,0:T(8,128)(2,1)S(1)}, u32[]{:S(2)}, u32[]{:S(2)}) collective-permute-start(bf16[80,2048]{1,0:T(8,128)(2,1)S(1)} %joined.3.refs_3_), channel_id=1, source_target_pairs={{0,1},{1,0},{2,3},{3,2},{4,5},{5,4},{6,7},{7,6},{8,9},{9,8},{10,11... | collective-permute-start | bytes 983048 | tf_op jit(solution)/shard_map/ppermute | solution.py:18
  34.1 13.3 %collective-permute-start.14 = (bf16[64,1792]{1,0:T(8,128)(2,1)S(1)}, bf16[64,1792]{1,0:T(8,128)(2,1)S(1)}, u32[]{:S(2)}, u32[]{:S(2)}) collective-permute-start(bf16[64,1792]{1,0:T(8,128)(2,1)S(1)} %get-tuple-element.33), channel_id=1, source_target_pairs={{0,64},{64,128},{128,192},{192,0},{1,65},{65,129},{129,193},{193,1... | collective-permute-start | bytes 688136 | tf_op jit(solution)/shard_map/ppermute | solution.py:22
  35.3 12.4 %collective-permute-start.15 = (bf16[64,1792]{1,0:T(8,128)(2,1)S(1)}, bf16[64,1792]{1,0:T(8,128)(2,1)S(1)}, u32[]{:S(2)}, u32[]{:S(2)}) collective-permute-start(bf16[64,1792]{1,0:T(8,128)(2,1)S(1)} %get-tuple-element.34), channel_id=1, source_target_pairs={{0,192},{64,0},{128,64},{192,128},{1,193},{65,1},{129,65},{193,129... | collective-permute-start | bytes 688136 | tf_op jit(solution)/shard_map/ppermute | solution.py:22
  36.8 11.5 %collective-permute-start.16 = (bf16[64,1792]{1,0:T(8,128)(2,1)S(1)}, bf16[64,1792]{1,0:T(8,128)(2,1)S(1)}, u32[]{:S(2)}, u32[]{:S(2)}) collective-permute-start(bf16[64,1792]{1,0:T(8,128)(2,1)S(1)} %get-tuple-element.35), channel_id=1, source_target_pairs={{0,128},{64,192},{128,0},{192,64},{1,129},{65,193},{129,1},{193,65... | collective-permute-start | bytes 688136 | tf_op jit(solution)/shard_map/ppermute | solution.py:22
  38.3 2.3 %collective-permute-start.9 = (bf16[48,2048]{1,0:T(8,128)(2,1)S(1)}, bf16[48,2048]{1,0:T(8,128)(2,1)S(1)}, u32[]{:S(2)}, u32[]{:S(2)}) collective-permute-start(bf16[48,2048]{1,0:T(8,128)(2,1)S(1)} %joined.2.refs_2_), channel_id=1, source_target_pairs={{0,1},{1,0},{2,3},{3,2},{4,5},{5,4},{6,7},{7,6},{8,9},{9,8},{10,11... | collective-permute-start | bytes 589832 | tf_op jit(solution)/shard_map/ppermute | solution.py:18
  44.7 9.1 %collective-permute-start.11 = (bf16[64,1792]{1,0:T(8,128)(2,1)S(1)}, bf16[64,1792]{1,0:T(8,128)(2,1)S(1)}, u32[]{:S(2)}, u32[]{:S(2)}) collective-permute-start(bf16[64,1792]{1,0:T(8,128)(2,1)S(1)} %get-tuple-element.30), channel_id=1, source_target_pairs={{0,64},{64,128},{128,192},{192,0},{1,65},{65,129},{129,193},{193,1... | collective-permute-start | bytes 688136 | tf_op jit(solution)/shard_map/ppermute | solution.py:22
  45.1 8.8 %collective-permute-start.12 = (bf16[64,1792]{1,0:T(8,128)(2,1)S(1)}, bf16[64,1792]{1,0:T(8,128)(2,1)S(1)}, u32[]{:S(2)}, u32[]{:S(2)}) collective-permute-start(bf16[64,1792]{1,0:T(8,128)(2,1)S(1)} %get-tuple-element.31), channel_id=1, source_target_pairs={{0,192},{64,0},{128,64},{192,128},{1,193},{65,1},{129,65},{193,129... | collective-permute-start | bytes 688136 | tf_op jit(solution)/shard_map/ppermute | solution.py:22
  47.4 10.7 %collective-permute-start.13 = (bf16[64,1792]{1,0:T(8,128)(2,1)S(1)}, bf16[64,1792]{1,0:T(8,128)(2,1)S(1)}, u32[]{:S(2)}, u32[]{:S(2)}) collective-permute-start(bf16[64,1792]{1,0:T(8,128)(2,1)S(1)} %get-tuple-element.32), channel_id=1, source_target_pairs={{0,128},{64,192},{128,0},{192,64},{1,129},{65,193},{129,1},{193,65... | collective-permute-start | bytes 688136 | tf_op jit(solution)/shard_map/ppermute | solution.py:22
  48.4 9.8 %collective-permute-start.17 = (bf16[64,1792]{1,0:T(8,128)(2,1)S(1)}, bf16[64,1792]{1,0:T(8,128)(2,1)S(1)}, u32[]{:S(2)}, u32[]{:S(2)}) collective-permute-start(bf16[64,1792]{1,0:T(8,128)(2,1)S(1)} %get-tuple-element.37), channel_id=1, source_target_pairs={{0,32},{32,0},{1,33},{33,1},{2,34},{34,2},{3,35},{35,3},{4,36},{36... | collective-permute-start | bytes 688136 | tf_op jit(solution)/shard_map/ppermute | solution.py:18
  58.3 7.5 %collective-permute-start.22 = (bf16[64,1792]{1,0:T(8,128)(2,1)S(1)}, bf16[64,1792]{1,0:T(8,128)(2,1)S(1)}, u32[]{:S(2)}, u32[]{:S(2)}) collective-permute-start(bf16[64,1792]{1,0:T(8,128)(2,1)S(1)} %get-tuple-element.42), channel_id=1, source_target_pairs={{0,32},{32,0},{1,33},{33,1},{2,34},{34,2},{3,35},{35,3},{4,36},{36... | collective-permute-start | bytes 688136 | tf_op jit(solution)/shard_map/ppermute | solution.py:18
  61.3 8.0 %collective-permute-start.20 = (bf16[64,896]{1,0:T(8,128)(2,1)S(1)}, bf16[64,896]{1,0:T(8,128)(2,1)S(1)}, u32[]{:S(2)}, u32[]{:S(2)}) collective-permute-start(bf16[64,896]{1,0:T(8,128)(2,1)S(1)} %get-tuple-element.38.refs_1_), channel_id=1, source_target_pairs={{0,192},{64,0},{128,64},{192,128},{1,193},{65,1},{129,65},{193,129... | collective-permute-start | bytes 344072 | tf_op jit(solution)/shard_map/ppermute | solution.py:22
  62.3 10.7 %collective-permute-start.19 = (bf16[64,896]{1,0:T(8,128)(2,1)S(1)}, bf16[64,896]{1,0:T(8,128)(2,1)S(1)}, u32[]{:S(2)}, u32[]{:S(2)}) collective-permute-start(bf16[64,896]{1,0:T(8,128)(2,1)S(1)} %get-tuple-element.38.refs_1_), channel_id=1, source_target_pairs={{0,128},{64,192},{128,0},{192,64},{1,129},{65,193},{129,1},{193,65... | collective-permute-start | bytes 344072 | tf_op jit(solution)/shard_map/ppermute | solution.py:22
  63.9 9.1 %collective-permute-start.18 = (bf16[64,896]{1,0:T(8,128)(2,1)S(1)}, bf16[64,896]{1,0:T(8,128)(2,1)S(1)}, u32[]{:S(2)}, u32[]{:S(2)}) collective-permute-start(bf16[64,896]{1,0:T(8,128)(2,1)S(1)} %get-tuple-element.38.refs_1_), channel_id=1, source_target_pairs={{0,64},{64,128},{128,192},{192,0},{1,65},{65,129},{129,193},{193,1... | collective-permute-start | bytes 344072 | tf_op jit(solution)/shard_map/ppermute | solution.py:22
  66.0 11.9 %collective-permute-start.25 = (bf16[64,896]{1,0:T(8,128)(2,1)S(1)}, bf16[64,896]{1,0:T(8,128)(2,1)S(1)}, u32[]{:S(2)}, u32[]{:S(2)}) collective-permute-start(bf16[64,896]{1,0:T(8,128)(2,1)S(1)} %hidden.1.refs_1_), channel_id=1, source_target_pairs={{0,192},{64,0},{128,64},{192,128},{1,193},{65,1},{129,65},{193,129... | collective-permute-start | bytes 344072 | tf_op jit(solution)/shard_map/ppermute | solution.py:22
  66.8 11.1 %collective-permute-start.24 = (bf16[64,896]{1,0:T(8,128)(2,1)S(1)}, bf16[64,896]{1,0:T(8,128)(2,1)S(1)}, u32[]{:S(2)}, u32[]{:S(2)}) collective-permute-start(bf16[64,896]{1,0:T(8,128)(2,1)S(1)} %hidden.1.refs_1_), channel_id=1, source_target_pairs={{0,128},{64,192},{128,0},{192,64},{1,129},{65,193},{129,1},{193,65... | collective-permute-start | bytes 344072 | tf_op jit(solution)/shard_map/ppermute | solution.py:22
  69.3 8.7 %collective-permute-start.23 = (bf16[64,896]{1,0:T(8,128)(2,1)S(1)}, bf16[64,896]{1,0:T(8,128)(2,1)S(1)}, u32[]{:S(2)}, u32[]{:S(2)}) collective-permute-start(bf16[64,896]{1,0:T(8,128)(2,1)S(1)} %hidden.1.refs_1_), channel_id=1, source_target_pairs={{0,64},{64,128},{128,192},{192,0},{1,65},{65,129},{129,193},{193,1... | collective-permute-start | bytes 344072 | tf_op jit(solution)/shard_map/ppermute | solution.py:22
  75.6 8.6 %collective-permute-start.21 = (bf16[128,2048]{1,0:T(8,128)(2,1)S(1)}, bf16[128,2048]{1,0:T(8,128)(2,1)S(1)}, u32[]{:S(2)}, u32[]{:S(2)}) collective-permute-start(bf16[128,2048]{1,0:T(8,128)(2,1)S(1)} %get-tuple-element.40.refs_6_), channel_id=1, source_target_pairs={{0,1},{1,0},{2,3},{3,2},{4,5},{5,4},{6,7},{7,6},{8,9},{9,8},{10,11... | collective-permute-start | bytes 1572872 | tf_op jit(solution)/shard_map/ppermute | solution.py:18
  80.5 3.2 %collective-permute-start.26 = (bf16[80,2048]{1,0:T(8,128)(2,1)S(1)}, bf16[80,2048]{1,0:T(8,128)(2,1)S(1)}, u32[]{:S(2)}, u32[]{:S(2)}) collective-permute-start(bf16[80,2048]{1,0:T(8,128)(2,1)S(1)} %get-tuple-element.44), channel_id=1, source_target_pairs={{0,1},{1,0},{2,3},{3,2},{4,5},{5,4},{6,7},{7,6},{8,9},{9,8},{10,11... | collective-permute-start | bytes 983048 | tf_op jit(solution)/shard_map/ppermute | solution.py:18
  82.6 6.4 %collective-permute-start.29 = (bf16[48,2048]{1,0:T(8,128)(2,1)S(1)}, bf16[48,2048]{1,0:T(8,128)(2,1)S(1)}, u32[]{:S(2)}, u32[]{:S(2)}) collective-permute-start(bf16[48,2048]{1,0:T(8,128)(2,1)S(1)} %sum_far.3), channel_id=1, source_target_pairs={{0,2},{2,0},{1,3},{3,1},{4,6},{6,4},{5,7},{7,5},{8,10},{10,8},{9,1... | collective-permute-start | bytes 589832 | tf_op jit(solution)/shard_map/ppermute | solution.py:18
  83.8 12.2 %collective-permute-start.27 = (bf16[80,2048]{1,0:T(8,128)(2,1)S(1)}, bf16[80,2048]{1,0:T(8,128)(2,1)S(1)}, u32[]{:S(2)}, u32[]{:S(2)}) collective-permute-start(bf16[80,2048]{1,0:T(8,128)(2,1)S(1)} %sum_far.2), channel_id=1, source_target_pairs={{0,2},{2,0},{1,3},{3,1},{4,6},{6,4},{5,7},{7,5},{8,10},{10,8},{9,1... | collective-permute-start | bytes 983048 | tf_op jit(solution)/shard_map/ppermute | solution.py:18
  89.1 8.8 %collective-permute-start.30 = (bf16[48,2048]{1,0:T(8,128)(2,1)S(1)}, bf16[48,2048]{1,0:T(8,128)(2,1)S(1)}, u32[]{:S(2)}, u32[]{:S(2)}) collective-permute-start(bf16[48,2048]{1,0:T(8,128)(2,1)S(1)} %sum_near.3), channel_id=1, source_target_pairs={{0,20},{1,13},{4,24},{5,17},{8,28},{9,21},{12,0},{13,25},{16,4},{1... | collective-permute-start | bytes 589832 | tf_op jit(solution)/shard_map/ppermute | solution.py:30
  96.1 7.1 %collective-permute-start.31 = (bf16[32,2048]{1,0:T(8,128)(2,1)S(1)}, bf16[32,2048]{1,0:T(8,128)(2,1)S(1)}, u32[]{:S(2)}, u32[]{:S(2)}) collective-permute-start(bf16[32,2048]{1,0:T(8,128)(2,1)S(1)} %get-tuple-element.47), channel_id=1, source_target_pairs={{0,24},{1,9},{4,28},{5,13},{8,0},{9,17},{12,4},{13,21},{16,8},{17,... | collective-permute-start | bytes 393224 | tf_op jit(solution)/shard_map/ppermute | solution.py:30
  97.9 6.4 %collective-permute-start.32 = (bf16[32,2048]{1,0:T(8,128)(2,1)S(1)}, bf16[32,2048]{1,0:T(8,128)(2,1)S(1)}, u32[]{:S(2)}, u32[]{:S(2)}) collective-permute-start(bf16[32,2048]{1,0:T(8,128)(2,1)S(1)} %relay.1), channel_id=1, source_target_pairs={{0,28},{1,5},{4,0},{5,9},{8,4},{9,13},{12,8},{13,17},{16,12},{17,2... | collective-permute-start | bytes 393224 | tf_op jit(solution)/shard_map/ppermute | solution.py:30
  104.4 3.4 %collective-permute-start.33 = (f32[16,2048]{1,0:T(8,128)S(1)}, f32[16,2048]{1,0:T(8,128)S(1)}, u32[]{:S(2)}, u32[]{:S(2)}) collective-permute-start(f32[16,2048]{1,0:T(8,128)S(1)} %get-tuple-element.50), channel_id=1, source_target_pairs={{0,1},{1,0},{2,3},{3,2},{4,5},{5,4},{6,7},{7,6},{8,9},{9,8},{10,11... | collective-permute-start | bytes 393224 | tf_op jit(solution)/shard_map/ppermute | solution.py:18
  (8 other events, 62.7 us)
